TPU v7x, 32 devices: a whole 2x2x4 slice. The times are simulated.
32 devices in a mesh: row: 4 (over z), col: 8 (over y, x, core).
Axes of the slice: x: 2, y: 2, z: 4, core: 2. Of those that a mesh axis runs over, the one named last changes fastest.
Arguments:
- eigvecs: bfloat16 [2048, 16384], P('row', 'col'), may hold values from -0.01171875 to 0.01171875
- pole_order: int32 [16384], P('col'), may hold values from 0 to 16383, as said below
- pole_weight: float32 [16384], P('col'), may hold values from 0.17 to 6
- root_gap: int32 [2048], replicated, may hold values from 1024 to 15358, as said below
- root_shift: float32 [2048], replicated, may hold values from -0.25 to 0.25
- column_weight: float32 [2048], replicated, may hold values from 4 to 40
- panel_vectors: bfloat16 [2, 2048, 256], P(None, 'row'), may hold values from -0.125 to 0.125
- panel_factors: float32 [2, 256, 256], replicated, as said below
Outputs:
- eigenvectors: bfloat16 [2048, 2048], P('row', 'col')
Inputs may be any that keep to these rules, and one draw needn't show every extreme that they name: `pole_order`: each value appears once. Distinct values; root j lies strictly between the poles at 2 * root_gap[j] and 2 * root_gap[j] + 2. `panel_factors`: upper triangular, with a diagonal between 2 and 4.
All inputs are finite; a program needn't handle non-finite values.
Results may differ from a plain program's by a relative error of at most 0.02.
Values may be sent and summed in bfloat16 or wider, within the bound.
No kernel may reach another device: no remote copies, remote signals or barrier semaphores. Data moves between devices by JAX's collectives and lax.ppermute only.
A program may use at most 64 MiB of HBM per device.

v0:
```python
import jax
import jax.numpy as jnp
from jax import lax
from jax.sharding import PartitionSpec as P


def cauchy_values(pole_values, weight_slice, root_gap, root_shift, column_weight):
    root_values = 2.0 * root_gap.astype(jnp.float32) + 1.0 + root_shift
    numer = weight_slice[:, None] * column_weight[None, :]
    return (numer / (pole_values[:, None] - root_values[None, :])).astype(jnp.bfloat16)


def shards(
    eigvecs,
    pole_order,
    pole_weight,
    root_gap,
    root_shift,
    column_weight,
    panel_vectors,
    panel_factors,
):
    matrix = cauchy_values(
        2.0 * pole_order.astype(jnp.float32), pole_weight, root_gap, root_shift, column_weight
    )
    partial_value = jnp.dot(eigvecs, matrix, preferred_element_type=jnp.float32)
    owned = lax.psum_scatter(
        partial_value.astype(jnp.bfloat16), "col", scatter_dimension=1, tiled=True
    )
    cyclic = lax.all_to_all(owned, "row", split_axis=0, concat_axis=0, tiled=True)
    current = cyclic.astype(jnp.float32)
    highest = lax.Precision.HIGHEST
    first_vectors = panel_vectors[0].astype(jnp.float32)
    second_vectors = panel_vectors[1].astype(jnp.float32)
    correlation_local = jnp.einsum("rp,rq->pq", second_vectors, first_vectors, precision=highest)
    correlation = lax.psum(correlation_local.astype(jnp.bfloat16), "row").astype(jnp.float32)
    first_local = jnp.einsum("rp,rc->pc", first_vectors, current, precision=highest)
    second_local = jnp.einsum("rp,rc->pc", second_vectors, current, precision=highest)
    first_project, second_project = (
        lax.psum(first_local.astype(jnp.bfloat16), "row").astype(jnp.float32),
        lax.psum(second_local.astype(jnp.bfloat16), "row").astype(jnp.float32),
    )
    first_factored = jnp.dot(panel_factors[0], first_project, precision=highest)
    second_project = second_project - jnp.dot(correlation, first_factored, precision=highest)
    second_factored = jnp.dot(panel_factors[1], second_project, precision=highest)
    current = current - jnp.dot(first_vectors, first_factored, precision=highest)
    current = current - jnp.dot(second_vectors, second_factored, precision=highest)
    return current.astype(jnp.bfloat16)


def solution(mesh):
    return jax.shard_map(
        shards,
        mesh=mesh,
        in_specs=(P("row", "col"), P("col"), P("col"), P(), P(), P(), P(None, "row", None), P()),
        out_specs=P("row", "col"),
        check_vma=False,
    )
```

profile of v0, /device:TPU:0, one launch (start us, length us, event | category | flops | bytes accessed | tf_op | source)
XLA Modules:
  0.0 124.1 jit_solution(8483011058258260257)
XLA Ops:
  6.5 0.0 copy-start
  6.5 0.0 reduce-scatter.2.cloned.1.call-start
  6.5 0.9 add_add_fusion
  7.4 0.7 copy-done
  8.2 7.8 %fusion.6 = bf16[512,2048]{0,1:T(8,128)(2,1)} fusion(bf16[512,2048]{1,0:T(8,128)(2,1)S(1)} %copy-done, f32[2048]{0:T(1024)S(1)} %get-tuple-element.8, f32[2048]{0:T(1024)S(1)} %get-tuple-element.9, f32[2048]{0:T(1024)} %param.13, f32[2048]{0:T(1024)} %param.10), kind=kOutput, calls=%fused_computation.7 | convolution fusion | flops 4312793088 | bytes 4227072 | tf_op jit(solution)/shard_map/dot_general | solution.py:26
  16.0 0.0 copy-start.2
  16.0 0.0 reduce-scatter.2.cloned.1.call-update
  16.0 0.0 copy-start.1
  16.0 44.0 %reduce-scatter.2.cloned.1.call-done = bf16[512,256]{0,1:T(8,128)(2,1)} async-done(((bf16[512,2048]{0,1:T(8,128)(2,1)}), bf16[512,256]{0,1:T(8,128)(2,1)}) %reduce-scatter.2.cloned.1.call-update) | async-done | bytes 262160 | tf_op jit(solution)/shard_map/reduce_scatter | solution.py:27
  60.0 1.7 %copy_bitcast_fusion = bf16[4,128,256]{1,2,0:T(8,128)(2,1)} fusion(bf16[512,256]{0,1:T(8,128)(2,1)} %reduce-scatter.2.cloned.1.call-done), kind=kLoop, calls=%fused_computation.21 | loop fusion | bytes 524288 | tf_op jit(solution)/shard_map/all_to_all | solution.py:30
  61.7 4.6 %all-to-all-start = ((bf16[4,128,256]{1,2,0:T(8,128)(2,1)}), bf16[4,128,256]{1,2,0:T(8,128)(2,1)S(1)}, u32[]{:S(2)}, u32[]{:S(2)}) async-start(bf16[4,128,256]{1,2,0:T(8,128)(2,1)} %copy_bitcast_fusion), calls=%async_computation.1 | async-start | bytes 524288 | tf_op jit(solution)/shard_map/all_to_all | solution.py:30
  66.3 0.0 all-reduce.3.cloned.1.call-start
  66.3 0.0 copy-done.2
  66.3 0.9 convolution_convert_fusion
  67.3 8.0 %all-to-all-done = bf16[4,128,256]{1,2,0:T(8,128)(2,1)S(1)} async-done(((bf16[4,128,256]{1,2,0:T(8,128)(2,1)}), bf16[4,128,256]{1,2,0:T(8,128)(2,1)S(1)}, u32[]{:S(2)}, u32[]{:S(2)}) %all-to-all-start) | async-done | bytes 262176 | tf_op jit(solution)/shard_map/all_to_all | solution.py:30
  75.3 0.9 fusion.10
  76.1 0.9 fusion.11
  77.0 0.0 all-reduce.3.cloned.1.call-update
  77.0 35.5 %all-reduce.3.cloned.1.call-done = (bf16[256,256]{1,0:T(8,128)(2,1)}, bf16[256,256]{0,1:T(8,128)(2,1)}, bf16[256,256]{0,1:T(8,128)(2,1)}) async-done(((bf16[256,256]{1,0:T(8,128)(2,1)}, bf16[256,256]{0,1:T(8,128)(2,1)}, bf16[256,256]{0,1:T(8,128)(2,1)}), (bf16[256,256]{1,0:T(8,128)(2,1)}, bf16[256,256]{0,1:T(8,128)(2,1)}, bf16[256,256]{0,1:T(8,128)(2,1)})) %all-reduce.3.cloned.1.call-update) | async-done | bytes 393232 | tf_op jit(solution)/shard_map/psum | solution.py:36
  112.6 0.0 copy-done.1
  112.6 1.2 fusion.19
  113.8 1.3 %convolution_subtract_fusion = f32[256,256]{0,1:T(8,128)S(1)} fusion(bf16[256,256]{1,0:T(8,128)(2,1)} %get-tuple-element.5, f32[256,256]{1,0:T(8,128)S(1)} %fusion.19, bf16[256,256]{0,1:T(8,128)(2,1)} %get-tuple-element.7), kind=kOutput, calls=%fused_computation.13 | convolution fusion | flops 201457664 | bytes 786432 | tf_op jit(solution)/shard_map/dot_general | solution.py:44
  115.1 0.4 fusion.14
  115.5 0.4 convolution_bitcast_fusion
  116.0 0.4 fusion.9
  116.4 0.8 copy.12
Async XLA Ops:
  6.5 1.6 %copy-start = (bf16[512,2048]{1,0:T(8,128)(2,1)S(1)}, bf16[512,2048]{1,0:T(8,128)(2,1)}, u32[]{:S(2)}) copy-start(bf16[512,2048]{1,0:T(8,128)(2,1)} %param.8) | copy-start | bytes 6291460
  6.5 53.5 %reduce-scatter.2.cloned.1.call-start = ((), (), s32[]{:S(2)}) async-start(), calls=%async_computation.2 | async-start | bytes 2359296 | tf_op jit(solution)/shard_map/reduce_scatter | solution.py:27
  16.0 50.4 %copy-start.2 = (bf16[2,512,256]{2,1,0:T(8,128)(2,1)S(1)}, bf16[2,512,256]{2,1,0:T(8,128)(2,1)}, u32[]{:S(2)}) copy-start(bf16[2,512,256]{2,1,0:T(8,128)(2,1)} %param.14) | copy-start | bytes 1572868
  16.0 96.6 %copy-start.1 = (f32[2,256,256]{2,1,0:T(8,128)S(1)}, f32[2,256,256]{2,1,0:T(8,128)}, u32[]{:S(2)}) copy-start(f32[2,256,256]{2,1,0:T(8,128)} %param.15) | copy-start | bytes 1572868
  61.7 13.5 %all-to-all-start = ((bf16[4,128,256]{1,2,0:T(8,128)(2,1)}), bf16[4,128,256]{1,2,0:T(8,128)(2,1)S(1)}, u32[]{:S(2)}, u32[]{:S(2)}) async-start(bf16[4,128,256]{1,2,0:T(8,128)(2,1)} %copy_bitcast_fusion), calls=%async_computation.1 | async-start | bytes 524288 | tf_op jit(solution)/shard_map/all_to_all | solution.py:30
  66.3 46.2 %all-reduce.3.cloned.1.call-start = ((), (), s32[]{:S(2)}) async-start(), calls=%async_computation.3 | async-start | bytes 786432 | tf_op jit(solution)/shard_map/psum | solution.py:36
Sparse Core Ops, SparseCore 0:
  16.1 43.8 reduce-scatter.1
  77.2 35.3 all-reduce.2
where the time goes:
time: 124 us
  waiting for transfers between devices  87.6 us (71%)
  matrix products  14.3 us (12%)
  between operations  13.4 us (11%)
  starting transfers between devices  4.61 us (4%)
  local copies, waits for them, and re-layouts  3.3 us (3%)
    reduce_scatter x1, waiting for transfers between devices, shards(): lax.psum_scatter(partial_value.astype(jnp.bfloat16), 'col', scatter_dimen...  44 us
    psum x1, waiting for transfers between devices, shards(): lax.psum(correlation_local.astype(jnp.bfloat16), 'row').astype(jnp.float32)  35.5 us
    all_to_all x1, waiting for transfers between devices, shards(): lax.all_to_all(owned, 'row', split_axis=0, concat_axis=0, tiled=True)  7.98 us
    dot_general x1, matrix products, shards(): partial_value = jnp.dot(eigvecs, matrix, preferred_element_type=jnp.float32)  7.78 us
    all_to_all x1, starting transfers between devices, shards(): lax.all_to_all(owned, 'row', split_axis=0, concat_axis=0, tiled=True)  4.61 us
  transfers between devices with their start and end apart: 3, of which 3 were waited for; matrix products, arithmetic and copies ran while one was open for 1% of the time, Pallas kernels for 0%

commit v1 on v0

v1 whole, which is shorter than its diff:
```python
import functools

import jax
import jax.numpy as jnp
from jax import lax
from jax.experimental import pallas as pl
from jax.experimental.pallas import tpu as pltpu
from jax.sharding import PartitionSpec as P

BF = jnp.bfloat16
F32 = jnp.float32
HIGHEST = lax.Precision.HIGHEST
MIB = 2**20


def bit_orders(size, first):
    bits = list(range(first, size.bit_length() - 1))
    half = len(bits) // 2
    return bits, bits[half:] + bits[:half]


def halving_codes(bits):
    if not bits:
        return [0]
    rest = halving_codes(bits[1:])
    return [(1 << bits[0]) | code for code in rest] + rest


def product_kernel(plan, width, depth, *refs):
    eig_hbm, order_hbm, weight_hbm, gap_hbm, shift_hbm, scale_hbm = refs[:6]
    outs = refs[6:6 + len(plan)]
    eig, order, weight, gap, shift, scale, eig_sem, small_sem = refs[6 + len(plan):]
    poles = eig.shape[1]
    small = [
        pltpu.make_async_copy(src, dst, small_sem.at[i])
        for i, (src, dst) in enumerate(
            [(order_hbm, order), (gap_hbm, gap), (shift_hbm, shift), (weight_hbm, weight), (scale_hbm, scale)]
        )
    ]
    pieces = range(0, poles, depth)
    large = [
        pltpu.make_async_copy(eig_hbm.at[:, k:k + depth], eig.at[:, k:k + depth], eig_sem.at[i])
        for i, k in enumerate(pieces)
    ]
    for copy in small + large:
        copy.start()
    me = lax.axis_index("col")
    even = lax.rem(me, 2) == 0
    for copy in small:
        copy.wait()
    pole_values = (2.0 * order[...].astype(F32)).reshape(1, poles)
    weights = weight[...].reshape(1, poles)
    first = True
    for out, codes in zip(outs, plan):
        for place, (even_code, odd_code) in enumerate(codes):
            start = pl.multiple_of(jnp.bitwise_xor(me, jnp.where(even, even_code, odd_code)) * width, width)
            roots = 2.0 * gap[pl.ds(start, width)].astype(F32) + 1.0 + shift[pl.ds(start, width)]
            roots = roots.reshape(1, width)
            roots = jnp.concatenate(
                [jnp.broadcast_to(roots[:, j:j + 128], (128, 128)).T for j in range(0, width, 128)], 0
            )
            total = None
            for i, k in enumerate(pieces):
                if first:
                    large[i].wait()
                gaps = pole_values[:, k:k + depth] - jnp.concatenate([roots] * (depth // 128), 1)
                matrix = (weights[:, k:k + depth] / gaps).astype(BF)
                term = lax.dot_general(
                    eig[:, k:k + depth], matrix, (((1,), (1,)), ((), ())), preferred_element_type=F32
                )
                total = term if total is None else total + term
            first = False
            out[:, place * width:(place + 1) * width] = (
                total * scale[pl.ds(start, width)].reshape(1, width)
            ).astype(BF)


def products(plan, parts, eigvecs, pole_order, pole_weight, root_gap, root_shift, column_weight):
    rows, poles = eigvecs.shape
    roots = root_gap.shape[0]
    width = roots // parts
    if width % 128 or poles % 1024:
        me = lax.axis_index("col")
        results = []
        for codes in plan:
            codes = jnp.array(codes, jnp.int32)
            places = jnp.bitwise_xor(me, jnp.where(me % 2 == 0, codes[:, 0], codes[:, 1]))
            pick = lambda v: v.reshape(parts, width)[places].reshape(-1)
            root_values = 2.0 * pick(root_gap).astype(F32) + 1.0 + pick(root_shift)
            numer = pole_weight[:, None] * pick(column_weight)[None, :]
            gaps = 2.0 * pole_order.astype(F32)[:, None] - root_values[None, :]
            matrix = (numer / gaps).astype(BF)
            results.append(jnp.dot(eigvecs, matrix, preferred_element_type=F32).astype(BF))
        return results
    depth = poles // 2
    count = sum(len(codes) for codes in plan)
    return pl.pallas_call(
        functools.partial(product_kernel, plan, width, depth),
        in_specs=[pl.BlockSpec(memory_space=pl.ANY)] * 6,
        out_specs=[pl.BlockSpec(memory_space=pltpu.VMEM)] * len(plan),
        out_shape=[jax.ShapeDtypeStruct((rows, width * len(codes)), BF) for codes in plan],
        scratch_shapes=[
            pltpu.VMEM((rows, poles), BF),
            pltpu.VMEM((poles,), jnp.int32),
            pltpu.VMEM((poles,), F32),
            pltpu.VMEM((roots,), jnp.int32),
            pltpu.VMEM((roots,), F32),
            pltpu.VMEM((roots,), F32),
            pltpu.SemaphoreType.DMA((2,)),
            pltpu.SemaphoreType.DMA((5,)),
        ],
        compiler_params=pltpu.CompilerParams(vmem_limit_bytes=60 * MIB),
        cost_estimate=pl.CostEstimate(
            flops=2 * rows * poles * width * count, bytes_accessed=3 * MIB, transcendentals=0
        ),
    )(eigvecs, pole_order, pole_weight, root_gap, root_shift, column_weight)


def shards(
    n_row,
    n_col,
    eigvecs,
    pole_order,
    pole_weight,
    root_gap,
    root_shift,
    column_weight,
    panel_vectors,
    panel_factors,
):
    col_orders = bit_orders(n_col, 1)
    row_orders = bit_orders(n_row, 0)
    row = lax.axis_index("row")
    core = lax.axis_index("col") % 2

    def swap_cores(value):
        return lax.ppermute(value, "col", [(i, i ^ 1) for i in range(n_col)])

    def swap_col(value, stage):
        return lax.ppermute(value, "col", [(i, i ^ (1 << col_orders[i % 2][stage])) for i in range(n_col)])

    def swap_row(value, stage):
        pairs = [
            (r * n_col + c, (r ^ (1 << row_orders[c % 2][stage])) * n_col + c)
            for r in range(n_row)
            for c in range(n_col)
        ]
        return lax.ppermute(value, ("row", "col"), pairs)

    def by_core(pair):
        return jnp.where(core == 0, pair[0], pair[1])

    def add(left, right):
        return left.astype(F32) + right.astype(F32)

    def pick_code(codes):
        return by_core((jnp.array(codes[0], jnp.int32), jnp.array(codes[1], jnp.int32)))

    row_codes = [halving_codes(order) for order in row_orders]

    def to_blocks(value):
        blocks = value.reshape((n_row, value.shape[0] // n_row) + value.shape[1:])
        return blocks[jnp.bitwise_xor(row, pick_code(row_codes))]

    def from_blocks(blocks, codes):
        inverse = [[list(c).index(d) for d in range(n_row)] for c in codes]
        places = pick_code(inverse)[jnp.bitwise_xor(row, jnp.arange(n_row, dtype=jnp.int32))]
        value = blocks[places]
        return value.reshape((-1,) + value.shape[2:])

    def source_codes():
        result = []
        for order in row_orders:
            codes = [0]
            for bit in order:
                codes = codes + [code | (1 << bit) for code in codes]
            result.append(codes)
        return result

    def exchange_step(blocks, stage, extra=None):
        half = blocks.shape[1] // 2
        sent, kept = blocks[:, :half], blocks[:, half:]
        shape = sent.shape
        if extra is None:
            got = swap_row(sent, stage)
            return jnp.concatenate([kept, got], 0), None
        flat = sent.reshape(-1, shape[-1])
        message = jnp.concatenate([extra, flat], 0)
        got = swap_row(message, stage)
        return (
            jnp.concatenate([kept, got[extra.shape[0]:].reshape(shape)], 0),
            got[:extra.shape[0]],
        )

    own = [halving_codes(order) for order in col_orders]
    own_codes = list(zip(own[0], own[1]))
    other_codes = [(1 ^ b, 1 ^ a) for a, b in own_codes]
    half = len(own_codes) // 2
    inputs = (eigvecs, pole_order, pole_weight, root_gap, root_shift, column_weight)
    other_sent, own_sent = products([other_codes[:half], own_codes[:half]], n_col, *inputs)
    got_sent = swap_cores(other_sent)
    sent = add(own_sent, got_sent).astype(BF)
    got = swap_col(sent, 0)
    other_kept, own_kept = products([other_codes[half:], own_codes[half:]], n_col, *inputs)
    got_kept = swap_cores(other_kept)

    mine = panel_vectors[core]
    panel_width = panel_vectors.shape[2]
    near = panel_width // 2
    first_vectors = panel_vectors[0]
    second_vectors = panel_vectors[1]
    second_half = lax.dynamic_slice_in_dim(second_vectors, core * near, near, 1)
    correlation = jnp.einsum("rp,rq->pq", second_half, first_vectors, preferred_element_type=F32)
    blocks = to_blocks(mine)[None]
    for stage in range(len(row_orders[0])):
        blocks, extra = exchange_step(blocks, stage, correlation.astype(BF))
        correlation = add(correlation, extra)
    mine_merged = from_blocks(blocks[:, 0], source_codes())
    both = swap_cores(jnp.concatenate([mine_merged, correlation.astype(BF)], 0))
    other_merged, other_correlation = both[:mine_merged.shape[0]], both[mine_merged.shape[0]:].astype(F32)
    correlation = jnp.where(
        core == 0,
        jnp.concatenate([correlation, other_correlation], 0),
        jnp.concatenate([other_correlation, correlation], 0),
    )
    across = jnp.dot(panel_factors[1], correlation, precision=HIGHEST)
    across = first_vectors.astype(F32) - jnp.dot(second_vectors.astype(F32), across, precision=HIGHEST)
    update_first = jnp.dot(across, panel_factors[0], precision=HIGHEST).astype(BF)
    update_second = jnp.dot(second_vectors.astype(F32), panel_factors[1], precision=HIGHEST).astype(BF)
    update = jnp.concatenate(
        [by_core((update_first, update_second)), by_core((update_second, update_first))], 1
    )
    merged_vectors = jnp.concatenate([mine_merged, other_merged], 1)

    kept = add(own_kept, got_kept)
    current = kept + got.astype(F32)
    for stage in range(1, len(col_orders[0])):
        middle = current.shape[1] // 2
        got = swap_col(current[:, :middle].astype(BF), stage)
        current = current[:, middle:] + got.astype(F32)
    merged = current.astype(BF)

    project = jnp.einsum("rp,rc->pc", merged_vectors, merged, preferred_element_type=F32)
    blocks = to_blocks(merged)[None]
    stages = len(row_orders[0])
    row_bits = [jnp.bitwise_and(lax.shift_right_logical(row, pick_code([[o[s]] for o in row_orders])[0]), 1) for s in range(stages)]
    for stage in range(stages - 1):
        middle = project.shape[0] // 2
        kept = lax.dynamic_slice_in_dim(project, row_bits[stage] * middle, middle, 0)
        sent = lax.dynamic_slice_in_dim(project, (1 - row_bits[stage]) * middle, middle, 0)
        blocks, extra = exchange_step(blocks, stage, sent.astype(BF))
        project = add(kept, extra)
    blocks, extra = exchange_step(blocks, stages - 1, project.astype(BF))
    project = add(project, extra).astype(BF)
    cyclic = from_blocks(blocks[:, 0], source_codes())
    for stage in reversed(range(stages - 1)):
        extra = swap_row(project, stage)
        project = jnp.where(
            row_bits[stage] == 0,
            jnp.concatenate([project, extra], 0),
            jnp.concatenate([extra, project], 0),
        )
    return (cyclic.astype(F32) - jnp.dot(update, project, preferred_element_type=F32)).astype(BF)


def solution(mesh):
    return jax.shard_map(
        functools.partial(shards, mesh.shape["row"], mesh.shape["col"]),
        mesh=mesh,
        in_specs=(P("row", "col"), P("col"), P("col"), P(), P(), P(), P(None, "row", None), P()),
        out_specs=P("row", "col"),
        check_vma=False,
    )
```

time: 124 us -> 66.2 us (0.53)
  waiting for transfers between devices: 87.6 us -> 31.3 us
  between operations: 13.4 us -> 0.36 us
  matrix products: 14.3 us -> 3.73 us
  Pallas kernels: 0 us -> 9.84 us
  starting transfers between devices: 4.61 us -> 10.1 us
  other arithmetic: 0.88 us -> 4.74 us
  local copies, waits for them, and re-layouts: 3.3 us -> 5.7 us
    reduce_scatter x1 -> x0, waiting for transfers between devices: 44 us -> none  [shards(): lax.psum_scatter(partial_value.astype(jnp.bfloat16), 'col', scatter_dimen...]
    psum x1 -> x0, waiting for transfers between devices: 35.5 us -> none  [shards(): lax.psum(correlation_local.astype(jnp.bfloat16), 'row').astype(jnp.float32)]
    ppermute x0 -> x10, waiting for transfers between devices: none -> 31.3 us  [the longest x5 24.7 us: swap_row(): return lax.ppermute(value, ('row', 'col'), pairs)]
    dot_general x9 -> x7, matrix products: 14.3 us -> 3.73 us  [the longest x1 1.05 us: shards(): jnp.dot(update, project, preferred_element_type=F32)]
    ppermute x0 -> x10, starting transfers between devices: none -> 10.1 us  [the longest x5 6.3 us: swap_row(): return lax.ppermute(value, ('row', 'col'), pairs)]
    pallas_call x0 -> x2, Pallas kernels: none -> 9.84 us  [products(): pl.pallas_call(functools.partial(product_kernel, plan, width, depth), in_...]
    all_to_all x1 -> x0, waiting for transfers between devices: 7.98 us -> none  [shards(): lax.all_to_all(owned, 'row', split_axis=0, concat_axis=0, tiled=True)]
    all_to_all x1 -> x0, starting transfers between devices: 4.61 us -> none  [shards(): lax.all_to_all(owned, 'row', split_axis=0, concat_axis=0, tiled=True)]
  transfers between devices with their start and end apart: 3 -> 10, of which waited for: 3 -> 6; matrix products, arithmetic and copies ran while one was open for 1% -> 13% of each run, Pallas kernels for 0% -> 15%
where the time goes in v1:
time: 66.2 us; the launch traced here: 65.8 us
  waiting for transfers between devices  31.3 us (47%)
  starting transfers between devices  10.1 us (15%)
  Pallas kernels  9.84 us (15%)
  local copies, waits for them, and re-layouts  5.7 us (9%)
  other arithmetic  4.74 us (7%)
  matrix products  3.73 us (6%)
    ppermute x5, waiting for transfers between devices, swap_row(): return lax.ppermute(value, ('row', 'col'), pairs)  24.7 us
    pallas_call x2, Pallas kernels, products(): pl.pallas_call(functools.partial(product_kernel, plan, width, depth), in_...  9.84 us
    ppermute x2, waiting for transfers between devices, swap_col(): lax.ppermute(value, 'col', [(i, i ^ 1 << col_orders[i % 2][stage]) for i...  6.68 us
    ppermute x5, starting transfers between devices, swap_row(): return lax.ppermute(value, ('row', 'col'), pairs)  6.3 us
    ppermute x2, starting transfers between devices, swap_col(): lax.ppermute(value, 'col', [(i, i ^ 1 << col_orders[i % 2][stage]) for i...  3.08 us
  transfers between devices with their start and end apart: 10, of which 6 were waited for; matrix products, arithmetic and copies ran while one was open for 13% of the time, Pallas kernels for 15%

profile of v1, /device:TPU:0, one launch (start us, length us, event | category | flops | bytes accessed | tf_op | source)
XLA Modules:
  0.0 65.8 jit_solution(3411930278424242101)
XLA Ops:
  0.0 0.7 %compare_select_fusion.2 = s32[4]{0:T(128)S(1)} fusion(s32[4]{0:T(128)} %constant.45.clone, s32[4]{0:T(128)} %constant.46.clone, pred[]{:T(512)S(6)} %eq.6, s32[]{:T(128)S(6)} %axis_index.23), kind=kLoop, calls=%fused_computation.81 | loop fusion | flops 20 | bytes 53 | tf_op jit(solution)/shard_map/select_n | solution.py:163
  0.7 1.1 %fusion.50 = (bf16[1,512,256]{2,1,0:T(8,128)(2,1)S(1)}, bf16[1,512,256]{2,1,0:T(8,128)(2,1)S(1)}) fusion(bf16[2,512,256]{2,1,0:T(8,128)(2,1)} %param.24, s32[]{:T(128)S(6)} %select_n.114), kind=kLoop, calls=%fused_computation.95 | loop fusion | bytes 1048580 | tf_op jit(solution)/shard_map/slice | solution.py:211
  1.8 0.6 gather_fusion.1
  2.4 0.2 fusion.53
  2.7 3.1 %collective-permute-start.4 = (bf16[384,256]{1,0:T(8,128)(2,1)S(1)}, bf16[384,256]{1,0:T(8,128)(2,1)S(1)}, u32[]{:S(2)}, u32[]{:S(2)}) collective-permute-start(bf16[384,256]{1,0:T(8,128)(2,1)S(1)} %pad_maximum_fusion.3), channel_id=1, source_target_pairs={{0,8},{1,17},{2,10},{3,19},{4,12},{5,21},{6,14},{7,23},{8,0},{9,25... | collective-permute-start | bytes 589832 | tf_op jit(solution)/shard_map/ppermute | solution.py:148
  5.8 4.9 %shard_map.173 = (bf16[512,512]{1,0:T(8,128)(2,1)}, bf16[512,512]{1,0:T(8,128)(2,1)}) custom-call(bf16[512,2048]{1,0:T(8,128)(2,1)} %refs_0_.3, s32[2048]{0:T(1024)} %refs_1_.3, f32[2048]{0:T(1024)} %refs_2_.3, s32[2048]{0:T(1024)} %refs_3_.3, f32[2048]{0:T(1024)} %refs_4_.3, f32[2048]{0:T(1024)} %refs_5_.3), custom_call_target="tpu_custom_call" | custom-call | flops 2147483648 | bytes 3145728 | tf_op jit(solution)/shard_map/pallas_call | solution.py:97
  10.7 0.0 copy-start.5
  10.7 0.6 collective-permute-start.1
  11.4 4.9 %shard_map.172 = (bf16[512,512]{1,0:T(8,128)(2,1)}, bf16[512,512]{1,0:T(8,128)(2,1)}) custom-call(bf16[512,2048]{1,0:T(8,128)(2,1)} %refs_0_.3, s32[2048]{0:T(1024)} %refs_1_.3, f32[2048]{0:T(1024)} %refs_2_.3, s32[2048]{0:T(1024)} %refs_3_.3, f32[2048]{0:T(1024)} %refs_4_.3, f32[2048]{0:T(1024)} %refs_5_.3), custom_call_target="tpu_custom_call" | custom-call | flops 2147483648 | bytes 3145728 | tf_op jit(solution)/shard_map/pallas_call | solution.py:97
  16.3 0.1 collective-permute-start
  16.4 0.6 gather_fusion.2
  17.1 0.0 collective-permute-done.4
  17.2 0.6 copy-done.4
  17.8 2.6 %collective-permute-start.5 = (bf16[384,256]{1,0:T(8,128)(2,1)S(1)}, bf16[384,256]{1,0:T(8,128)(2,1)S(1)}, u32[]{:S(2)}, u32[]{:S(2)}) collective-permute-start(bf16[384,256]{1,0:T(8,128)(2,1)S(1)} %pad_maximum_fusion.4), channel_id=1, source_target_pairs={{0,16},{1,9},{2,18},{3,11},{4,20},{5,13},{6,22},{7,15},{8,24},{9,1... | collective-permute-start | bytes 589832 | tf_op jit(solution)/shard_map/ppermute | solution.py:148
  20.3 0.0 collective-permute-done.1
  20.3 0.9 %add_convert_fusion = bf16[512,512]{1,0:T(8,128)(2,1)} fusion(bf16[512,512]{1,0:T(8,128)(2,1)S(1)} %collective-permute-done.1, bf16[512,512]{1,0:T(8,128)(2,1)S(1)} %copy-done.3), kind=kLoop, calls=%fused_computation.12 | loop fusion | flops 1048576 | bytes 1572864 | tf_op jit(solution)/shard_map/convert_element_type | solution.py:202
  21.3 1.5 %collective-permute-start.2 = (bf16[512,512]{1,0:T(8,128)(2,1)}, bf16[512,512]{1,0:T(8,128)(2,1)S(1)}, u32[]{:S(2)}, u32[]{:S(2)}) collective-permute-start(bf16[512,512]{1,0:T(8,128)(2,1)} %add_convert_fusion), channel_id=1, source_target_pairs={{0,2},{1,5},{2,0},{3,7},{4,6},{5,1},{6,4},{7,3},{8,10},{9,13},{10,... | collective-permute-start | bytes 1572872 | tf_op jit(solution)/shard_map/ppermute | solution.py:140
  22.8 2.8 %collective-permute-done.5 = bf16[384,256]{1,0:T(8,128)(2,1)S(1)} collective-permute-done((bf16[384,256]{1,0:T(8,128)(2,1)S(1)}, bf16[384,256]{1,0:T(8,128)(2,1)S(1)}, u32[]{:S(2)}, u32[]{:S(2)}) %collective-permute-start.5) | collective-permute-done | bytes 196640 | tf_op jit(solution)/shard_map/ppermute | solution.py:148
  25.7 0.6 gather_fusion.3
  26.2 0.9 %fusion.49 = (bf16[128,256]{1,0:T(8,128)(2,1)S(1)}, f32[128,256]{1,0:T(8,128)S(1)}) fusion(bf16[384,256]{1,0:T(8,128)(2,1)S(1)} %collective-permute-done.5, f32[128,256]{1,0:T(8,128)S(1)} %get-tuple-element.28, bf16[384,256]{1,0:T(8,128)(2,1)} %copy-done.4), kind=kLoop, calls=%fused_computation.94 | loop fusion | flops 163840 | bytes 458752 | tf_op jit(solution)/shard_map/convert_element_type | solution.py:219
  27.1 0.8 %pad_maximum_fusion = bf16[640,256]{1,0:T(8,128)(2,1)} fusion(bf16[128,256]{1,0:T(8,128)(2,1)S(1)} %get-tuple-element.13, bf16[512,256]{1,0:T(8,128)(2,1)S(1)} %bitcast.62), kind=kLoop, calls=%fused_computation.23 | loop fusion | flops 655360 | bytes 655360 | tf_op jit(solution)/shard_map/concatenate | solution.py:219
  27.9 0.0 collective-permute-start.6
  27.9 0.0 collective-permute-done
  27.9 2.8 %collective-permute-done.2 = bf16[512,512]{1,0:T(8,128)(2,1)S(1)} collective-permute-done((bf16[512,512]{1,0:T(8,128)(2,1)}, bf16[512,512]{1,0:T(8,128)(2,1)S(1)}, u32[]{:S(2)}, u32[]{:S(2)}) %collective-permute-start.2) | collective-permute-done | bytes 524320 | tf_op jit(solution)/shard_map/ppermute | solution.py:140
  30.7 0.2 convert_add_fusion
  30.9 1.6 %collective-permute-start.3 = (bf16[512,256]{1,0:T(8,128)(2,1)S(1)}, bf16[512,256]{1,0:T(8,128)(2,1)S(1)}, u32[]{:S(2)}, u32[]{:S(2)}) collective-permute-start(bf16[512,256]{1,0:T(8,128)(2,1)S(1)} %slice.176), channel_id=1, source_target_pairs={{0,4},{1,3},{2,6},{3,1},{4,0},{5,7},{6,2},{7,5},{8,12},{9,11},{10,... | collective-permute-start | bytes 786440 | tf_op jit(solution)/shard_map/ppermute | solution.py:140
  32.5 0.0 collective-permute-done.6
  32.5 1.0 %slice.119 = bf16[512,256]{1,0:T(8,128)(2,1)S(1)} slice(bf16[640,256]{1,0:T(8,128)(2,1)} %collective-permute-done.6), slice={[0:512], [0:256]} | slice | bytes 524288 | tf_op jit(solution)/shard_map/slice | solution.py:220
  33.5 0.0 copy-start.1
  33.5 3.9 %collective-permute-done.3 = bf16[512,256]{1,0:T(8,128)(2,1)S(1)} collective-permute-done((bf16[512,256]{1,0:T(8,128)(2,1)S(1)}, bf16[512,256]{1,0:T(8,128)(2,1)S(1)}, u32[]{:S(2)}, u32[]{:S(2)}) %collective-permute-start.3) | collective-permute-done | bytes 262176 | tf_op jit(solution)/shard_map/ppermute | solution.py:140
  37.4 0.1 fusion.2
  37.5 0.3 fusion.3
  37.8 0.6 gather_fusion
  38.5 0.5 collective-permute-start.7
  39.0 0.0 copy-done.1
  39.0 0.4 convolution_convert_fusion
  39.4 0.9 %slice_convert_fusion.1 = f32[128,256]{1,0:T(8,128)S(1)} fusion(bf16[640,256]{1,0:T(8,128)(2,1)} %collective-permute-done.6), kind=kLoop, calls=%fused_computation.75 | loop fusion | flops 32768 | bytes 196608 | tf_op jit(solution)/shard_map/convert_element_type | solution.py:220
  40.3 7.1 %collective-permute-done.7 = bf16[512,256]{1,0:T(8,128)(2,1)S(1)} collective-permute-done((bf16[512,256]{1,0:T(8,128)(2,1)S(1)}, bf16[512,256]{1,0:T(8,128)(2,1)S(1)}, u32[]{:S(2)}, u32[]{:S(2)}) %collective-permute-start.7) | collective-permute-done | bytes 262176 | tf_op jit(solution)/shard_map/ppermute | solution.py:148
  47.4 0.1 collective-permute-start.8
  47.5 0.6 fusion.10
  48.1 0.4 fusion
  48.5 11.1 %collective-permute-done.8 = bf16[512,256]{1,0:T(8,128)(2,1)S(1)} collective-permute-done((bf16[512,256]{1,0:T(8,128)(2,1)S(1)}, bf16[512,256]{1,0:T(8,128)(2,1)S(1)}, u32[]{:S(2)}, u32[]{:S(2)}) %collective-permute-start.8) | collective-permute-done | bytes 262176 | tf_op jit(solution)/shard_map/ppermute | solution.py:148
  59.7 0.1 add_convert_fusion.1
  59.7 0.1 collective-permute-start.9
  59.8 0.7 %broadcast_select_fusion.1 = (bf16[512,256]{0,1:T(8,128)(2,1)S(1)}, bf16[512,256]{0,1:T(8,128)(2,1)S(1)}) fusion(bf16[512,256]{0,1:T(8,128)(2,1)S(1)} %convolution_convert_fusion, pred[]{:T(512)S(6)} %eq.6, f32[512,256]{1,0:T(8,128)S(1)} %fusion, f32[2,256,256]{2,1,0:T(8,128)S(1)} %copy-done.1), kind=kOutput, calls=%fused_computation.58 | convolution fusion | flops 403046400 | bytes 1572865 | tf_op jit(solution)/shard_map/dot_general | solution.py:228
  60.5 0.6 gather_fusion.4
  61.1 3.6 %collective-permute-done.9 = bf16[256,256]{1,0:T(8,128)(2,1)S(1)} collective-permute-done((bf16[256,256]{1,0:T(8,128)(2,1)S(1)}, bf16[256,256]{1,0:T(8,128)(2,1)S(1)}, u32[]{:S(2)}, u32[]{:S(2)}) %collective-permute-start.9) | collective-permute-done | bytes 131104 | tf_op jit(solution)/shard_map/ppermute | solution.py:148
  64.8 1.1 %fusion.1 = bf16[512,256]{1,0:T(8,128)(2,1)} fusion(bf16[512,256]{0,1:T(8,128)(2,1)S(1)} %get-tuple-element.16, bf16[512,256]{0,1:T(8,128)(2,1)S(1)} %get-tuple-element.15, bf16[512,256]{1,0:T(8,128)(2,1)S(1)} %bitcast.76, bf16[256,256]{1,0:T(8,128)(2,1)S(1)} %collective-permute-done.9, bf16[256,256]{1,0:T(8,128)(2,1)S(1)} %add_convert_fusion.1, pred[]{:T(512)S(6)} %eq.7), kind=kOutput, calls=%fused_computation.8 | convolution fusion | flops 136839168 | bytes 1310721 | tf_op jit(solution)/shard_map/dot_general | solution.py:263
  (32 shorter events, 0.4 us)
Async XLA Ops:
  0.0 2.4 %copy-start = (bf16[2,512,256]{2,1,0:T(8,128)(2,1)S(1)}, bf16[2,512,256]{2,1,0:T(8,128)(2,1)}, u32[]{:S(2)}) copy-start(bf16[2,512,256]{2,1,0:T(8,128)(2,1)} %param.24) | copy-start | bytes 1572868
  2.7 14.4 %collective-permute-start.4 = (bf16[384,256]{1,0:T(8,128)(2,1)S(1)}, bf16[384,256]{1,0:T(8,128)(2,1)S(1)}, u32[]{:S(2)}, u32[]{:S(2)}) collective-permute-start(bf16[384,256]{1,0:T(8,128)(2,1)S(1)} %pad_maximum_fusion.3), channel_id=1, source_target_pairs={{0,8},{1,17},{2,10},{3,19},{4,12},{5,21},{6,14},{7,23},{8,0},{9,25... | collective-permute-start | bytes 589832 | tf_op jit(solution)/shard_map/ppermute | solution.py:148
  10.7 5.7 %copy-start.5 = (s32[4]{0:T(128)S(1)}, s32[4]{0:T(128)}, u32[]{:S(2)}) copy-start(s32[4]{0:T(128)} %constant.47.clone) | copy-start | bytes 52
  10.7 9.6 %collective-permute-start.1 = (bf16[512,512]{1,0:T(8,128)(2,1)}, bf16[512,512]{1,0:T(8,128)(2,1)S(1)}, u32[]{:S(2)}, u32[]{:S(2)}) collective-permute-start(bf16[512,512]{1,0:T(8,128)(2,1)} %get-tuple-element.12), channel_id=1, source_target_pairs={{0,1},{1,0},{2,3},{3,2},{4,5},{5,4},{6,7},{7,6},{8,9},{9,8},{10,11... | collective-permute-start | bytes 1572872 | tf_op jit(solution)/shard_map/ppermute | solution.py:137
  16.3 4.1 %copy-start.3 = (bf16[512,512]{1,0:T(8,128)(2,1)S(1)}, bf16[512,512]{1,0:T(8,128)(2,1)}, u32[]{:S(2)}) copy-start(bf16[512,512]{1,0:T(8,128)(2,1)} %get-tuple-element.11) | copy-start | bytes 1572868
  16.3 11.6 %collective-permute-start = (bf16[512,512]{1,0:T(8,128)(2,1)}, bf16[512,512]{1,0:T(8,128)(2,1)S(1)}, u32[]{:S(2)}, u32[]{:S(2)}) collective-permute-start(bf16[512,512]{1,0:T(8,128)(2,1)} %get-tuple-element.10), channel_id=1, source_target_pairs={{0,1},{1,0},{2,3},{3,2},{4,5},{5,4},{6,7},{7,6},{8,9},{9,8},{10,11... | collective-permute-start | bytes 1572872 | tf_op jit(solution)/shard_map/ppermute | solution.py:137
  17.1 0.7 %copy-start.4 = (bf16[384,256]{1,0:T(8,128)(2,1)}, bf16[384,256]{1,0:T(8,128)(2,1)S(1)}, u32[]{:S(2)}) copy-start(bf16[384,256]{1,0:T(8,128)(2,1)S(1)} %collective-permute-done.4) | copy-start | bytes 589828
  17.8 12.9 %copy-start.2 = (bf16[512,512]{1,0:T(8,128)(2,1)S(1)}, bf16[512,512]{1,0:T(8,128)(2,1)}, u32[]{:S(2)}) copy-start(bf16[512,512]{1,0:T(8,128)(2,1)} %get-tuple-element.9) | copy-start | bytes 1572868
  17.8 7.8 %collective-permute-start.5 = (bf16[384,256]{1,0:T(8,128)(2,1)S(1)}, bf16[384,256]{1,0:T(8,128)(2,1)S(1)}, u32[]{:S(2)}, u32[]{:S(2)}) collective-permute-start(bf16[384,256]{1,0:T(8,128)(2,1)S(1)} %pad_maximum_fusion.4), channel_id=1, source_target_pairs={{0,16},{1,9},{2,18},{3,11},{4,20},{5,13},{6,22},{7,15},{8,24},{9,1... | collective-permute-start | bytes 589832 | tf_op jit(solution)/shard_map/ppermute | solution.py:148
  21.3 9.4 %collective-permute-start.2 = (bf16[512,512]{1,0:T(8,128)(2,1)}, bf16[512,512]{1,0:T(8,128)(2,1)S(1)}, u32[]{:S(2)}, u32[]{:S(2)}) collective-permute-start(bf16[512,512]{1,0:T(8,128)(2,1)} %add_convert_fusion), channel_id=1, source_target_pairs={{0,2},{1,5},{2,0},{3,7},{4,6},{5,1},{6,4},{7,3},{8,10},{9,13},{10,... | collective-permute-start | bytes 1572872 | tf_op jit(solution)/shard_map/ppermute | solution.py:140
  27.9 4.7 %collective-permute-start.6 = (bf16[640,256]{1,0:T(8,128)(2,1)}, bf16[640,256]{1,0:T(8,128)(2,1)}, u32[]{:S(2)}, u32[]{:S(2)}) collective-permute-start(bf16[640,256]{1,0:T(8,128)(2,1)} %pad_maximum_fusion), channel_id=1, source_target_pairs={{0,1},{1,0},{2,3},{3,2},{4,5},{5,4},{6,7},{7,6},{8,9},{9,8},{10,11... | collective-permute-start | bytes 983048 | tf_op jit(solution)/shard_map/ppermute | solution.py:137
  30.9 6.4 %collective-permute-start.3 = (bf16[512,256]{1,0:T(8,128)(2,1)S(1)}, bf16[512,256]{1,0:T(8,128)(2,1)S(1)}, u32[]{:S(2)}, u32[]{:S(2)}) collective-permute-start(bf16[512,256]{1,0:T(8,128)(2,1)S(1)} %slice.176), channel_id=1, source_target_pairs={{0,4},{1,3},{2,6},{3,1},{4,0},{5,7},{6,2},{7,5},{8,12},{9,11},{10,... | collective-permute-start | bytes 786440 | tf_op jit(solution)/shard_map/ppermute | solution.py:140
  33.5 5.5 %copy-start.1 = (f32[2,256,256]{2,1,0:T(8,128)S(1)}, f32[2,256,256]{2,1,0:T(8,128)}, u32[]{:S(2)}) copy-start(f32[2,256,256]{2,1,0:T(8,128)} %param.25) | copy-start | bytes 1572868
  38.5 8.9 %collective-permute-start.7 = (bf16[512,256]{1,0:T(8,128)(2,1)S(1)}, bf16[512,256]{1,0:T(8,128)(2,1)S(1)}, u32[]{:S(2)}, u32[]{:S(2)}) collective-permute-start(bf16[512,256]{1,0:T(8,128)(2,1)S(1)} %pad_maximum_fusion.1), channel_id=1, source_target_pairs={{0,8},{1,17},{2,10},{3,19},{4,12},{5,21},{6,14},{7,23},{8,0},{9,25... | collective-permute-start | bytes 786440 | tf_op jit(solution)/shard_map/ppermute | solution.py:148
  47.4 12.2 %collective-permute-start.8 = (bf16[512,256]{1,0:T(8,128)(2,1)S(1)}, bf16[512,256]{1,0:T(8,128)(2,1)S(1)}, u32[]{:S(2)}, u32[]{:S(2)}) collective-permute-start(bf16[512,256]{1,0:T(8,128)(2,1)S(1)} %pad_maximum_fusion.2), channel_id=1, source_target_pairs={{0,16},{1,9},{2,18},{3,11},{4,20},{5,13},{6,22},{7,15},{8,24},{9,1... | collective-permute-start | bytes 786440 | tf_op jit(solution)/shard_map/ppermute | solution.py:148
  59.7 5.0 %collective-permute-start.9 = (bf16[256,256]{1,0:T(8,128)(2,1)S(1)}, bf16[256,256]{1,0:T(8,128)(2,1)S(1)}, u32[]{:S(2)}, u32[]{:S(2)}) collective-permute-start(bf16[256,256]{1,0:T(8,128)(2,1)S(1)} %add_convert_fusion.1), channel_id=1, source_target_pairs={{0,8},{1,17},{2,10},{3,19},{4,12},{5,21},{6,14},{7,23},{8,0},{9,25... | collective-permute-start | bytes 393224 | tf_op jit(solution)/shard_map/ppermute | solution.py:148

commit v2 on v0

v2 whole, which is shorter than its diff:
```python
import functools

import jax
import jax.numpy as jnp
from jax import lax
from jax.experimental import pallas as pl
from jax.experimental.pallas import tpu as pltpu
from jax.sharding import PartitionSpec as P

BF = jnp.bfloat16
F32 = jnp.float32
HIGHEST = lax.Precision.HIGHEST
MIB = 2**20
CHUNKS = 1


def bit_orders(size, first):
    bits = list(range(first, size.bit_length() - 1))
    half = len(bits) // 2
    return bits, bits[half:] + bits[:half]


def target_codes(bits):
    if not bits:
        return [0]
    rest = target_codes(bits[1:])
    return rest + [(1 << bits[0]) | code for code in rest]


def source_codes(bits):
    codes = [0]
    for bit in bits:
        codes = codes + [(1 << bit) | code for code in codes]
    return codes


def other_places(orders):
    even, odd = [target_codes(order) for order in orders]
    places = [even.index(code) for code in odd]
    assert places == [odd.index(code) for code in even]
    return places


def is_even():
    return lax.rem(lax.axis_index("col"), 2) == 0


def select_code(even, pair):
    return pair[0] if pair[0] == pair[1] else jnp.where(even, pair[0], pair[1])


def row_bit(row_orders, stage):
    shift = select_code(is_even(), (row_orders[0][stage], row_orders[1][stage]))
    return jnp.bitwise_and(lax.shift_right_logical(lax.axis_index("row"), shift), 1) == 0


def swap_groups(value, axis, row_orders):
    size = value.shape[axis]
    for stage in range(len(row_orders[0]) - 1):
        step = size >> (stage + 1)
        pieces = [lax.slice_in_dim(value, i, i + step, axis=axis) for i in range(0, size, step)]
        flipped = jnp.concatenate([pieces[i ^ 1] for i in range(len(pieces))], axis)
        value = jnp.where(row_bit(row_orders, stage), value, flipped)
    return value


def local(fn, outs, values, after=()):
    outs = [jax.ShapeDtypeStruct(shape, dtype) for shape, dtype in outs]
    if any(v.shape[-1] % 128 or v.shape[-2] % 16 for v in list(values) + outs):
        return list(fn(*values))

    def kernel(*refs):
        ins = refs[:len(values)]
        results = fn(*[ref[...] for ref in ins])
        for ref, result in zip(refs[len(values) + len(after):], results):
            ref[...] = result

    return list(
        pl.pallas_call(
            kernel,
            in_specs=[pl.BlockSpec(memory_space=pltpu.VMEM)] * len(values)
            + [pl.BlockSpec(memory_space=pl.ANY)] * len(after),
            out_specs=[pl.BlockSpec(memory_space=pltpu.VMEM)] * len(outs),
            out_shape=[pltpu.VMEM(o.shape, o.dtype) for o in outs],
            compiler_params=pltpu.CompilerParams(vmem_limit_bytes=16 * MIB),
            cost_estimate=pl.CostEstimate(flops=1, bytes_accessed=1, transcendentals=0),
        )(*[pltpu.with_memory_space_constraint(v, pltpu.VMEM) for v in values], *after)
    )


def product_kernel(plan, row_codes, row_places, width, depth, n_after, *refs):
    eig_hbm, order_hbm, weight_hbm, gap_hbm, shift_hbm, scale_hbm = refs[:6]
    refs = refs[6 + n_after:]
    outs = refs[:len(plan)]
    eig, order, weight, gap, shift, scale, eig_sem, small_sem = refs[len(plan):]
    rows, poles = eig.shape
    me = lax.axis_index("col")
    row = lax.axis_index("row")
    even = is_even()
    small = [
        pltpu.make_async_copy(src, dst, small_sem.at[i])
        for i, (src, dst) in enumerate(
            [(order_hbm, order), (gap_hbm, gap), (shift_hbm, shift), (weight_hbm, weight), (scale_hbm, scale)]
        )
    ]
    pieces = range(0, poles, depth)
    block = rows // len(row_codes)
    large = []
    for i, k in enumerate(pieces):
        group = []
        for place, pair in enumerate(row_codes):
            start = pl.multiple_of(jnp.bitwise_xor(row, select_code(even, pair)) * block, block)
            group.append(
                pltpu.make_async_copy(
                    eig_hbm.at[pl.ds(start, block), k:k + depth],
                    eig.at[place * block:(place + 1) * block, k:k + depth],
                    eig_sem.at[i, place],
                )
            )
        large.append(group)
    for copy in small + sum(large, []):
        copy.start()
    for copy in small:
        copy.wait()
    pole_values = (2.0 * order[...].astype(F32)).reshape(1, poles)
    weights = weight[...].reshape(1, poles)
    first = True
    for out, codes, places in zip(outs, plan, row_places):
        piece = width // CHUNKS
        for place, pair in enumerate(codes):
            start = pl.multiple_of(jnp.bitwise_xor(me, select_code(even, pair)) * width, width)
            roots = 2.0 * gap[pl.ds(start, width)].astype(F32) + 1.0 + shift[pl.ds(start, width)]
            roots = roots.reshape(1, width)
            roots = jnp.concatenate(
                [jnp.broadcast_to(roots[:, j:j + 128], (128, 128)).T for j in range(0, width, 128)], 0
            )
            total = None
            for i, k in enumerate(pieces):
                if first:
                    for copy in large[i]:
                        copy.wait()
                gaps = pole_values[:, k:k + depth] - jnp.concatenate([roots] * (depth // 128), 1)
                matrix = (weights[:, k:k + depth] / gaps).astype(BF)
                term = lax.dot_general(
                    eig[:, k:k + depth], matrix, (((1,), (1,)), ((), ())), preferred_element_type=F32
                )
                total = term if total is None else total + term
            first = False
            total = (total * scale[pl.ds(start, width)].reshape(1, width)).astype(BF)
            for chunk in range(CHUNKS):
                at = (chunk * len(codes) + place) * piece
                columns = total[:, chunk * piece:(chunk + 1) * piece]
                for target, source in enumerate(places):
                    out[target * block:(target + 1) * block, at:at + piece] = columns[
                        source * block:(source + 1) * block
                    ]


def products(plan, row_codes, row_places, parts, operands, after=()):
    eigvecs, pole_order, pole_weight, root_gap, root_shift, column_weight = operands
    rows, poles = eigvecs.shape
    roots = root_gap.shape[0]
    width = roots // parts
    if width % (128 * CHUNKS) or poles % 256:
        me = lax.axis_index("col")
        numbers = lambda pairs: jnp.array([[a, b] for a, b in pairs], jnp.int32)
        places = numbers(row_codes)
        places = jnp.bitwise_xor(lax.axis_index("row"), jnp.where(is_even(), places[:, 0], places[:, 1]))
        ordered = eigvecs.reshape(len(row_codes), -1, poles)[places].reshape(rows, poles)
        results = []
        for codes, row_place in zip(plan, row_places):
            places = numbers(codes)
            places = jnp.bitwise_xor(me, jnp.where(is_even(), places[:, 0], places[:, 1]))
            pick = lambda v: v.reshape(parts, CHUNKS, -1)[places].transpose(1, 0, 2).reshape(-1)
            root_values = 2.0 * pick(root_gap).astype(F32) + 1.0 + pick(root_shift)
            numer = pole_weight[:, None] * pick(column_weight)[None, :]
            gaps = 2.0 * pole_order.astype(F32)[:, None] - root_values[None, :]
            matrix = (numer / gaps).astype(BF)
            result = jnp.dot(ordered, matrix, preferred_element_type=F32).astype(BF)
            result = result.reshape(len(row_codes), -1, result.shape[1])
            results.append(jnp.concatenate([result[i] for i in row_place], 0))
        return results
    depth = poles // 2
    return pl.pallas_call(
        functools.partial(product_kernel, plan, row_codes, row_places, width, depth, len(after)),
        in_specs=[pl.BlockSpec(memory_space=pl.ANY)] * (6 + len(after)),
        out_specs=[pl.BlockSpec(memory_space=pltpu.VMEM)] * len(plan),
        out_shape=[pltpu.VMEM((rows, width * len(codes)), BF) for codes in plan],
        scratch_shapes=[
            pltpu.VMEM((rows, poles), BF),
            pltpu.VMEM((poles,), jnp.int32),
            pltpu.VMEM((poles,), F32),
            pltpu.VMEM((roots,), jnp.int32),
            pltpu.VMEM((roots,), F32),
            pltpu.VMEM((roots,), F32),
            pltpu.SemaphoreType.DMA((2, len(row_codes))),
            pltpu.SemaphoreType.DMA((5,)),
        ],
        compiler_params=pltpu.CompilerParams(vmem_limit_bytes=24 * MIB),
        cost_estimate=pl.CostEstimate(flops=1, bytes_accessed=1, transcendentals=0),
    )(*[pltpu.with_memory_space_constraint(operand, pltpu.HBM) for operand in operands], *after)


def panel_kernel(row_orders, blocks, near, *refs):
    panel, vectors_out, correlation_out = refs[:3]
    mine_out = refs[3:]
    even = is_even()
    row = lax.axis_index("row")
    block = panel.shape[1] // blocks
    sources = list(zip(*[source_codes(order) for order in row_orders]))
    targets = list(zip(*[target_codes(order) for order in row_orders]))
    at = lambda pair: pl.ds(pl.multiple_of(jnp.bitwise_xor(row, select_code(even, pair)) * block, block), block)
    for place, pair in enumerate(sources):
        vectors_out[0, place * block:(place + 1) * block] = panel[0, at(pair)]
        vectors_out[1, place * block:(place + 1) * block] = panel[1, at(pair)]
    core = jnp.where(even, 0, 1)
    for out, pair in zip(mine_out, targets):
        out[...] = panel[core, at(pair)]
    half = panel[1, :, pl.ds(pl.multiple_of(core * near, near), near)]
    correlation_out[...] = lax.dot_general(
        half, panel[0], (((0,), (0,)), ((), ())), preferred_element_type=F32
    ).astype(BF)


def panel_blocks(row_orders, panel_vectors):
    panels, rows, width = panel_vectors.shape
    blocks = 1 << len(row_orders[0])
    near = width // 2
    shapes = [(panels, rows, width), (near, width)] + [(rows // blocks, width)] * blocks
    return pl.pallas_call(
        functools.partial(panel_kernel, row_orders, blocks, near),
        in_specs=[pl.BlockSpec(memory_space=pltpu.VMEM)],
        out_specs=[pl.BlockSpec(memory_space=pltpu.VMEM)] * len(shapes),
        out_shape=[pltpu.VMEM(shape, BF) for shape in shapes],
        compiler_params=pltpu.CompilerParams(vmem_limit_bytes=16 * MIB),
        cost_estimate=pl.CostEstimate(flops=1, bytes_accessed=1, transcendentals=0),
    )(pltpu.with_memory_space_constraint(panel_vectors, pltpu.VMEM))


def finish_kernel(row_orders, blocks, refs_in, *refs):
    totals, update, project, out_hbm, result, sem = refs
    rows = totals.shape[0]
    block = rows // blocks
    even = is_even()
    row = lax.axis_index("row")
    sources = list(zip(*[source_codes(order) for order in row_orders]))
    value = totals[...] - jnp.dot(update[...], project[...], preferred_element_type=F32)
    result[...] = value.astype(BF)
    copies = []
    for place, pair in enumerate(sources):
        start = pl.multiple_of(jnp.bitwise_xor(row, select_code(even, pair)) * block, block)
        copies.append(
            pltpu.make_async_copy(
                result.at[place * block:(place + 1) * block], out_hbm.at[pl.ds(start, block)], sem.at[place]
            )
        )
    for copy in copies:
        copy.start()
    for copy in copies:
        copy.wait()


def finish(row_orders, totals, update, project):
    rows, width = totals.shape
    blocks = 1 << len(row_orders[0])
    if width % 128:
        result = (totals - jnp.dot(update, project, preferred_element_type=F32)).astype(BF)
        result = result.reshape(blocks, -1, width)
        sources = [source_codes(order) for order in row_orders]
        ordered = [[s.index(code) for code in range(blocks)] for s in sources]
        places = jnp.where(is_even(), jnp.array(ordered[0]), jnp.array(ordered[1]))
        return result[places[jnp.bitwise_xor(lax.axis_index("row"), jnp.arange(blocks))]].reshape(rows, width)
    return pl.pallas_call(
        functools.partial(finish_kernel, row_orders, blocks, None),
        in_specs=[pl.BlockSpec(memory_space=pltpu.VMEM)] * 3,
        out_specs=pl.BlockSpec(memory_space=pl.ANY),
        out_shape=jax.ShapeDtypeStruct((rows, width), BF),
        scratch_shapes=[pltpu.VMEM((rows, width), BF), pltpu.SemaphoreType.DMA((blocks,))],
        compiler_params=pltpu.CompilerParams(vmem_limit_bytes=16 * MIB),
        cost_estimate=pl.CostEstimate(flops=1, bytes_accessed=1, transcendentals=0),
    )(*[pltpu.with_memory_space_constraint(v, pltpu.VMEM) for v in (totals, update, project)])


def shards(
    n_row,
    n_col,
    eigvecs,
    pole_order,
    pole_weight,
    root_gap,
    root_shift,
    column_weight,
    panel_vectors,
    panel_factors,
):
    col_orders = bit_orders(n_col, 1)
    row_orders = bit_orders(n_row, 0)
    col_stages = len(col_orders[0])
    row_stages = len(row_orders[0])
    rows = eigvecs.shape[0]
    block = rows // n_row
    panel_width = panel_vectors.shape[2]
    near = panel_width // 2

    def swap_cores(value):
        return lax.ppermute(value, "col", [(i, i ^ 1) for i in range(n_col)])

    def swap_col(value, stage):
        return lax.ppermute(value, "col", [(i, i ^ (1 << col_orders[i % 2][stage])) for i in range(n_col)])

    def swap_row(value, stage):
        pairs = [
            (r * n_col + c, (r ^ (1 << row_orders[c % 2][stage])) * n_col + c)
            for r in range(n_row)
            for c in range(n_col)
        ]
        return lax.ppermute(value, ("row", "col"), pairs)

    def split_targets(blocks):
        sources, targets = blocks
        count = sum(s.shape[0] for s in sources) // (targets * block)
        kept, sent = [], []
        for source in sources:
            for i in range(0, source.shape[0], targets * block):
                middle = i + targets * block // 2
                kept.append(source[i:middle])
                sent.append(source[middle:i + targets * block])
        return jnp.concatenate(kept, 0), jnp.concatenate(sent, 0)

    targets = list(zip(*[target_codes(order) for order in row_orders]))
    own_codes = list(zip(*[target_codes(order) for order in col_orders]))
    other_codes = [(1 ^ odd, 1 ^ even) for even, odd in own_codes]
    half = len(own_codes) // 2
    operands = (eigvecs, pole_order, pole_weight, root_gap, root_shift, column_weight)
    other_rows = other_places(row_orders)
    row_places = [other_rows, list(range(n_row))]
    other_sent, own_sent = products(
        [other_codes[half:], own_codes[half:]], targets, row_places, n_col, operands
    )
    got_sent = swap_cores(other_sent)
    (sent,) = local(
        lambda a, b: [(a.astype(F32) + b.astype(F32)).astype(BF)], [(own_sent.shape, BF)], [own_sent, got_sent]
    )
    got = swap_col(sent, 0)

    vectors, correlation, *mine = panel_blocks(row_orders, panel_vectors)
    codes = list(zip(*[target_codes(order) for order in row_orders]))[1:]

    def send_to(value, pair):
        pairs = [(r * n_col + c, (r ^ pair[c % 2]) * n_col + c) for r in range(n_row) for c in range(n_col)]
        return lax.ppermute(value, ("row", "col"), pairs)

    panel_got = [send_to(message, pair) for message, pair in zip(mine[1:], codes)]
    correlation_got = [send_to(correlation, pair) for pair in codes]
    other_kept, own_kept = products(
        [other_codes[:half], own_codes[:half]], targets, row_places, n_col, operands, after=(sent, vectors)
    )
    got_kept = swap_cores(other_kept)

    piece = own_kept.shape[1] // 2 if col_stages > 1 else own_kept.shape[1]

    (current,) = local(
        lambda kept, got: [kept.astype(F32) + got.astype(F32)], [(own_kept.shape, F32)], [own_kept, got]
    )

    def first_sum(current, got):
        total = current + got.astype(F32)
        return total[:, :piece], total[:, piece:].astype(BF)

    current, sent = local(first_sum, [((rows, piece), F32), ((rows, piece), BF)], [current, got_kept])
    for stage in range(1, col_stages):
        got = swap_col(sent, stage)
        if stage < col_stages - 1:
            piece = piece // 2

            def next_sum(current, got, piece=piece):
                total = current + got.astype(F32)
                return total[:, :piece], total[:, piece:].astype(BF)

            current, sent = local(next_sum, [((rows, piece), F32), ((rows, piece), BF)], [current, got])

    mine_all, mine_sent = local(
        lambda *parts: [jnp.concatenate(parts, 0), jnp.concatenate([parts[i] for i in other_rows], 0)],
        [((rows, panel_width), BF)] * 2,
        mine[:1] + panel_got,
        after=(sent,),
    )
    other_all = swap_cores(mine_sent)

    width = piece

    (merged,) = local(
        lambda current, got: [(current + got.astype(F32)).astype(BF)], [((rows, width), BF)], [current, got]
    )

    def projections(merged, mine_all, other_all):
        dims = (((0,), (0,)), ((), ()))
        project = jnp.concatenate(
            [
                lax.dot_general(v, merged, dims, preferred_element_type=F32)
                for v in (mine_all, other_all)
            ],
            0,
        )
        project = swap_groups(project, 0, row_orders)
        middle = project.shape[0] // 2
        kept, moved = split_targets(([merged], n_row))
        if row_stages == 1:
            return project, project.astype(BF), kept, moved
        return project[:middle], project[middle:].astype(BF), kept, moved

    wide = 2 * panel_width
    kept_rows = wide // 2 if row_stages > 1 else wide
    project, project_sent, blocks, blocks_sent = local(
        projections,
        [((kept_rows, width), F32), ((kept_rows, width), BF), ((rows // 2, width), BF), ((rows // 2, width), BF)],
        [merged, mine_all, other_all],
    )
    project_got = swap_row(project_sent, 0)
    blocks_got = swap_row(blocks_sent, 0)

    def correlation_sum(*parts):
        return [sum(part.astype(F32) for part in parts).astype(BF)]

    (correlation,) = local(
        correlation_sum, [((near, panel_width), BF)], [correlation] + correlation_got, after=(merged,)
    )
    other_correlation = swap_cores(correlation)

    def update_factor(first_vectors, second_vectors, factor_first, factor_second, mine, other):
        mine, other = mine.astype(F32), other.astype(F32)
        even = is_even()
        correlation = jnp.concatenate([jnp.where(even, mine, other), jnp.where(even, other, mine)], 0)
        second_vectors = second_vectors.astype(F32)
        across = jnp.dot(factor_second, correlation, precision=HIGHEST, preferred_element_type=F32)
        across = jnp.dot(second_vectors, across, precision=HIGHEST, preferred_element_type=F32)
        across = first_vectors.astype(F32) - across
        first = jnp.dot(across, factor_first, precision=HIGHEST, preferred_element_type=F32)
        second = jnp.dot(second_vectors, factor_second, precision=HIGHEST, preferred_element_type=F32)
        update = jnp.concatenate([jnp.where(even, first, second), jnp.where(even, second, first)], 1)
        return [swap_groups(update, 1, row_orders).astype(BF)]

    (update,) = local(
        update_factor,
        [((rows, wide), BF)],
        [vectors[0], vectors[1], panel_factors[0], panel_factors[1], correlation, other_correlation],
        after=(project_sent,),
    )

    for stage in range(1, row_stages):
        last = stage == row_stages - 1
        middle = kept_rows if last else kept_rows // 2

        def next_project(project, got, last=last, middle=middle):
            total = project + got.astype(F32)
            if last:
                return total, total.astype(BF)
            return total[:middle], total[middle:].astype(BF)

        project, project_sent = local(
            next_project, [((middle, width), F32), ((middle, width), BF)], [project, project_got]
        )
        kept_rows = middle
        project_got = swap_row(project_sent, stage)
        blocks, blocks_sent = local(
            lambda blocks, got, targets=n_row >> stage: split_targets(([jnp.concatenate([blocks, got], 0)], targets)),
            [((rows // 2, width), BF), ((rows // 2, width), BF)],
            [blocks, blocks_got],
            after=(project_sent,),
        )
        blocks_got = swap_row(blocks_sent, stage)
    (project,) = local(
        lambda project, got: [(project + got.astype(F32)).astype(BF)], [((kept_rows, width), BF)], [project, project_got]
    )
    total = None
    start = 0
    for stage in reversed(range(row_stages - 1)):
        got = swap_row(project, stage)
        if total is None:
            (total,) = local(
                lambda blocks, blocks_got, update, project: [
                    jnp.concatenate([blocks, blocks_got], 0).astype(F32)
                    - jnp.dot(update[:, :project.shape[0]], project, preferred_element_type=F32)
                ],
                [((rows, width), F32)],
                [blocks, blocks_got, update, project],
                after=(project,),
            )
            start = project.shape[0]
        if stage > 0:
            project = jnp.concatenate([project, got], 0)
        else:
            rest = got if row_stages == 2 else jnp.concatenate([project, got], 0)[start:]
    return finish(row_orders, total, update[:, start:], rest)


def solution(mesh):
    return jax.shard_map(
        functools.partial(shards, mesh.shape["row"], mesh.shape["col"]),
        mesh=mesh,
        in_specs=(P("row", "col"), P("col"), P("col"), P(), P(), P(), P(None, "row", None), P()),
        out_specs=P("row", "col"),
        check_vma=False,
    )
```

time: 124 us -> 52.5 us (0.42)
  waiting for transfers between devices: 87.6 us -> 21.8 us
  matrix products: 14.3 us -> 0 us
  between operations: 13.4 us -> 0.18 us
  Pallas kernels: 0 us -> 12.9 us
  starting transfers between devices: 4.61 us -> 17.3 us
  local copies, waits for them, and re-layouts: 3.3 us -> 0.1 us
    reduce_scatter x1 -> x0, waiting for transfers between devices: 44 us -> none  [shards(): lax.psum_scatter(partial_value.astype(jnp.bfloat16), 'col', scatter_dimen...]
    psum x1 -> x0, waiting for transfers between devices: 35.5 us -> none  [shards(): lax.psum(correlation_local.astype(jnp.bfloat16), 'row').astype(jnp.float32)]
    ppermute x0 -> x17, waiting for transfers between devices: none -> 21.8 us  [the longest x5 12.4 us: swap_row(): return lax.ppermute(value, ('row', 'col'), pairs)]
    ppermute x0 -> x17, starting transfers between devices: none -> 17.3 us  [the longest x6 9.09 us: send_to(): return lax.ppermute(value, ('row', 'col'), pairs)]
    dot_general x9 -> x0, matrix products: 14.3 us -> none  [the longest x1 7.78 us: shards(): partial_value = jnp.dot(eigvecs, matrix, preferred_element_type=jnp.float32)]
    pallas_call x0 -> x16, Pallas kernels: none -> 12.9 us  [the longest x2 8.44 us: products(): pl.pallas_call(functools.partial(product_kernel, plan, row_codes, row_pla...]
    all_to_all x1 -> x0, waiting for transfers between devices: 7.98 us -> none  [shards(): lax.all_to_all(owned, 'row', split_axis=0, concat_axis=0, tiled=True)]
    all_to_all x1 -> x0, starting transfers between devices: 4.61 us -> none  [shards(): lax.all_to_all(owned, 'row', split_axis=0, concat_axis=0, tiled=True)]
  transfers between devices with their start and end apart: 3 -> 17, of which waited for: 3 -> 12; matrix products, arithmetic and copies ran while one was open for 1% -> 0% of each run, Pallas kernels for 0% -> 14%
where the time goes in v2:
time: 52.5 us; the launch traced here: 52.3 us
  waiting for transfers between devices  21.8 us (42%)
  starting transfers between devices  17.3 us (33%)
  Pallas kernels  12.9 us (25%)
    ppermute x5, waiting for transfers between devices, swap_row(): return lax.ppermute(value, ('row', 'col'), pairs)  12.4 us
    ppermute x6, starting transfers between devices, send_to(): return lax.ppermute(value, ('row', 'col'), pairs)  9.09 us
    pallas_call x2, Pallas kernels, products(): pl.pallas_call(functools.partial(product_kernel, plan, row_codes, row_pla...  8.44 us
    ppermute x6, waiting for transfers between devices, send_to(): return lax.ppermute(value, ('row', 'col'), pairs)  6.62 us
    ppermute x2, starting transfers between devices, swap_col(): lax.ppermute(value, 'col', [(i, i ^ 1 << col_orders[i % 2][stage]) for i...  4.51 us
    pallas_call x12, Pallas kernels, local(): pl.pallas_call(kernel, in_specs=[pl.BlockSpec(memory_space=pltpu.VMEM)] *...  3.22 us
    ppermute x5, starting transfers between devices, swap_row(): return lax.ppermute(value, ('row', 'col'), pairs)  2.35 us
    ppermute x4, waiting for transfers between devices, swap_cores(): return lax.ppermute(value, 'col', [(i, i ^ 1) for i in range(n_col)])  2.01 us
  transfers between devices with their start and end apart: 17, of which 12 were waited for; matrix products, arithmetic and copies ran while one was open for 0% of the time, Pallas kernels for 14%

profile of v2, /device:TPU:0, one launch (start us, length us, event | category | flops | bytes accessed | tf_op | source)
XLA Modules:
  0.0 52.3 jit_solution(5324616312099248816)
XLA Ops:
  0.0 0.0 copy-start
  0.0 4.2 %shard_map.82 = (bf16[512,512]{1,0:T(8,128)(2,1)S(1)}, bf16[512,512]{1,0:T(8,128)(2,1)S(1)}) custom-call(bf16[512,2048]{1,0:T(8,128)(2,1)} %refs_0_.5, s32[2048]{0:T(1024)} %refs_1_.3, f32[2048]{0:T(1024)} %refs_2_.3, s32[2048]{0:T(1024)} %refs_3_.3, f32[2048]{0:T(1024)} %refs_4_.3, f32[2048]{0:T(1024)} %refs_5_.3), custom_call_target="tpu_custom_call" | custom-call | flops 1 | bytes 1 | tf_op jit(solution)/shard_map/pallas_call | solution.py:184
  4.2 0.5 collective-permute-start
  4.8 0.0 copy-done
  4.8 0.3 shard_map.84
  5.0 1.2 %collective-permute-done.refs_1_ = bf16[512,512]{1,0:T(8,128)(2,1)S(1)} collective-permute-done((bf16[512,512]{1,0:T(8,128)(2,1)S(1)}, bf16[512,512]{1,0:T(8,128)(2,1)S(1)}, u32[]{:S(2)}, u32[]{:S(2)}) %collective-permute-start) | collective-permute-done | bytes 524320 | tf_op jit(solution)/shard_map/ppermute | solution.py:306
  6.3 0.1 shard_map.83.refs_6_
  6.4 2.9 %collective-permute-start.1 = (bf16[512,512]{1,0:T(8,128)(2,1)S(1)}, bf16[512,512]{1,0:T(8,128)(2,1)S(1)}, u32[]{:S(2)}, u32[]{:S(2)}) collective-permute-start(bf16[512,512]{1,0:T(8,128)(2,1)S(1)} %shard_map.83.refs_6_), channel_id=1, source_target_pairs={{0,2},{1,5},{2,0},{3,7},{4,6},{5,1},{6,4},{7,3},{8,10},{9,13},{10,... | collective-permute-start | bytes 1572872 | tf_op jit(solution)/shard_map/ppermute | solution.py:309
  9.3 4.2 %shard_map.85 = (bf16[512,512]{1,0:T(8,128)(2,1)S(1)}, bf16[512,512]{1,0:T(8,128)(2,1)S(1)}) custom-call(bf16[512,2048]{1,0:T(8,128)(2,1)} %refs_0_.5, s32[2048]{0:T(1024)} %refs_1_.3, f32[2048]{0:T(1024)} %refs_2_.3, s32[2048]{0:T(1024)} %refs_3_.3, f32[2048]{0:T(1024)} %refs_4_.3, f32[2048]{0:T(1024)} %refs_5_.3, bf16[512,512]{1,0:T(8,128)(2,1)S(1)} %shard_map.83.refs_6_, ...), custom_call_target="tpu_custom_call" | custom-call | flops 1 | bytes 1 | tf_op jit(solution)/shard_map/pallas_call | solution.py:184
  13.6 0.1 collective-permute-start.2
  13.6 2.6 %collective-permute-start.4 = (bf16[128,256]{1,0:T(8,128)(2,1)S(1)}, bf16[128,256]{1,0:T(8,128)(2,1)S(1)}, u32[]{:S(2)}, u32[]{:S(2)}) collective-permute-start(bf16[128,256]{1,0:T(8,128)(2,1)S(1)} %get-tuple-element.35), channel_id=1, source_target_pairs={{0,16},{1,9},{2,18},{3,11},{4,20},{5,13},{6,22},{7,15},{8,24},{9,1... | collective-permute-start | bytes 196616 | tf_op jit(solution)/shard_map/ppermute | solution.py:351
  16.3 1.6 %collective-permute-start.5 = (bf16[128,256]{1,0:T(8,128)(2,1)S(1)}, bf16[128,256]{1,0:T(8,128)(2,1)S(1)}, u32[]{:S(2)}, u32[]{:S(2)}) collective-permute-start(bf16[128,256]{1,0:T(8,128)(2,1)S(1)} %get-tuple-element.36), channel_id=1, source_target_pairs={{0,8},{1,17},{2,10},{3,19},{4,12},{5,21},{6,14},{7,23},{8,0},{9,25... | collective-permute-start | bytes 196616 | tf_op jit(solution)/shard_map/ppermute | solution.py:351
  17.9 0.2 collective-permute-start.6
  18.1 0.0 collective-permute-done.1.refs_1_
  18.1 0.1 shard_map.86.refs_0_
  18.2 0.0 collective-permute-done.2.refs_1_
  18.2 0.1 shard_map.87
  18.3 1.6 %collective-permute-start.3 = (bf16[512,256]{1,0:T(8,128)(2,1)S(1)}, bf16[512,256]{1,0:T(8,128)(2,1)S(1)}, u32[]{:S(2)}, u32[]{:S(2)}) collective-permute-start(bf16[512,256]{1,0:T(8,128)(2,1)S(1)} %get-tuple-element.33.refs_4_), channel_id=1, source_target_pairs={{0,4},{1,3},{2,6},{3,1},{4,0},{5,7},{6,2},{7,5},{8,12},{9,11},{10,... | collective-permute-start | bytes 786440 | tf_op jit(solution)/shard_map/ppermute | solution.py:309
  19.9 0.0 collective-permute-done.4.refs_1_
  19.9 0.7 %collective-permute-done.5.refs_2_ = bf16[128,256]{1,0:T(8,128)(2,1)S(1)} collective-permute-done((bf16[128,256]{1,0:T(8,128)(2,1)S(1)}, bf16[128,256]{1,0:T(8,128)(2,1)S(1)}, u32[]{:S(2)}, u32[]{:S(2)}) %collective-permute-start.5) | collective-permute-done | bytes 65568 | tf_op jit(solution)/shard_map/ppermute | solution.py:351
  20.6 3.4 %collective-permute-done.6.refs_3_ = bf16[128,256]{1,0:T(8,128)(2,1)S(1)} collective-permute-done((bf16[128,256]{1,0:T(8,128)(2,1)S(1)}, bf16[128,256]{1,0:T(8,128)(2,1)S(1)}, u32[]{:S(2)}, u32[]{:S(2)}) %collective-permute-start.6) | collective-permute-done | bytes 65568 | tf_op jit(solution)/shard_map/ppermute | solution.py:351
  24.0 0.1 collective-permute-start.7
  24.1 0.7 %collective-permute-done.3.refs_1_ = bf16[512,256]{1,0:T(8,128)(2,1)S(1)} collective-permute-done((bf16[512,256]{1,0:T(8,128)(2,1)S(1)}, bf16[512,256]{1,0:T(8,128)(2,1)S(1)}, u32[]{:S(2)}, u32[]{:S(2)}) %collective-permute-start.3) | collective-permute-done | bytes 262176 | tf_op jit(solution)/shard_map/ppermute | solution.py:309
  24.8 0.0 copy-start.1
  24.8 0.8 %collective-permute-done.7.refs_2_ = bf16[512,256]{1,0:T(8,128)(2,1)S(1)} collective-permute-done((bf16[512,256]{1,0:T(8,128)(2,1)S(1)}, bf16[512,256]{1,0:T(8,128)(2,1)S(1)}, u32[]{:S(2)}, u32[]{:S(2)}) %collective-permute-start.7) | collective-permute-done | bytes 262176 | tf_op jit(solution)/shard_map/ppermute | solution.py:306
  25.6 0.3 shard_map.90
  25.9 0.3 collective-permute-start.9
  26.2 3.2 %collective-permute-start.11 = (bf16[128,256]{1,0:T(8,128)(2,1)S(1)}, bf16[128,256]{1,0:T(8,128)(2,1)S(1)}, u32[]{:S(2)}, u32[]{:S(2)}) collective-permute-start(bf16[128,256]{1,0:T(8,128)(2,1)S(1)} %get-tuple-element.47.refs_0_), channel_id=1, source_target_pairs={{0,16},{1,9},{2,18},{3,11},{4,20},{5,13},{6,22},{7,15},{8,24},{9,1... | collective-permute-start | bytes 196616 | tf_op jit(solution)/shard_map/ppermute | solution.py:351
  29.4 0.8 %collective-permute-start.12 = (bf16[128,256]{1,0:T(8,128)(2,1)S(1)}, bf16[128,256]{1,0:T(8,128)(2,1)S(1)}, u32[]{:S(2)}, u32[]{:S(2)}) collective-permute-start(bf16[128,256]{1,0:T(8,128)(2,1)S(1)} %get-tuple-element.47.refs_0_), channel_id=1, source_target_pairs={{0,8},{1,17},{2,10},{3,19},{4,12},{5,21},{6,14},{7,23},{8,0},{9,25... | collective-permute-start | bytes 196616 | tf_op jit(solution)/shard_map/ppermute | solution.py:351
  30.2 0.7 %collective-permute-start.13 = (bf16[128,256]{1,0:T(8,128)(2,1)S(1)}, bf16[128,256]{1,0:T(8,128)(2,1)S(1)}, u32[]{:S(2)}, u32[]{:S(2)}) collective-permute-start(bf16[128,256]{1,0:T(8,128)(2,1)S(1)} %get-tuple-element.47.refs_0_), channel_id=1, source_target_pairs={{0,24},{1,25},{2,26},{3,27},{4,28},{5,29},{6,30},{7,31},{8,16},{9,... | collective-permute-start | bytes 196616 | tf_op jit(solution)/shard_map/ppermute | solution.py:351
  30.9 0.6 %collective-permute-start.8 = (bf16[256,256]{1,0:T(8,128)(2,1)S(1)}, bf16[256,256]{1,0:T(8,128)(2,1)S(1)}, u32[]{:S(2)}, u32[]{:S(2)}) collective-permute-start(bf16[256,256]{1,0:T(8,128)(2,1)S(1)} %get-tuple-element.41), channel_id=1, source_target_pairs={{0,8},{1,17},{2,10},{3,19},{4,12},{5,21},{6,14},{7,23},{8,0},{9,25... | collective-permute-start | bytes 393224 | tf_op jit(solution)/shard_map/ppermute | solution.py:317
  31.5 2.1 %collective-permute-done.9.refs_1_ = bf16[256,256]{1,0:T(8,128)(2,1)S(1)} collective-permute-done((bf16[256,256]{1,0:T(8,128)(2,1)S(1)}, bf16[256,256]{1,0:T(8,128)(2,1)S(1)}, u32[]{:S(2)}, u32[]{:S(2)}) %collective-permute-start.9) | collective-permute-done | bytes 131104 | tf_op jit(solution)/shard_map/ppermute | solution.py:317
  33.7 1.0 %collective-permute-start.15 = (bf16[256,256]{1,0:T(8,128)(2,1)S(1)}, bf16[256,256]{1,0:T(8,128)(2,1)S(1)}, u32[]{:S(2)}, u32[]{:S(2)}) collective-permute-start(bf16[256,256]{1,0:T(8,128)(2,1)S(1)} %get-tuple-element.44.refs_2_), channel_id=1, source_target_pairs={{0,16},{1,9},{2,18},{3,11},{4,20},{5,13},{6,22},{7,15},{8,24},{9,1... | collective-permute-start | bytes 393224 | tf_op jit(solution)/shard_map/ppermute | solution.py:317
  34.7 0.0 collective-permute-done.11.refs_1_
  34.7 0.8 %collective-permute-done.12.refs_2_ = bf16[128,256]{1,0:T(8,128)(2,1)S(1)} collective-permute-done((bf16[128,256]{1,0:T(8,128)(2,1)S(1)}, bf16[128,256]{1,0:T(8,128)(2,1)S(1)}, u32[]{:S(2)}, u32[]{:S(2)}) %collective-permute-start.12) | collective-permute-done | bytes 65568 | tf_op jit(solution)/shard_map/ppermute | solution.py:351
  35.6 1.8 %collective-permute-done.13.refs_3_ = bf16[128,256]{1,0:T(8,128)(2,1)S(1)} collective-permute-done((bf16[128,256]{1,0:T(8,128)(2,1)S(1)}, bf16[128,256]{1,0:T(8,128)(2,1)S(1)}, u32[]{:S(2)}, u32[]{:S(2)}) %collective-permute-start.13) | collective-permute-done | bytes 65568 | tf_op jit(solution)/shard_map/ppermute | solution.py:351
  37.4 0.7 %collective-permute-start.14 = (bf16[128,256]{1,0:T(8,128)(2,1)S(1)}, bf16[128,256]{1,0:T(8,128)(2,1)S(1)}, u32[]{:S(2)}, u32[]{:S(2)}) collective-permute-start(bf16[128,256]{1,0:T(8,128)(2,1)S(1)} %shard_map.93.refs_4_), channel_id=1, source_target_pairs={{0,1},{1,0},{2,3},{3,2},{4,5},{5,4},{6,7},{7,6},{8,9},{9,8},{10,11... | collective-permute-start | bytes 196616 | tf_op jit(solution)/shard_map/ppermute | solution.py:306
  38.0 2.4 %collective-permute-done.8.refs_1_ = bf16[256,256]{1,0:T(8,128)(2,1)S(1)} collective-permute-done((bf16[256,256]{1,0:T(8,128)(2,1)S(1)}, bf16[256,256]{1,0:T(8,128)(2,1)S(1)}, u32[]{:S(2)}, u32[]{:S(2)}) %collective-permute-start.8) | collective-permute-done | bytes 131104 | tf_op jit(solution)/shard_map/ppermute | solution.py:317
  40.5 0.3 collective-permute-start.10
  40.8 2.1 %collective-permute-done.15.refs_1_ = bf16[256,256]{1,0:T(8,128)(2,1)S(1)} collective-permute-done((bf16[256,256]{1,0:T(8,128)(2,1)S(1)}, bf16[256,256]{1,0:T(8,128)(2,1)S(1)}, u32[]{:S(2)}, u32[]{:S(2)}) %collective-permute-start.15) | collective-permute-done | bytes 131104 | tf_op jit(solution)/shard_map/ppermute | solution.py:317
  42.9 0.1 collective-permute-start.16
  43.0 0.0 copy-done.1
  43.1 0.0 collective-permute-done.14.refs_5_
  43.1 2.1 %shard_map.94.refs_2_ = bf16[512,512]{1,0:T(8,128)(2,1)S(1)} custom-call(bf16[512,256]{1,0:T(8,128)(2,1)S(1)} %get-tuple-element.52.refs_0_, bf16[512,256]{1,0:T(8,128)(2,1)S(1)} %get-tuple-element.51.refs_1_, f32[256,256]{1,0:T(8,128)S(1)} %get-tuple-element.50.refs_2_, f32[256,256]{1,0:T(8,128)S(1)} %get-tuple-element.49.refs_3_, ...), custom_call_target="tpu_custom_call" | custom-call | flops 1 | bytes 1 | tf_op jit(solution)/shard_map/pallas_call | solution.py:79
  45.2 1.9 %collective-permute-done.10.refs_1_ = bf16[256,256]{1,0:T(8,128)(2,1)S(1)} collective-permute-done((bf16[256,256]{1,0:T(8,128)(2,1)S(1)}, bf16[256,256]{1,0:T(8,128)(2,1)S(1)}, u32[]{:S(2)}, u32[]{:S(2)}) %collective-permute-start.10) | collective-permute-done | bytes 131104 | tf_op jit(solution)/shard_map/ppermute | solution.py:317
  47.2 0.2 shard_map.96.refs_0_
  47.4 3.9 %collective-permute-done.16.refs_2_ = bf16[256,256]{1,0:T(8,128)(2,1)S(1)} collective-permute-done((bf16[256,256]{1,0:T(8,128)(2,1)S(1)}, bf16[256,256]{1,0:T(8,128)(2,1)S(1)}, u32[]{:S(2)}, u32[]{:S(2)}) %collective-permute-start.16) | collective-permute-done | bytes 131104 | tf_op jit(solution)/shard_map/ppermute | solution.py:317
  51.3 1.0 %shard_map.97 = bf16[512,256]{1,0:T(8,128)(2,1)} custom-call(f32[512,256]{1,0:T(8,128)S(1)} %shard_map.96.refs_0_, bf16[512,256]{1,0:T(8,128)(2,1)S(1)} %slice.20.refs_1_, bf16[256,256]{1,0:T(8,128)(2,1)S(1)} %collective-permute-done.16.refs_2_), custom_call_target="tpu_custom_call" | custom-call | flops 1 | bytes 1 | tf_op jit(solution)/shard_map/pallas_call | solution.py:273
  (9 shorter events, 0.3 us)
Async XLA Ops:
  0.0 4.8 %copy-start = (bf16[2,512,256]{2,1,0:T(8,128)(2,1)S(1)}, bf16[2,512,256]{2,1,0:T(8,128)(2,1)}, u32[]{:S(2)}) copy-start(bf16[2,512,256]{2,1,0:T(8,128)(2,1)} %refs_0_.4) | copy-start | bytes 1572868
  4.2 2.1 %collective-permute-start = (bf16[512,512]{1,0:T(8,128)(2,1)S(1)}, bf16[512,512]{1,0:T(8,128)(2,1)S(1)}, u32[]{:S(2)}, u32[]{:S(2)}) collective-permute-start(bf16[512,512]{1,0:T(8,128)(2,1)S(1)} %get-tuple-element.28), channel_id=1, source_target_pairs={{0,1},{1,0},{2,3},{3,2},{4,5},{5,4},{6,7},{7,6},{8,9},{9,8},{10,11... | collective-permute-start | bytes 1572872 | tf_op jit(solution)/shard_map/ppermute | solution.py:306
  6.4 11.7 %collective-permute-start.1 = (bf16[512,512]{1,0:T(8,128)(2,1)S(1)}, bf16[512,512]{1,0:T(8,128)(2,1)S(1)}, u32[]{:S(2)}, u32[]{:S(2)}) collective-permute-start(bf16[512,512]{1,0:T(8,128)(2,1)S(1)} %shard_map.83.refs_6_), channel_id=1, source_target_pairs={{0,2},{1,5},{2,0},{3,7},{4,6},{5,1},{6,4},{7,3},{8,10},{9,13},{10,... | collective-permute-start | bytes 1572872 | tf_op jit(solution)/shard_map/ppermute | solution.py:309
  13.6 4.6 %collective-permute-start.2 = (bf16[512,512]{1,0:T(8,128)(2,1)S(1)}, bf16[512,512]{1,0:T(8,128)(2,1)S(1)}, u32[]{:S(2)}, u32[]{:S(2)}) collective-permute-start(bf16[512,512]{1,0:T(8,128)(2,1)S(1)} %get-tuple-element.31), channel_id=1, source_target_pairs={{0,1},{1,0},{2,3},{3,2},{4,5},{5,4},{6,7},{7,6},{8,9},{9,8},{10,11... | collective-permute-start | bytes 1572872 | tf_op jit(solution)/shard_map/ppermute | solution.py:306
  13.6 6.3 %collective-permute-start.4 = (bf16[128,256]{1,0:T(8,128)(2,1)S(1)}, bf16[128,256]{1,0:T(8,128)(2,1)S(1)}, u32[]{:S(2)}, u32[]{:S(2)}) collective-permute-start(bf16[128,256]{1,0:T(8,128)(2,1)S(1)} %get-tuple-element.35), channel_id=1, source_target_pairs={{0,16},{1,9},{2,18},{3,11},{4,20},{5,13},{6,22},{7,15},{8,24},{9,1... | collective-permute-start | bytes 196616 | tf_op jit(solution)/shard_map/ppermute | solution.py:351
  16.3 4.3 %collective-permute-start.5 = (bf16[128,256]{1,0:T(8,128)(2,1)S(1)}, bf16[128,256]{1,0:T(8,128)(2,1)S(1)}, u32[]{:S(2)}, u32[]{:S(2)}) collective-permute-start(bf16[128,256]{1,0:T(8,128)(2,1)S(1)} %get-tuple-element.36), channel_id=1, source_target_pairs={{0,8},{1,17},{2,10},{3,19},{4,12},{5,21},{6,14},{7,23},{8,0},{9,25... | collective-permute-start | bytes 196616 | tf_op jit(solution)/shard_map/ppermute | solution.py:351
  17.9 6.1 %collective-permute-start.6 = (bf16[128,256]{1,0:T(8,128)(2,1)S(1)}, bf16[128,256]{1,0:T(8,128)(2,1)S(1)}, u32[]{:S(2)}, u32[]{:S(2)}) collective-permute-start(bf16[128,256]{1,0:T(8,128)(2,1)S(1)} %get-tuple-element.37), channel_id=1, source_target_pairs={{0,24},{1,25},{2,26},{3,27},{4,28},{5,29},{6,30},{7,31},{8,16},{9,... | collective-permute-start | bytes 196616 | tf_op jit(solution)/shard_map/ppermute | solution.py:351
  18.3 6.4 %collective-permute-start.3 = (bf16[512,256]{1,0:T(8,128)(2,1)S(1)}, bf16[512,256]{1,0:T(8,128)(2,1)S(1)}, u32[]{:S(2)}, u32[]{:S(2)}) collective-permute-start(bf16[512,256]{1,0:T(8,128)(2,1)S(1)} %get-tuple-element.33.refs_4_), channel_id=1, source_target_pairs={{0,4},{1,3},{2,6},{3,1},{4,0},{5,7},{6,2},{7,5},{8,12},{9,11},{10,... | collective-permute-start | bytes 786440 | tf_op jit(solution)/shard_map/ppermute | solution.py:309
  24.0 1.6 %collective-permute-start.7 = (bf16[512,256]{1,0:T(8,128)(2,1)S(1)}, bf16[512,256]{1,0:T(8,128)(2,1)S(1)}, u32[]{:S(2)}, u32[]{:S(2)}) collective-permute-start(bf16[512,256]{1,0:T(8,128)(2,1)S(1)} %get-tuple-element.39), channel_id=1, source_target_pairs={{0,1},{1,0},{2,3},{3,2},{4,5},{5,4},{6,7},{7,6},{8,9},{9,8},{10,11... | collective-permute-start | bytes 786440 | tf_op jit(solution)/shard_map/ppermute | solution.py:306
  24.8 18.2 %copy-start.1 = (f32[2,256,256]{2,1,0:T(8,128)S(1)}, f32[2,256,256]{2,1,0:T(8,128)}, u32[]{:S(2)}) copy-start(f32[2,256,256]{2,1,0:T(8,128)} %param.15) | copy-start | bytes 1572868
  25.9 7.7 %collective-permute-start.9 = (bf16[256,256]{1,0:T(8,128)(2,1)S(1)}, bf16[256,256]{1,0:T(8,128)(2,1)S(1)}, u32[]{:S(2)}, u32[]{:S(2)}) collective-permute-start(bf16[256,256]{1,0:T(8,128)(2,1)S(1)} %get-tuple-element.43.refs_6_), channel_id=1, source_target_pairs={{0,8},{1,17},{2,10},{3,19},{4,12},{5,21},{6,14},{7,23},{8,0},{9,25... | collective-permute-start | bytes 393224 | tf_op jit(solution)/shard_map/ppermute | solution.py:317
  26.2 8.5 %collective-permute-start.11 = (bf16[128,256]{1,0:T(8,128)(2,1)S(1)}, bf16[128,256]{1,0:T(8,128)(2,1)S(1)}, u32[]{:S(2)}, u32[]{:S(2)}) collective-permute-start(bf16[128,256]{1,0:T(8,128)(2,1)S(1)} %get-tuple-element.47.refs_0_), channel_id=1, source_target_pairs={{0,16},{1,9},{2,18},{3,11},{4,20},{5,13},{6,22},{7,15},{8,24},{9,1... | collective-permute-start | bytes 196616 | tf_op jit(solution)/shard_map/ppermute | solution.py:351
  29.4 6.1 %collective-permute-start.12 = (bf16[128,256]{1,0:T(8,128)(2,1)S(1)}, bf16[128,256]{1,0:T(8,128)(2,1)S(1)}, u32[]{:S(2)}, u32[]{:S(2)}) collective-permute-start(bf16[128,256]{1,0:T(8,128)(2,1)S(1)} %get-tuple-element.47.refs_0_), channel_id=1, source_target_pairs={{0,8},{1,17},{2,10},{3,19},{4,12},{5,21},{6,14},{7,23},{8,0},{9,25... | collective-permute-start | bytes 196616 | tf_op jit(solution)/shard_map/ppermute | solution.py:351
  30.2 7.1 %collective-permute-start.13 = (bf16[128,256]{1,0:T(8,128)(2,1)S(1)}, bf16[128,256]{1,0:T(8,128)(2,1)S(1)}, u32[]{:S(2)}, u32[]{:S(2)}) collective-permute-start(bf16[128,256]{1,0:T(8,128)(2,1)S(1)} %get-tuple-element.47.refs_0_), channel_id=1, source_target_pairs={{0,24},{1,25},{2,26},{3,27},{4,28},{5,29},{6,30},{7,31},{8,16},{9,... | collective-permute-start | bytes 196616 | tf_op jit(solution)/shard_map/ppermute | solution.py:351
  30.9 9.6 %collective-permute-start.8 = (bf16[256,256]{1,0:T(8,128)(2,1)S(1)}, bf16[256,256]{1,0:T(8,128)(2,1)S(1)}, u32[]{:S(2)}, u32[]{:S(2)}) collective-permute-start(bf16[256,256]{1,0:T(8,128)(2,1)S(1)} %get-tuple-element.41), channel_id=1, source_target_pairs={{0,8},{1,17},{2,10},{3,19},{4,12},{5,21},{6,14},{7,23},{8,0},{9,25... | collective-permute-start | bytes 393224 | tf_op jit(solution)/shard_map/ppermute | solution.py:317
  33.7 9.2 %collective-permute-start.15 = (bf16[256,256]{1,0:T(8,128)(2,1)S(1)}, bf16[256,256]{1,0:T(8,128)(2,1)S(1)}, u32[]{:S(2)}, u32[]{:S(2)}) collective-permute-start(bf16[256,256]{1,0:T(8,128)(2,1)S(1)} %get-tuple-element.44.refs_2_), channel_id=1, source_target_pairs={{0,16},{1,9},{2,18},{3,11},{4,20},{5,13},{6,22},{7,15},{8,24},{9,1... | collective-permute-start | bytes 393224 | tf_op jit(solution)/shard_map/ppermute | solution.py:317
  37.4 5.7 %collective-permute-start.14 = (bf16[128,256]{1,0:T(8,128)(2,1)S(1)}, bf16[128,256]{1,0:T(8,128)(2,1)S(1)}, u32[]{:S(2)}, u32[]{:S(2)}) collective-permute-start(bf16[128,256]{1,0:T(8,128)(2,1)S(1)} %shard_map.93.refs_4_), channel_id=1, source_target_pairs={{0,1},{1,0},{2,3},{3,2},{4,5},{5,4},{6,7},{7,6},{8,9},{9,8},{10,11... | collective-permute-start | bytes 196616 | tf_op jit(solution)/shard_map/ppermute | solution.py:306
  40.5 6.7 %collective-permute-start.10 = (bf16[256,256]{1,0:T(8,128)(2,1)S(1)}, bf16[256,256]{1,0:T(8,128)(2,1)S(1)}, u32[]{:S(2)}, u32[]{:S(2)}) collective-permute-start(bf16[256,256]{1,0:T(8,128)(2,1)S(1)} %get-tuple-element.46), channel_id=1, source_target_pairs={{0,16},{1,9},{2,18},{3,11},{4,20},{5,13},{6,22},{7,15},{8,24},{9,1... | collective-permute-start | bytes 393224 | tf_op jit(solution)/shard_map/ppermute | solution.py:317
  42.9 8.4 %collective-permute-start.16 = (bf16[256,256]{1,0:T(8,128)(2,1)S(1)}, bf16[256,256]{1,0:T(8,128)(2,1)S(1)}, u32[]{:S(2)}, u32[]{:S(2)}) collective-permute-start(bf16[256,256]{1,0:T(8,128)(2,1)S(1)} %shard_map.95.refs_3_.refs_4_), channel_id=1, source_target_pairs={{0,8},{1,17},{2,10},{3,19},{4,12},{5,21},{6,14},{7,23},{8,0},{9,25... | collective-permute-start | bytes 393224 | tf_op jit(solution)/shard_map/ppermute | solution.py:317

commit v3 on v0

v3 whole, which is shorter than its diff:
```python
import functools

import jax
import jax.numpy as jnp
from jax import lax
from jax.experimental import pallas as pl
from jax.experimental.pallas import tpu as pltpu
from jax.sharding import PartitionSpec as P

BF = jnp.bfloat16
F32 = jnp.float32
HIGHEST = lax.Precision.HIGHEST
MIB = 2**20


def bit_orders(size, first):
    bits = list(range(first, size.bit_length() - 1))
    half = len(bits) // 2
    return bits, bits[half:] + bits[:half]


def target_codes(bits):
    if not bits:
        return [0]
    rest = target_codes(bits[1:])
    return rest + [(1 << bits[0]) | code for code in rest]


def source_codes(bits):
    codes = [0]
    for bit in bits:
        codes = codes + [(1 << bit) | code for code in codes]
    return codes


def is_even():
    return lax.rem(lax.axis_index("col"), 2) == 0


def select_code(even, pair):
    return pair[0] if pair[0] == pair[1] else jnp.where(even, pair[0], pair[1])


def row_bit(order, stage):
    return jnp.bitwise_and(lax.shift_right_logical(lax.axis_index("row"), order[stage]), 1) == 0


def swap_groups(value, axis, order):
    size = value.shape[axis]
    for stage in range(len(order) - 1):
        step = size >> (stage + 1)
        pieces = [lax.slice_in_dim(value, i, i + step, axis=axis) for i in range(0, size, step)]
        flipped = jnp.concatenate([pieces[i ^ 1] for i in range(len(pieces))], axis)
        value = jnp.where(row_bit(order, stage), value, flipped)
    return value


def local(fn, outs, values, after=()):
    outs = [jax.ShapeDtypeStruct(shape, dtype) for shape, dtype in outs]
    if any(v.shape[-1] % 128 or v.shape[-2] % 16 for v in list(values) + outs):
        return list(fn(*values))

    def kernel(*refs):
        ins = refs[:len(values)]
        results = fn(*[ref[...] for ref in ins])
        for ref, result in zip(refs[len(values) + len(after):], results):
            ref[...] = result

    return list(
        pl.pallas_call(
            kernel,
            in_specs=[pl.BlockSpec(memory_space=pltpu.VMEM)] * len(values)
            + [pl.BlockSpec(memory_space=pl.ANY)] * len(after),
            out_specs=[pl.BlockSpec(memory_space=pltpu.VMEM)] * len(outs),
            out_shape=[pltpu.VMEM(o.shape, o.dtype) for o in outs],
            compiler_params=pltpu.CompilerParams(vmem_limit_bytes=16 * MIB),
            cost_estimate=pl.CostEstimate(flops=1, bytes_accessed=1, transcendentals=0),
        )(*[pltpu.with_memory_space_constraint(v, pltpu.VMEM) for v in values], *after)
    )


def product_kernel(plan, width, depth, chunks, n_after, *refs):
    eig, pole_values, weights, roots, scale = refs[:5]
    outs = refs[5 + n_after:]
    rows, poles = eig.shape
    me = lax.axis_index("col")
    even = is_even()
    piece = width // chunks
    pole_values = pole_values[...]
    weights = weights[...]
    for entry, codes in enumerate(plan):
        for place, pair in enumerate(codes):
            at = pl.ds(pl.multiple_of(jnp.bitwise_xor(me, select_code(even, pair)) * width, width), width)
            near = roots[:, at]
            near = jnp.concatenate(
                [jnp.broadcast_to(near[:, j:j + 128], (128, 128)).T for j in range(0, width, 128)], 0
            )
            total = None
            for k in range(0, poles, depth):
                gaps = pole_values[:, k:k + depth] - jnp.concatenate([near] * (depth // 128), 1)
                matrix = (weights[:, k:k + depth] / gaps).astype(BF)
                term = lax.dot_general(
                    eig[:, k:k + depth], matrix, (((1,), (1,)), ((), ())), preferred_element_type=F32
                )
                total = term if total is None else total + term
            total = (total * scale[:, at]).astype(BF)
            for chunk in range(chunks):
                outs[entry * chunks + chunk][:, place * piece:(place + 1) * piece] = total[
                    :, chunk * piece:(chunk + 1) * piece
                ]


def plain_products(plan, row_codes, parts, chunks, operands):
    eigvecs, pole_order, pole_weight, root_gap, root_shift, column_weight = operands
    poles = eigvecs.shape[1]
    me = lax.axis_index("col")
    places = jnp.bitwise_xor(lax.axis_index("row"), jnp.array(row_codes, jnp.int32))
    ordered = eigvecs.reshape(len(row_codes), -1, poles)[places].reshape(eigvecs.shape)
    results = []
    for codes in plan:
        places = jnp.array([[a, b] for a, b in codes], jnp.int32)
        places = jnp.bitwise_xor(me, jnp.where(is_even(), places[:, 0], places[:, 1]))
        pick = lambda v: v.reshape(parts, chunks, -1)[places].transpose(1, 0, 2).reshape(-1)
        root_values = 2.0 * pick(root_gap).astype(F32) + 1.0 + pick(root_shift)
        numer = pole_weight[:, None] * pick(column_weight)[None, :]
        gaps = 2.0 * pole_order.astype(F32)[:, None] - root_values[None, :]
        result = jnp.dot(ordered, (numer / gaps).astype(BF), preferred_element_type=F32).astype(BF)
        results += jnp.split(result, chunks, 1)
    return results


def products(plan, *, row_codes, parts, chunks, operands, state, after=()):
    rows, poles = operands[0].shape
    width = operands[3].shape[0] // parts
    if state is None:
        return plain_products(plan, row_codes, parts, chunks, operands)
    outs = [pltpu.VMEM((rows, width // chunks * len(codes)), BF) for codes in plan for _ in range(chunks)]
    return pl.pallas_call(
        functools.partial(
            product_kernel, plan, width, poles // 2, chunks, len(after)
        ),
        in_specs=[pl.BlockSpec(memory_space=pltpu.VMEM)] * 5 + [pl.BlockSpec(memory_space=pl.ANY)] * len(after),
        out_specs=[pl.BlockSpec(memory_space=pltpu.VMEM)] * len(outs),
        out_shape=outs,
        compiler_params=pltpu.CompilerParams(vmem_limit_bytes=16 * MIB),
        cost_estimate=pl.CostEstimate(flops=1, bytes_accessed=1, transcendentals=0),
    )(*[pltpu.with_memory_space_constraint(operand, pltpu.VMEM) for operand in state], *after)


def panel_kernel(row_codes, row_orders, blocks, *refs):
    eig_hbm, panel_hbm, order_hbm, weight_hbm, gap_hbm, shift_hbm, scale_hbm = refs[:7]
    vectors_out, kept_out, message, correlation_out, eig, pole_values, weights, roots, scales = refs[7:16]
    panel, correlation, order, weight, gap, shift, scale, sem, eig_sem = refs[16:]
    even = is_even()
    row = lax.axis_index("row")
    block = panel.shape[1] // blocks
    targets = list(zip(*[target_codes(order) for order in row_orders]))
    at = lambda code: pl.ds(pl.multiple_of(jnp.bitwise_xor(row, code) * block, block), block)
    copies = [
        pltpu.make_async_copy(src, dst, sem.at[i])
        for i, (src, dst) in enumerate(
            [
                (panel_hbm, panel),
                (order_hbm, order),
                (weight_hbm, weight),
                (gap_hbm, gap),
                (shift_hbm, shift),
                (scale_hbm, scale),
            ]
        )
    ]
    for place, code in enumerate(row_codes):
        copies.append(
            pltpu.make_async_copy(
                eig_hbm.at[at(code)], eig.at[place * block:(place + 1) * block], eig_sem.at[place]
            )
        )
    for copy in copies:
        copy.start()
    for copy in copies[1:6]:
        copy.wait()
    pole_values[...] = (2.0 * order[...].astype(F32)).reshape(pole_values.shape)
    weights[...] = weight[...].reshape(weights.shape)
    roots[...] = (2.0 * gap[...].astype(F32) + 1.0 + shift[...]).reshape(roots.shape)
    scales[...] = scale[...].reshape(scales.shape)
    copies[0].wait()
    for code in range(blocks):
        vectors_out[0, code * block:(code + 1) * block] = panel[0, at(code)]
        vectors_out[1, code * block:(code + 1) * block] = panel[1, at(code)]
    core = jnp.where(even, 0, 1)
    correlation[...] = lax.dot_general(panel[1], panel[0], (((0,), (0,)), ((), ())), preferred_element_type=F32)
    near = correlation_out.shape[0]
    place = lax.shift_right_logical(lax.axis_index("col"), 1)
    part = correlation[pl.ds(pl.multiple_of(place * near, near), near)]
    correlation_out[...] = part
    message[:near] = part.astype(BF)
    for place, pair in enumerate(targets):
        value = panel[core, at(select_code(even, pair))]
        if place < blocks // 2:
            kept_out[place * block:(place + 1) * block] = value
        else:
            start = near + (place - blocks // 2) * block
            message[start:start + block] = value
    for copy in copies[6:]:
        copy.wait()


def panel_blocks(row_codes, row_orders, parts, panel_vectors, operands):
    panels, rows, width = panel_vectors.shape
    blocks = 1 << len(row_orders[0])
    near = width // parts
    poles, roots = operands[1].shape[0], operands[3].shape[0]
    eig_rows = operands[0].shape[0]
    outs = [
        pltpu.VMEM((panels, rows, width), BF),
        pltpu.VMEM((rows // 2, width), BF),
        pltpu.VMEM((near + rows // 2, width), BF),
        pltpu.VMEM((near, width), F32),
        pltpu.VMEM((eig_rows, poles), BF),
        pltpu.VMEM((1, poles), F32),
        pltpu.VMEM((1, poles), F32),
        pltpu.VMEM((1, roots), F32),
        pltpu.VMEM((1, roots), F32),
    ]
    results = pl.pallas_call(
        functools.partial(panel_kernel, row_codes, row_orders, blocks),
        in_specs=[pl.BlockSpec(memory_space=pl.ANY)] * 7,
        out_specs=[pl.BlockSpec(memory_space=pltpu.VMEM)] * len(outs),
        out_shape=outs,
        scratch_shapes=[
            pltpu.VMEM((panels, rows, width), BF),
            pltpu.VMEM((width, width), F32),
            pltpu.VMEM((poles,), jnp.int32),
            pltpu.VMEM((poles,), F32),
            pltpu.VMEM((roots,), jnp.int32),
            pltpu.VMEM((roots,), F32),
            pltpu.VMEM((roots,), F32),
            pltpu.SemaphoreType.DMA((6,)),
            pltpu.SemaphoreType.DMA((blocks,)),
        ],
        compiler_params=pltpu.CompilerParams(vmem_limit_bytes=16 * MIB),
        cost_estimate=pl.CostEstimate(flops=1, bytes_accessed=1, transcendentals=0),
    )(*[pltpu.with_memory_space_constraint(v, pltpu.HBM) for v in (operands[0], panel_vectors, *operands[1:])])
    return results[:4], results[4:]


def finish_kernel(blocks, start, total, update, project, out_hbm, result, sem):
    block = total.shape[0] // blocks
    row = lax.axis_index("row")
    value = total[...] - jnp.dot(update[:, start:], project[...], preferred_element_type=F32)
    result[...] = value.astype(BF)
    copies = []
    for code in range(blocks):
        at = pl.multiple_of(jnp.bitwise_xor(row, code) * block, block)
        copies.append(
            pltpu.make_async_copy(
                result.at[code * block:(code + 1) * block], out_hbm.at[pl.ds(at, block)], sem.at[code]
            )
        )
        copies[-1].start()
    for copy in copies:
        copy.wait()


def finish(blocks, total, update, project, start):
    rows, width = total.shape
    if width % 128:
        result = (total - jnp.dot(update[:, start:], project, preferred_element_type=F32)).astype(BF)
        places = jnp.bitwise_xor(lax.axis_index("row"), jnp.arange(blocks))
        return result.reshape(blocks, -1, width)[places].reshape(rows, width)
    return pl.pallas_call(
        functools.partial(finish_kernel, blocks, start),
        in_specs=[pl.BlockSpec(memory_space=pltpu.VMEM)] * 3,
        out_specs=pl.BlockSpec(memory_space=pl.ANY),
        out_shape=jax.ShapeDtypeStruct((rows, width), BF),
        scratch_shapes=[pltpu.VMEM((rows, width), BF), pltpu.SemaphoreType.DMA((blocks,))],
        compiler_params=pltpu.CompilerParams(vmem_limit_bytes=16 * MIB),
        cost_estimate=pl.CostEstimate(flops=1, bytes_accessed=1, transcendentals=0),
    )(*[pltpu.with_memory_space_constraint(v, pltpu.VMEM) for v in (total, update, project)])


def split_dot(left, right):
    def parts(value):
        if value.dtype == BF:
            return [value]
        high = value.astype(BF)
        return [high, (value - high.astype(F32)).astype(BF)]

    total = None
    for i, a in enumerate(parts(left)):
        for j, b in enumerate(parts(right)):
            if i + j < 2:
                term = jnp.dot(a, b, preferred_element_type=F32)
                total = term if total is None else total + term
    return total


def shards(
    n_row,
    n_col,
    eigvecs,
    pole_order,
    pole_weight,
    root_gap,
    root_shift,
    column_weight,
    panel_vectors,
    panel_factors,
):
    col_orders = bit_orders(n_col, 1)
    row_orders = bit_orders(n_row, 0)
    col_stages = len(col_orders[0])
    row_stages = len(row_orders[0])
    rows = eigvecs.shape[0]
    block = rows // n_row
    panel_width = panel_vectors.shape[2]
    parts = n_col // 2
    near = panel_width // parts
    width = root_gap.shape[0] // n_col
    chunks = 2 if width % 256 == 0 else 1
    piece = width // chunks
    sum_order = row_orders[0]
    move_order = sum_order[::-1]

    def swap_cores(value):
        return lax.ppermute(value, "col", [(i, i ^ 1) for i in range(n_col)])

    def swap_col(value, stage):
        return lax.ppermute(value, "col", [(i, i ^ (1 << col_orders[i % 2][stage])) for i in range(n_col)])

    def swap_row(value, bits):
        pairs = [(r * n_col + c, (r ^ (1 << bits[c % 2])) * n_col + c) for r in range(n_row) for c in range(n_col)]
        return lax.ppermute(value, ("row", "col"), pairs)

    def split_targets(value, targets):
        step = targets * block
        kept = [value[i:i + step // 2] for i in range(0, value.shape[0], step)]
        sent = [value[i + step // 2:i + step] for i in range(0, value.shape[0], step)]
        return jnp.concatenate(kept, 0), jnp.concatenate(sent, 0)

    def pick_blocks(value, places):
        return jnp.concatenate([value[i * block:(i + 1) * block] for i in places], 0)

    targets = target_codes(move_order)
    own_codes = list(zip(*[target_codes(order) for order in col_orders]))
    other_codes = [(1 ^ odd, 1 ^ even) for even, odd in own_codes]
    half = len(own_codes) // 2
    operands = (eigvecs, pole_order, pole_weight, root_gap, root_shift, column_weight)
    (vectors, kept, message, correlation), state = panel_blocks(
        targets, row_orders, parts, panel_vectors, operands
    )
    if width % (128 * chunks) or eigvecs.shape[1] % 256:
        state = None
    multiply = functools.partial(
        products, row_codes=targets, parts=n_col, chunks=chunks, operands=operands, state=state
    )
    first = multiply([other_codes[half:], own_codes[half:]])
    other_sent, own_sent = first[:chunks], first[chunks:]
    got_sent = [swap_cores(value) for value in other_sent]
    other_kept = multiply([other_codes[:half]])
    got_kept = [swap_cores(value) for value in other_kept]
    long = half * piece
    sent = []
    for own, got in zip(own_sent, got_sent):
        (value,) = local(
            lambda own, got: [(own.astype(F32) + got.astype(F32)).astype(BF)],
            [((rows, long), BF)],
            [own, got],
            after=(other_kept[0], *sent),
        )
        sent.append(value)
    got = [swap_col(message, 0) for message in sent]
    own_kept = multiply([own_codes[:half]], after=(sent[0],))

    current = [[own, other, new] for own, other, new in zip(own_kept, got_kept, got)]
    for stage in range(1, col_stages):
        long //= 2

        def next_sums(*values, long=long):
            count = len(values) // chunks
            totals = [sum(v.astype(F32) for v in values[i:i + count]) for i in range(0, len(values), count)]
            out = jnp.concatenate([total[:, long:] for total in totals], 1).astype(BF)
            return *[total[:, :long] for total in totals], out

        *totals, col_message = local(
            next_sums,
            [((rows, long), F32)] * chunks + [((rows, chunks * long), BF)],
            sum(current, []),
        )
        if stage == 1:
            first_message = col_message
        got = swap_col(col_message, stage)
        current = [[total, got] for total in totals]
        if stage < col_stages - 1:
            current = [[total, got[:, i * long:(i + 1) * long]] for i, total in enumerate(totals)]

    for stage in range(row_stages):
        panel_got = swap_row(message, [order[stage] for order in row_orders])

        if stage < row_stages - 1:

            def next_panel(kept, correlation, got, targets=n_row >> (stage + 1)):
                correlation = correlation + got[:near].astype(F32)
                kept, moved = split_targets(jnp.concatenate([kept, got[near:]], 0), targets)
                return kept, jnp.concatenate([correlation.astype(BF), moved], 0), correlation

            kept, message, correlation = local(
                next_panel,
                [((rows // 2, panel_width), BF), ((near + rows // 2, panel_width), BF), ((near, panel_width), F32)],
                [kept, correlation, panel_got],
                after=(other_kept[0],),
            )
    panel_places = [[source_codes(order).index(code) for code in range(n_row)] for order in row_orders]

    first_rows = 3 * rows // 4

    def panel_done(kept, correlation, got):
        correlation = (correlation + got[:near].astype(F32)).astype(BF)
        value = jnp.concatenate([kept, got[near:]], 0)
        orders = [pick_blocks(value, places).astype(F32) for places in panel_places]
        value = jnp.where(is_even(), orders[0], orders[1]).astype(BF)
        return value, correlation, value[:first_rows], value[first_rows:]

    mine, correlation, *mine_sent = local(
        panel_done,
        [((r, panel_width), BF) for r in (rows, near, first_rows, rows - first_rows)],
        [kept, correlation, panel_got],
        after=(first_message,),
    )
    other = [swap_cores(value) for value in mine_sent]

    wide = 2 * panel_width
    summed = wide // 2 if row_stages > 1 else wide

    def projections(mine, *values):
        other, values = values[:2], values[2:]
        merged = jnp.concatenate(values[:chunks], 1) + jnp.concatenate(values[chunks:], 1).astype(F32)
        merged = merged.astype(BF)
        dims = (((0,), (0,)), ((), ()))
        project = jnp.concatenate(
            [
                lax.dot_general(pick_blocks(v, targets), merged, dims, preferred_element_type=F32)
                for v in (mine, jnp.concatenate(other, 0))
            ],
            0,
        )
        project = swap_groups(project, 0, sum_order)
        out = project if row_stages == 1 else project[summed:]
        return project[:summed], out.astype(BF), *split_targets(merged, n_row)

    shapes = lambda size: [((size, width), F32), ((size, width), BF)]
    halves = [((rows // 2, width), BF)] * 2
    last_got = [current[0][1]] if col_stages > 1 else [c[1] for c in current]
    project, message, blocks, moved = local(
        projections,
        shapes(summed) + halves,
        [mine, *other, *[c[0] for c in current], *last_got],
    )
    project_got = swap_row(message, [sum_order[0]] * 2)
    blocks_got = swap_row(moved, [move_order[0]] * 2)

    def join(mine, got, stage):
        shift = select_code(is_even(), (col_orders[0][stage], col_orders[1][stage]))
        low = jnp.bitwise_and(lax.shift_right_logical(lax.axis_index("col"), shift), 1) == 0
        mine, got = mine.astype(F32), got.astype(F32)
        return jnp.concatenate([jnp.where(low, mine, got), jnp.where(low, got, mine)], 0)

    joined = near
    for stage in range(col_stages - 1):
        joined *= 2
        (correlation,) = local(
            lambda mine, got, stage=stage: [join(mine, got, stage).astype(BF)],
            [((joined, panel_width), BF)],
            [correlation, swap_col(correlation, stage)],
            after=(message,),
        )
    other_correlation = swap_col(correlation, col_stages - 1)
    part_orders = [source_codes([bit - 1 for bit in order]) for order in col_orders]
    part_orders = [[order.index(part) for part in range(parts)] for order in part_orders]

    def update_factor(vectors, factors, mine, other):
        even = is_even()
        correlation = join(mine, other, col_stages - 1)
        ordered = [
            jnp.concatenate([correlation[i * near:(i + 1) * near] for i in order], 0) for order in part_orders
        ]
        correlation = jnp.where(even, ordered[0], ordered[1]).astype(BF)
        across = split_dot(vectors[1], split_dot(factors[1], correlation))
        first = split_dot(vectors[0].astype(F32) - across, factors[0])
        second = split_dot(vectors[1], factors[1])
        update = jnp.concatenate([jnp.where(even, first, second), jnp.where(even, second, first)], 1)
        return [swap_groups(update, 1, sum_order).astype(BF)]

    for stage in range(1, row_stages):
        last = stage == row_stages - 1
        size = summed if last else summed // 2

        def next_project(project, got, last=last, size=size):
            total = project + got.astype(F32)
            return total[:size], (total if last else total[size:]).astype(BF)

        project, message = local(
            next_project, shapes(size), [project, project_got], after=(correlation,) if stage == 1 else ()
        )
        project_got = swap_row(message, [sum_order[stage]] * 2)
        summed = size
    (update,) = local(
        update_factor,
        [((rows, wide), BF)],
        [vectors, panel_factors, correlation, other_correlation],
        after=(message,),
    )

    for stage in range(1, row_stages):
        blocks, moved = local(
            lambda blocks, got, targets=n_row >> stage: split_targets(jnp.concatenate([blocks, got], 0), targets),
            halves,
            [blocks, blocks_got],
        )
        blocks_got = swap_row(moved, [move_order[stage]] * 2)
    move_places = [source_codes(move_order).index(code) for code in range(n_row)]
    (cyclic,) = local(
        lambda blocks, got: [pick_blocks(jnp.concatenate([blocks, got], 0), move_places)],
        [((rows, width), BF)],
        [blocks, blocks_got],
    )
    (project,) = local(
        lambda project, got: [(project + got.astype(F32)).astype(BF)],
        [((summed, width), BF)],
        [project, project_got],
        after=(cyclic, update),
    )
    (total,) = local(
        lambda update, cyclic, project: [
            cyclic.astype(F32) - jnp.dot(update[:, :summed], project, preferred_element_type=F32)
        ],
        [((rows, width), F32)],
        [update, cyclic, project],
    )
    for stage in reversed(range(row_stages - 1)):
        got = swap_row(project, [sum_order[stage]] * 2)
        project = got if row_stages == 2 else jnp.concatenate([project, got], 0)
    rest = project if row_stages == 2 else project[summed:]
    return finish(n_row, total, update, rest, summed)


def solution(mesh):
    return jax.shard_map(
        functools.partial(shards, mesh.shape["row"], mesh.shape["col"]),
        mesh=mesh,
        in_specs=(P("row", "col"), P("col"), P("col"), P(), P(), P(), P(None, "row", None), P()),
        out_specs=P("row", "col"),
        check_vma=False,
    )
```

time: 124 us -> 48.7 us (0.39)
  waiting for transfers between devices: 87.6 us -> 17.6 us
  starting transfers between devices: 4.61 us -> 20.5 us
  matrix products: 14.3 us -> 0 us
  between operations: 13.4 us -> 0.16 us
  Pallas kernels: 0 us -> 10.2 us
  local copies, waits for them, and re-layouts: 3.3 us -> 0.01 us
    reduce_scatter x1 -> x0, waiting for transfers between devices: 44 us -> none  [shards(): lax.psum_scatter(partial_value.astype(jnp.bfloat16), 'col', scatter_dimen...]
    psum x1 -> x0, waiting for transfers between devices: 35.5 us -> none  [shards(): lax.psum(correlation_local.astype(jnp.bfloat16), 'row').astype(jnp.float32)]
    ppermute x0 -> x18, starting transfers between devices: none -> 20.5 us  [the longest x7 11.7 us: swap_row(): return lax.ppermute(value, ('row', 'col'), pairs)]
    ppermute x0 -> x18, waiting for transfers between devices: none -> 17.6 us  [the longest x5 11.4 us: swap_col(): lax.ppermute(value, 'col', [(i, i ^ 1 << col_orders[i % 2][stage]) for i...]
    dot_general x9 -> x0, matrix products: 14.3 us -> none  [the longest x1 7.78 us: shards(): partial_value = jnp.dot(eigvecs, matrix, preferred_element_type=jnp.float32)]
    pallas_call x0 -> x18, Pallas kernels: none -> 10.2 us  [the longest x3 5.23 us: products(): pl.pallas_call(functools.partial(product_kernel, plan, width, poles // 2,...]
    all_to_all x1 -> x0, waiting for transfers between devices: 7.98 us -> none  [shards(): lax.all_to_all(owned, 'row', split_axis=0, concat_axis=0, tiled=True)]
    all_to_all x1 -> x0, starting transfers between devices: 4.61 us -> none  [shards(): lax.all_to_all(owned, 'row', split_axis=0, concat_axis=0, tiled=True)]
  transfers between devices with their start and end apart: 3 -> 18, of which waited for: 3 -> 9; matrix products, arithmetic and copies ran while one was open for 1% -> 0% of each run, Pallas kernels for 0% -> 9%
where the time goes in v3:
time: 48.7 us; the launch traced here: 48.5 us
  starting transfers between devices  20.5 us (42%)
  waiting for transfers between devices  17.6 us (36%)
  Pallas kernels  10.2 us (21%)
    ppermute x7, starting transfers between devices, swap_row(): return lax.ppermute(value, ('row', 'col'), pairs)  11.7 us
    ppermute x5, waiting for transfers between devices, swap_col(): lax.ppermute(value, 'col', [(i, i ^ 1 << col_orders[i % 2][stage]) for i...  11.4 us
    ppermute x5, starting transfers between devices, swap_col(): lax.ppermute(value, 'col', [(i, i ^ 1 << col_orders[i % 2][stage]) for i...  6.75 us
    pallas_call x3, Pallas kernels, products(): pl.pallas_call(functools.partial(product_kernel, plan, width, poles // 2,...  5.23 us
    ppermute x7, waiting for transfers between devices, swap_row(): return lax.ppermute(value, ('row', 'col'), pairs)  5.22 us
    pallas_call x13, Pallas kernels, local(): pl.pallas_call(kernel, in_specs=[pl.BlockSpec(memory_space=pltpu.VMEM)] *...  2.15 us
    ppermute x6, starting transfers between devices, swap_cores(): return lax.ppermute(value, 'col', [(i, i ^ 1) for i in range(n_col)])  2.08 us
    pallas_call x1, Pallas kernels, panel_blocks(): pl.pallas_call(functools.partial(panel_kernel, row_codes, row_orders, blo...  1.87 us
  transfers between devices with their start and end apart: 18, of which 9 were waited for; matrix products, arithmetic and copies ran while one was open for 0% of the time, Pallas kernels for 9%

profile of v3, /device:TPU:0, one launch (start us, length us, event | category | flops | bytes accessed | tf_op | source)
XLA Modules:
  0.0 48.5 jit_solution(16384570449265205313)
XLA Ops:
  0.0 1.9 %shard_map.82 = (bf16[2,512,256]{2,1,0:T(8,128)(2,1)S(1)}, bf16[256,256]{1,0:T(8,128)(2,1)S(1)}, bf16[320,256]{1,0:T(8,128)(2,1)S(1)}, f32[64,256]{1,0:T(8,128)S...) custom-call(bf16[512,2048]{1,0:T(8,128)(2,1)} %refs_0_.1, ...), custom_call_target="tpu_custom_call" | custom-call | flops 1 | bytes 1 | tf_op jit(solution)/shard_map/pallas_call | solution.py:225
  1.9 2.5 %shard_map.85 = (bf16[512,256]{1,0:T(8,128)(2,1)S(1)}, bf16[512,256]{1,0:T(8,128)(2,1)S(1)}, bf16[512,256]{1,0:T(8,128)(2,1)S(1)}, bf16[512,256]{1,0:T(8,128)(2,1)S(1)}) custom-call(bf16[512,2048]{1,0:T(8,128)(2,1)S(1)} %get-tuple-element.44.refs_0_, f32[1,2048]{1,0:T(1,128)S(1)} %get-tuple-element.45.refs_1_, f32[1,2048]{1,0:T(1,128)S(1)} %get-tuple-element.46.refs_2_, ...), custom_call_target="tpu_custom_call" | custom-call | flops 1 | bytes 1 | tf_op jit(solution)/shard_map/pallas_call | solution.py:138
  4.4 0.5 %collective-permute-start.2 = (bf16[512,256]{1,0:T(8,128)(2,1)S(1)}, bf16[512,256]{1,0:T(8,128)(2,1)S(1)}, u32[]{:S(2)}, u32[]{:S(2)}) collective-permute-start(bf16[512,256]{1,0:T(8,128)(2,1)S(1)} %get-tuple-element.54), channel_id=1, source_target_pairs={{0,1},{1,0},{2,3},{3,2},{4,5},{5,4},{6,7},{7,6},{8,9},{9,8},{10,11... | collective-permute-start | bytes 786440 | tf_op jit(solution)/shard_map/ppermute | solution.py:326
  4.9 0.1 collective-permute-start.6
  5.0 3.0 %collective-permute-start = (bf16[320,256]{1,0:T(8,128)(2,1)S(1)}, bf16[320,256]{1,0:T(8,128)(2,1)S(1)}, u32[]{:S(2)}, u32[]{:S(2)}) collective-permute-start(bf16[320,256]{1,0:T(8,128)(2,1)S(1)} %get-tuple-element.43), channel_id=1, source_target_pairs={{0,8},{1,17},{2,10},{3,19},{4,12},{5,21},{6,14},{7,23},{8,0},{9,25... | collective-permute-start | bytes 491528 | tf_op jit(solution)/shard_map/ppermute | solution.py:333
  8.0 1.4 %shard_map.83 = (bf16[512,256]{1,0:T(8,128)(2,1)S(1)}, bf16[512,256]{1,0:T(8,128)(2,1)S(1)}) custom-call(bf16[512,2048]{1,0:T(8,128)(2,1)S(1)} %get-tuple-element.44.refs_0_, f32[1,2048]{1,0:T(1,128)S(1)} %get-tuple-element.45.refs_1_, f32[1,2048]{1,0:T(1,128)S(1)} %get-tuple-element.46.refs_2_, f32[1,2048]{1,0:T(1,128)S(1)} %get-tuple-element.47.refs_3_, ...), custom_call_target="tpu_custom_call" | custom-call | flops 1 | bytes 1 | tf_op jit(solution)/shard_map/pallas_call | solution.py:138
  9.3 0.8 %collective-permute-start.3 = (bf16[512,256]{1,0:T(8,128)(2,1)S(1)}, bf16[512,256]{1,0:T(8,128)(2,1)S(1)}, u32[]{:S(2)}, u32[]{:S(2)}) collective-permute-start(bf16[512,256]{1,0:T(8,128)(2,1)S(1)} %get-tuple-element.49.refs_3_.refs_2_), channel_id=1, source_target_pairs={{0,1},{1,0},{2,3},{3,2},{4,5},{5,4},{6,7},{7,6},{8,9},{9,8},{10,11... | collective-permute-start | bytes 786440 | tf_op jit(solution)/shard_map/ppermute | solution.py:326
  10.2 0.1 collective-permute-start.5
  10.3 0.0 collective-permute-done.2.refs_1_
  10.3 0.1 shard_map.86.refs_5_.refs_3_
  10.3 1.6 %collective-permute-start.4 = (bf16[512,256]{1,0:T(8,128)(2,1)S(1)}, bf16[512,256]{1,0:T(8,128)(2,1)S(1)}, u32[]{:S(2)}, u32[]{:S(2)}) collective-permute-start(bf16[512,256]{1,0:T(8,128)(2,1)S(1)} %shard_map.86.refs_5_.refs_3_), channel_id=1, source_target_pairs={{0,2},{1,5},{2,0},{3,7},{4,6},{5,1},{6,4},{7,3},{8,10},{9,13},{10,... | collective-permute-start | bytes 786440 | tf_op jit(solution)/shard_map/ppermute | solution.py:329
  11.9 0.0 collective-permute-done.6.refs_1_
  11.9 0.1 shard_map.88
  12.0 0.6 %collective-permute-start.7 = (bf16[512,256]{1,0:T(8,128)(2,1)S(1)}, bf16[512,256]{1,0:T(8,128)(2,1)S(1)}, u32[]{:S(2)}, u32[]{:S(2)}) collective-permute-start(bf16[512,256]{1,0:T(8,128)(2,1)S(1)} %shard_map.88), channel_id=1, source_target_pairs={{0,2},{1,5},{2,0},{3,7},{4,6},{5,1},{6,4},{7,3},{8,10},{9,13},{10,... | collective-permute-start | bytes 786440 | tf_op jit(solution)/shard_map/ppermute | solution.py:329
  12.6 0.2 collective-permute-done.refs_2_
  12.8 2.4 %collective-permute-start.1 = (bf16[320,256]{1,0:T(8,128)(2,1)S(1)}, bf16[320,256]{1,0:T(8,128)(2,1)S(1)}, u32[]{:S(2)}, u32[]{:S(2)}) collective-permute-start(bf16[320,256]{1,0:T(8,128)(2,1)S(1)} %get-tuple-element.52), channel_id=1, source_target_pairs={{0,16},{1,9},{2,18},{3,11},{4,20},{5,13},{6,22},{7,15},{8,24},{9,1... | collective-permute-start | bytes 491528 | tf_op jit(solution)/shard_map/ppermute | solution.py:333
  15.2 1.4 %shard_map.87 = (bf16[512,256]{1,0:T(8,128)(2,1)S(1)}, bf16[512,256]{1,0:T(8,128)(2,1)S(1)}) custom-call(bf16[512,2048]{1,0:T(8,128)(2,1)S(1)} %get-tuple-element.44.refs_0_, f32[1,2048]{1,0:T(1,128)S(1)} %get-tuple-element.45.refs_1_, f32[1,2048]{1,0:T(1,128)S(1)} %get-tuple-element.46.refs_2_, f32[1,2048]{1,0:T(1,128)S(1)} %get-tuple-element.47.refs_3_, ...), custom_call_target="tpu_custom_call" | custom-call | flops 1 | bytes 1 | tf_op jit(solution)/shard_map/pallas_call | solution.py:138
  16.6 0.0 collective-permute-done.3.refs_1_
  16.6 0.0 collective-permute-done.5.refs_4_
  16.6 0.2 collective-permute-done.4.refs_2_
  16.8 2.8 %collective-permute-done.7.refs_5_ = bf16[512,256]{1,0:T(8,128)(2,1)S(1)} collective-permute-done((bf16[512,256]{1,0:T(8,128)(2,1)S(1)}, bf16[512,256]{1,0:T(8,128)(2,1)S(1)}, u32[]{:S(2)}, u32[]{:S(2)}) %collective-permute-start.7) | collective-permute-done | bytes 262176 | tf_op jit(solution)/shard_map/ppermute | solution.py:329
  19.6 0.2 shard_map.89
  19.8 1.6 %collective-permute-start.11 = (bf16[512,256]{1,0:T(8,128)(2,1)S(1)}, bf16[512,256]{1,0:T(8,128)(2,1)S(1)}, u32[]{:S(2)}, u32[]{:S(2)}) collective-permute-start(bf16[512,256]{1,0:T(8,128)(2,1)S(1)} %get-tuple-element.60.refs_3_), channel_id=1, source_target_pairs={{0,4},{1,3},{2,6},{3,1},{4,0},{5,7},{6,2},{7,5},{8,12},{9,11},{10,... | collective-permute-start | bytes 786440 | tf_op jit(solution)/shard_map/ppermute | solution.py:329
  21.4 0.0 collective-permute-done.1.refs_2_
  21.4 0.1 shard_map.90
  21.4 0.1 collective-permute-start.9
  21.5 0.5 %collective-permute-start.10 = (bf16[128,256]{1,0:T(8,128)(2,1)S(1)}, bf16[128,256]{1,0:T(8,128)(2,1)S(1)}, u32[]{:S(2)}, u32[]{:S(2)}) collective-permute-start(bf16[128,256]{1,0:T(8,128)(2,1)S(1)} %get-tuple-element.64), channel_id=1, source_target_pairs={{0,1},{1,0},{2,3},{3,2},{4,5},{5,4},{6,7},{7,6},{8,9},{9,8},{10,11... | collective-permute-start | bytes 196616 | tf_op jit(solution)/shard_map/ppermute | solution.py:326
  22.0 1.0 %collective-permute-done.10.refs_2_ = bf16[128,256]{1,0:T(8,128)(2,1)S(1)} collective-permute-done((bf16[128,256]{1,0:T(8,128)(2,1)S(1)}, bf16[128,256]{1,0:T(8,128)(2,1)S(1)}, u32[]{:S(2)}, u32[]{:S(2)}) %collective-permute-start.10) | collective-permute-done | bytes 65568 | tf_op jit(solution)/shard_map/ppermute | solution.py:326
  23.0 0.0 collective-permute-done.9.refs_1_
  23.0 3.2 %collective-permute-done.11.refs_5_ = bf16[512,256]{1,0:T(8,128)(2,1)S(1)} collective-permute-done((bf16[512,256]{1,0:T(8,128)(2,1)S(1)}, bf16[512,256]{1,0:T(8,128)(2,1)S(1)}, u32[]{:S(2)}, u32[]{:S(2)}) %collective-permute-start.11) | collective-permute-done | bytes 262176 | tf_op jit(solution)/shard_map/ppermute | solution.py:329
  26.2 0.3 shard_map.91
  26.6 2.3 %collective-permute-start.14 = (bf16[256,256]{1,0:T(8,128)(2,1)S(1)}, bf16[256,256]{1,0:T(8,128)(2,1)S(1)}, u32[]{:S(2)}, u32[]{:S(2)}) collective-permute-start(bf16[256,256]{1,0:T(8,128)(2,1)S(1)} %get-tuple-element.71), channel_id=1, source_target_pairs={{0,16},{1,17},{2,18},{3,19},{4,20},{5,21},{6,22},{7,23},{8,24},{9,... | collective-permute-start | bytes 393224 | tf_op jit(solution)/shard_map/ppermute | solution.py:333
  28.9 0.4 collective-permute-start.13
  29.3 1.5 %collective-permute-start.8 = (bf16[64,256]{1,0:T(8,128)(2,1)S(1)}, bf16[64,256]{1,0:T(8,128)(2,1)S(1)}, u32[]{:S(2)}, u32[]{:S(2)}) collective-permute-start(bf16[64,256]{1,0:T(8,128)(2,1)S(1)} %get-tuple-element.61.refs_0_), channel_id=1, source_target_pairs={{0,2},{1,5},{2,0},{3,7},{4,6},{5,1},{6,4},{7,3},{8,10},{9,13},{10,... | collective-permute-start | bytes 98312 | tf_op jit(solution)/shard_map/ppermute | solution.py:329
  30.8 2.4 %collective-permute-done.8.refs_1_ = bf16[64,256]{1,0:T(8,128)(2,1)S(1)} collective-permute-done((bf16[64,256]{1,0:T(8,128)(2,1)S(1)}, bf16[64,256]{1,0:T(8,128)(2,1)S(1)}, u32[]{:S(2)}, u32[]{:S(2)}) %collective-permute-start.8) | collective-permute-done | bytes 32800 | tf_op jit(solution)/shard_map/ppermute | solution.py:329
  33.2 1.3 %collective-permute-done.14.refs_1_ = bf16[256,256]{1,0:T(8,128)(2,1)S(1)} collective-permute-done((bf16[256,256]{1,0:T(8,128)(2,1)S(1)}, bf16[256,256]{1,0:T(8,128)(2,1)S(1)}, u32[]{:S(2)}, u32[]{:S(2)}) %collective-permute-start.14) | collective-permute-done | bytes 131104 | tf_op jit(solution)/shard_map/ppermute | solution.py:333
  34.6 0.3 collective-permute-start.15
  34.9 0.0 collective-permute-done.13.refs_1_
  35.0 2.1 %collective-permute-start.16 = (bf16[256,256]{1,0:T(8,128)(2,1)S(1)}, bf16[256,256]{1,0:T(8,128)(2,1)S(1)}, u32[]{:S(2)}, u32[]{:S(2)}) collective-permute-start(bf16[256,256]{1,0:T(8,128)(2,1)S(1)} %get-tuple-element.69.refs_4_), channel_id=1, source_target_pairs={{0,16},{1,17},{2,18},{3,19},{4,20},{5,21},{6,22},{7,23},{8,24},{9,... | collective-permute-start | bytes 393224 | tf_op jit(solution)/shard_map/ppermute | solution.py:333
  37.1 1.5 %collective-permute-start.12 = (bf16[128,256]{1,0:T(8,128)(2,1)S(1)}, bf16[128,256]{1,0:T(8,128)(2,1)S(1)}, u32[]{:S(2)}, u32[]{:S(2)}) collective-permute-start(bf16[128,256]{1,0:T(8,128)(2,1)S(1)} %shard_map.92.refs_2_), channel_id=1, source_target_pairs={{0,4},{1,3},{2,6},{3,1},{4,0},{5,7},{6,2},{7,5},{8,12},{9,11},{10,... | collective-permute-start | bytes 196616 | tf_op jit(solution)/shard_map/ppermute | solution.py:329
  38.6 2.7 %collective-permute-done.12.refs_3_ = bf16[128,256]{1,0:T(8,128)(2,1)S(1)} collective-permute-done((bf16[128,256]{1,0:T(8,128)(2,1)S(1)}, bf16[128,256]{1,0:T(8,128)(2,1)S(1)}, u32[]{:S(2)}, u32[]{:S(2)}) %collective-permute-start.12) | collective-permute-done | bytes 65568 | tf_op jit(solution)/shard_map/ppermute | solution.py:329
  41.3 1.1 %shard_map.94.refs_3_.refs_0_.update = bf16[512,512]{1,0:T(8,128)(2,1)S(1)} custom-call(bf16[2,512,256]{2,1,0:T(8,128)(2,1)S(1)} %get-tuple-element.40.refs_0_, f32[2,256,256]{2,1,0:T(8,128)S(1)} %copy-done, bf16[128,256]{1,0:T(8,128)(2,1)S(1)} %shard_map.92.refs_2_, bf16[128,256]{1,0:T(8,128)(2,1)S(1)} %collective-permute-done.12.refs_3_, ...), custom_call_target="tpu_custom_call" | custom-call | flops 1 | bytes 1 | tf_op jit(solution)/shard_map/pallas_call | solution.py:70
  42.4 0.0 collective-permute-done.15.refs_1_
  42.5 0.0 collective-permute-done.16.refs_1_
  42.5 1.1 %collective-permute-start.17 = (bf16[256,256]{1,0:T(8,128)(2,1)S(1)}, bf16[256,256]{1,0:T(8,128)(2,1)S(1)}, u32[]{:S(2)}, u32[]{:S(2)}) collective-permute-start(bf16[256,256]{1,0:T(8,128)(2,1)S(1)} %shard_map.97.refs_2_), channel_id=1, source_target_pairs={{0,8},{1,9},{2,10},{3,11},{4,12},{5,13},{6,14},{7,15},{8,0},{9,1},... | collective-permute-start | bytes 393224 | tf_op jit(solution)/shard_map/ppermute | solution.py:333
  43.6 0.2 shard_map.98.total
  43.9 3.7 %collective-permute-done.17.project = bf16[256,256]{1,0:T(8,128)(2,1)S(1)} collective-permute-done((bf16[256,256]{1,0:T(8,128)(2,1)S(1)}, bf16[256,256]{1,0:T(8,128)(2,1)S(1)}, u32[]{:S(2)}, u32[]{:S(2)}) %collective-permute-start.17) | collective-permute-done | bytes 131104 | tf_op jit(solution)/shard_map/ppermute | solution.py:333
  47.5 1.0 %shard_map.99 = bf16[512,256]{1,0:T(8,128)(2,1)} custom-call(f32[512,256]{1,0:T(8,128)S(1)} %shard_map.98.total, bf16[512,512]{1,0:T(8,128)(2,1)S(1)} %shard_map.94.refs_3_.refs_0_.update, bf16[256,256]{1,0:T(8,128)(2,1)S(1)} %collective-permute-done.17.project), custom_call_target="tpu_custom_call" | custom-call | flops 1 | bytes 1 | tf_op jit(solution)/shard_map/pallas_call | solution.py:271
  (8 shorter events, 0.1 us)
Async XLA Ops:
  4.4 5.9 %collective-permute-start.2 = (bf16[512,256]{1,0:T(8,128)(2,1)S(1)}, bf16[512,256]{1,0:T(8,128)(2,1)S(1)}, u32[]{:S(2)}, u32[]{:S(2)}) collective-permute-start(bf16[512,256]{1,0:T(8,128)(2,1)S(1)} %get-tuple-element.54), channel_id=1, source_target_pairs={{0,1},{1,0},{2,3},{3,2},{4,5},{5,4},{6,7},{7,6},{8,9},{9,8},{10,11... | collective-permute-start | bytes 786440 | tf_op jit(solution)/shard_map/ppermute | solution.py:326
  4.9 7.0 %collective-permute-start.6 = (bf16[512,256]{1,0:T(8,128)(2,1)S(1)}, bf16[512,256]{1,0:T(8,128)(2,1)S(1)}, u32[]{:S(2)}, u32[]{:S(2)}) collective-permute-start(bf16[512,256]{1,0:T(8,128)(2,1)S(1)} %get-tuple-element.59), channel_id=1, source_target_pairs={{0,1},{1,0},{2,3},{3,2},{4,5},{5,4},{6,7},{7,6},{8,9},{9,8},{10,11... | collective-permute-start | bytes 786440 | tf_op jit(solution)/shard_map/ppermute | solution.py:326
  5.0 7.8 %collective-permute-start = (bf16[320,256]{1,0:T(8,128)(2,1)S(1)}, bf16[320,256]{1,0:T(8,128)(2,1)S(1)}, u32[]{:S(2)}, u32[]{:S(2)}) collective-permute-start(bf16[320,256]{1,0:T(8,128)(2,1)S(1)} %get-tuple-element.43), channel_id=1, source_target_pairs={{0,8},{1,17},{2,10},{3,19},{4,12},{5,21},{6,14},{7,23},{8,0},{9,25... | collective-permute-start | bytes 491528 | tf_op jit(solution)/shard_map/ppermute | solution.py:333
  9.3 7.2 %collective-permute-start.3 = (bf16[512,256]{1,0:T(8,128)(2,1)S(1)}, bf16[512,256]{1,0:T(8,128)(2,1)S(1)}, u32[]{:S(2)}, u32[]{:S(2)}) collective-permute-start(bf16[512,256]{1,0:T(8,128)(2,1)S(1)} %get-tuple-element.49.refs_3_.refs_2_), channel_id=1, source_target_pairs={{0,1},{1,0},{2,3},{3,2},{4,5},{5,4},{6,7},{7,6},{8,9},{9,8},{10,11... | collective-permute-start | bytes 786440 | tf_op jit(solution)/shard_map/ppermute | solution.py:326
  10.2 6.4 %collective-permute-start.5 = (bf16[512,256]{1,0:T(8,128)(2,1)S(1)}, bf16[512,256]{1,0:T(8,128)(2,1)S(1)}, u32[]{:S(2)}, u32[]{:S(2)}) collective-permute-start(bf16[512,256]{1,0:T(8,128)(2,1)S(1)} %get-tuple-element.57), channel_id=1, source_target_pairs={{0,1},{1,0},{2,3},{3,2},{4,5},{5,4},{6,7},{7,6},{8,9},{9,8},{10,11... | collective-permute-start | bytes 786440 | tf_op jit(solution)/shard_map/ppermute | solution.py:326
  10.3 6.4 %collective-permute-start.4 = (bf16[512,256]{1,0:T(8,128)(2,1)S(1)}, bf16[512,256]{1,0:T(8,128)(2,1)S(1)}, u32[]{:S(2)}, u32[]{:S(2)}) collective-permute-start(bf16[512,256]{1,0:T(8,128)(2,1)S(1)} %shard_map.86.refs_5_.refs_3_), channel_id=1, source_target_pairs={{0,2},{1,5},{2,0},{3,7},{4,6},{5,1},{6,4},{7,3},{8,10},{9,13},{10,... | collective-permute-start | bytes 786440 | tf_op jit(solution)/shard_map/ppermute | solution.py:329
  12.0 7.6 %collective-permute-start.7 = (bf16[512,256]{1,0:T(8,128)(2,1)S(1)}, bf16[512,256]{1,0:T(8,128)(2,1)S(1)}, u32[]{:S(2)}, u32[]{:S(2)}) collective-permute-start(bf16[512,256]{1,0:T(8,128)(2,1)S(1)} %shard_map.88), channel_id=1, source_target_pairs={{0,2},{1,5},{2,0},{3,7},{4,6},{5,1},{6,4},{7,3},{8,10},{9,13},{10,... | collective-permute-start | bytes 786440 | tf_op jit(solution)/shard_map/ppermute | solution.py:329
  12.8 8.6 %collective-permute-start.1 = (bf16[320,256]{1,0:T(8,128)(2,1)S(1)}, bf16[320,256]{1,0:T(8,128)(2,1)S(1)}, u32[]{:S(2)}, u32[]{:S(2)}) collective-permute-start(bf16[320,256]{1,0:T(8,128)(2,1)S(1)} %get-tuple-element.52), channel_id=1, source_target_pairs={{0,16},{1,9},{2,18},{3,11},{4,20},{5,13},{6,22},{7,15},{8,24},{9,1... | collective-permute-start | bytes 491528 | tf_op jit(solution)/shard_map/ppermute | solution.py:333
  19.6 21.8 %copy-start = (f32[2,256,256]{2,1,0:T(8,128)S(1)}, f32[2,256,256]{2,1,0:T(8,128)}, u32[]{:S(2)}) copy-start(f32[2,256,256]{2,1,0:T(8,128)} %refs_1_.3) | copy-start | bytes 1572868
  19.8 6.4 %collective-permute-start.11 = (bf16[512,256]{1,0:T(8,128)(2,1)S(1)}, bf16[512,256]{1,0:T(8,128)(2,1)S(1)}, u32[]{:S(2)}, u32[]{:S(2)}) collective-permute-start(bf16[512,256]{1,0:T(8,128)(2,1)S(1)} %get-tuple-element.60.refs_3_), channel_id=1, source_target_pairs={{0,4},{1,3},{2,6},{3,1},{4,0},{5,7},{6,2},{7,5},{8,12},{9,11},{10,... | collective-permute-start | bytes 786440 | tf_op jit(solution)/shard_map/ppermute | solution.py:329
  21.4 1.6 %collective-permute-start.9 = (bf16[384,256]{1,0:T(8,128)(2,1)S(1)}, bf16[384,256]{1,0:T(8,128)(2,1)S(1)}, u32[]{:S(2)}, u32[]{:S(2)}) collective-permute-start(bf16[384,256]{1,0:T(8,128)(2,1)S(1)} %get-tuple-element.63), channel_id=1, source_target_pairs={{0,1},{1,0},{2,3},{3,2},{4,5},{5,4},{6,7},{7,6},{8,9},{9,8},{10,11... | collective-permute-start | bytes 589832 | tf_op jit(solution)/shard_map/ppermute | solution.py:326
  21.5 1.5 %collective-permute-start.10 = (bf16[128,256]{1,0:T(8,128)(2,1)S(1)}, bf16[128,256]{1,0:T(8,128)(2,1)S(1)}, u32[]{:S(2)}, u32[]{:S(2)}) collective-permute-start(bf16[128,256]{1,0:T(8,128)(2,1)S(1)} %get-tuple-element.64), channel_id=1, source_target_pairs={{0,1},{1,0},{2,3},{3,2},{4,5},{5,4},{6,7},{7,6},{8,9},{9,8},{10,11... | collective-permute-start | bytes 196616 | tf_op jit(solution)/shard_map/ppermute | solution.py:326
  26.6 8.0 %collective-permute-start.14 = (bf16[256,256]{1,0:T(8,128)(2,1)S(1)}, bf16[256,256]{1,0:T(8,128)(2,1)S(1)}, u32[]{:S(2)}, u32[]{:S(2)}) collective-permute-start(bf16[256,256]{1,0:T(8,128)(2,1)S(1)} %get-tuple-element.71), channel_id=1, source_target_pairs={{0,16},{1,17},{2,18},{3,19},{4,20},{5,21},{6,22},{7,23},{8,24},{9,... | collective-permute-start | bytes 393224 | tf_op jit(solution)/shard_map/ppermute | solution.py:333
  28.9 6.1 %collective-permute-start.13 = (bf16[256,256]{1,0:T(8,128)(2,1)S(1)}, bf16[256,256]{1,0:T(8,128)(2,1)S(1)}, u32[]{:S(2)}, u32[]{:S(2)}) collective-permute-start(bf16[256,256]{1,0:T(8,128)(2,1)S(1)} %get-tuple-element.67.refs_2_), channel_id=1, source_target_pairs={{0,8},{1,9},{2,10},{3,11},{4,12},{5,13},{6,14},{7,15},{8,0},{9,1},... | collective-permute-start | bytes 393224 | tf_op jit(solution)/shard_map/ppermute | solution.py:333
  29.3 3.9 %collective-permute-start.8 = (bf16[64,256]{1,0:T(8,128)(2,1)S(1)}, bf16[64,256]{1,0:T(8,128)(2,1)S(1)}, u32[]{:S(2)}, u32[]{:S(2)}) collective-permute-start(bf16[64,256]{1,0:T(8,128)(2,1)S(1)} %get-tuple-element.61.refs_0_), channel_id=1, source_target_pairs={{0,2},{1,5},{2,0},{3,7},{4,6},{5,1},{6,4},{7,3},{8,10},{9,13},{10,... | collective-permute-start | bytes 98312 | tf_op jit(solution)/shard_map/ppermute | solution.py:329
  34.6 7.9 %collective-permute-start.15 = (bf16[256,256]{1,0:T(8,128)(2,1)S(1)}, bf16[256,256]{1,0:T(8,128)(2,1)S(1)}, u32[]{:S(2)}, u32[]{:S(2)}) collective-permute-start(bf16[256,256]{1,0:T(8,128)(2,1)S(1)} %get-tuple-element.73), channel_id=1, source_target_pairs={{0,8},{1,9},{2,10},{3,11},{4,12},{5,13},{6,14},{7,15},{8,0},{9,1},... | collective-permute-start | bytes 393224 | tf_op jit(solution)/shard_map/ppermute | solution.py:333
  35.0 7.5 %collective-permute-start.16 = (bf16[256,256]{1,0:T(8,128)(2,1)S(1)}, bf16[256,256]{1,0:T(8,128)(2,1)S(1)}, u32[]{:S(2)}, u32[]{:S(2)}) collective-permute-start(bf16[256,256]{1,0:T(8,128)(2,1)S(1)} %get-tuple-element.69.refs_4_), channel_id=1, source_target_pairs={{0,16},{1,17},{2,18},{3,19},{4,20},{5,21},{6,22},{7,23},{8,24},{9,... | collective-permute-start | bytes 393224 | tf_op jit(solution)/shard_map/ppermute | solution.py:333
  37.1 4.3 %collective-permute-start.12 = (bf16[128,256]{1,0:T(8,128)(2,1)S(1)}, bf16[128,256]{1,0:T(8,128)(2,1)S(1)}, u32[]{:S(2)}, u32[]{:S(2)}) collective-permute-start(bf16[128,256]{1,0:T(8,128)(2,1)S(1)} %shard_map.92.refs_2_), channel_id=1, source_target_pairs={{0,4},{1,3},{2,6},{3,1},{4,0},{5,7},{6,2},{7,5},{8,12},{9,11},{10,... | collective-permute-start | bytes 196616 | tf_op jit(solution)/shard_map/ppermute | solution.py:329
  42.5 5.0 %collective-permute-start.17 = (bf16[256,256]{1,0:T(8,128)(2,1)S(1)}, bf16[256,256]{1,0:T(8,128)(2,1)S(1)}, u32[]{:S(2)}, u32[]{:S(2)}) collective-permute-start(bf16[256,256]{1,0:T(8,128)(2,1)S(1)} %shard_map.97.refs_2_), channel_id=1, source_target_pairs={{0,8},{1,9},{2,10},{3,11},{4,12},{5,13},{6,14},{7,15},{8,0},{9,1},... | collective-permute-start | bytes 393224 | tf_op jit(solution)/shard_map/ppermute | solution.py:333

commit v4 on v3

--- a/solution.py
+++ b/solution.py
@@ -79,21 +79,27 @@
     )
 
 
-def product_kernel(plan, width, depth, chunks, n_after, *refs):
+def product_kernel(plan, width, chunks, depth, n_after, *refs):
     eig, pole_values, weights, roots, scale = refs[:5]
     outs = refs[5 + n_after:]
-    rows, poles = eig.shape
+    poles = eig.shape[1]
     me = lax.axis_index("col")
     even = is_even()
     piece = width // chunks
+    group = max(256 // piece, 1)
     pole_values = pole_values[...]
     weights = weights[...]
-    for entry, codes in enumerate(plan):
-        for place, pair in enumerate(codes):
-            at = pl.ds(pl.multiple_of(jnp.bitwise_xor(me, select_code(even, pair)) * width, width), width)
-            near = roots[:, at]
+    for out, (chunk, codes) in zip(outs, plan):
+        for place in range(0, len(codes), group):
+            columns = [
+                pl.ds(
+                    pl.multiple_of(jnp.bitwise_xor(me, select_code(even, pair)) * width + chunk * piece, piece), piece
+                )
+                for pair in codes[place:place + group]
+            ]
+            near = jnp.concatenate([roots[:, at] for at in columns], 1)
             near = jnp.concatenate(
-                [jnp.broadcast_to(near[:, j:j + 128], (128, 128)).T for j in range(0, width, 128)], 0
+                [jnp.broadcast_to(near[:, j:j + 128], (128, 128)).T for j in range(0, near.shape[1], 128)], 0
             )
             total = None
             for k in range(0, poles, depth):
@@ -103,11 +109,8 @@
                     eig[:, k:k + depth], matrix, (((1,), (1,)), ((), ())), preferred_element_type=F32
                 )
                 total = term if total is None else total + term
-            total = (total * scale[:, at]).astype(BF)
-            for chunk in range(chunks):
-                outs[entry * chunks + chunk][:, place * piece:(place + 1) * piece] = total[
-                    :, chunk * piece:(chunk + 1) * piece
-                ]
+            total = total * jnp.concatenate([scale[:, at] for at in columns], 1)
+            out[:, place * piece:place * piece + total.shape[1]] = total.astype(BF)
 
 
 def plain_products(plan, row_codes, parts, chunks, operands):
@@ -117,15 +120,14 @@
     places = jnp.bitwise_xor(lax.axis_index("row"), jnp.array(row_codes, jnp.int32))
     ordered = eigvecs.reshape(len(row_codes), -1, poles)[places].reshape(eigvecs.shape)
     results = []
-    for codes in plan:
+    for chunk, codes in plan:
         places = jnp.array([[a, b] for a, b in codes], jnp.int32)
         places = jnp.bitwise_xor(me, jnp.where(is_even(), places[:, 0], places[:, 1]))
-        pick = lambda v: v.reshape(parts, chunks, -1)[places].transpose(1, 0, 2).reshape(-1)
+        pick = lambda v: v.reshape(parts, chunks, -1)[places, chunk].reshape(-1)
         root_values = 2.0 * pick(root_gap).astype(F32) + 1.0 + pick(root_shift)
         numer = pole_weight[:, None] * pick(column_weight)[None, :]
         gaps = 2.0 * pole_order.astype(F32)[:, None] - root_values[None, :]
-        result = jnp.dot(ordered, (numer / gaps).astype(BF), preferred_element_type=F32).astype(BF)
-        results += jnp.split(result, chunks, 1)
+        results.append(jnp.dot(ordered, (numer / gaps).astype(BF), preferred_element_type=F32).astype(BF))
     return results
 
 
@@ -134,11 +136,9 @@
     width = operands[3].shape[0] // parts
     if state is None:
         return plain_products(plan, row_codes, parts, chunks, operands)
-    outs = [pltpu.VMEM((rows, width // chunks * len(codes)), BF) for codes in plan for _ in range(chunks)]
+    outs = [pltpu.VMEM((rows, width // chunks * len(codes)), BF) for _, codes in plan]
     return pl.pallas_call(
-        functools.partial(
-            product_kernel, plan, width, poles // 2, chunks, len(after)
-        ),
+        functools.partial(product_kernel, plan, width, chunks, poles // 2, len(after)),
         in_specs=[pl.BlockSpec(memory_space=pltpu.VMEM)] * 5 + [pl.BlockSpec(memory_space=pl.ANY)] * len(after),
         out_specs=[pl.BlockSpec(memory_space=pltpu.VMEM)] * len(outs),
         out_shape=outs,
@@ -354,11 +354,12 @@
     multiply = functools.partial(
         products, row_codes=targets, parts=n_col, chunks=chunks, operands=operands, state=state
     )
-    first = multiply([other_codes[half:], own_codes[half:]])
-    other_sent, own_sent = first[:chunks], first[chunks:]
-    got_sent = [swap_cores(value) for value in other_sent]
-    other_kept = multiply([other_codes[:half]])
-    got_kept = [swap_cores(value) for value in other_kept]
+    got_sent, own_sent, made = [], [], ()
+    for chunk in range(chunks):
+        other, own = multiply([(chunk, other_codes[half:]), (chunk, own_codes[half:])], after=made)
+        got_sent.append(swap_cores(other))
+        own_sent.append(own)
+        made = (own,)
     long = half * piece
     sent = []
     for own, got in zip(own_sent, got_sent):
@@ -366,11 +367,13 @@
             lambda own, got: [(own.astype(F32) + got.astype(F32)).astype(BF)],
             [((rows, long), BF)],
             [own, got],
-            after=(other_kept[0], *sent),
+            after=(*made, *sent),
         )
         sent.append(value)
     got = [swap_col(message, 0) for message in sent]
-    own_kept = multiply([own_codes[:half]], after=(sent[0],))
+    other_kept = multiply([(chunk, other_codes[:half]) for chunk in range(chunks)], after=(sent[-1],))
+    got_kept = [swap_cores(value) for value in other_kept]
+    own_kept = multiply([(chunk, own_codes[:half]) for chunk in range(chunks)], after=(other_kept[0],))
 
     current = [[own, other, new] for own, other, new in zip(own_kept, got_kept, got)]
     for stage in range(1, col_stages):

time: 48.7 us -> 47.9 us (0.984)
  waiting for transfers between devices: 17.6 us -> 16.7 us
    ppermute x5, waiting for transfers between devices: 11.4 us -> 8.91 us  [swap_col(): lax.ppermute(value, 'col', [(i, i ^ 1 << col_orders[i % 2][stage]) for i...]
    ppermute x7, waiting for transfers between devices: 5.22 us -> 6.8 us  [swap_row(): return lax.ppermute(value, ('row', 'col'), pairs)]
    pallas_call x3 -> x4, Pallas kernels: 5.23 us -> 5.48 us  [products(): pl.pallas_call(functools.partial(product_kernel, plan, width, chunks, pol...]
  transfers between devices with their start and end apart: 18 -> 18, of which waited for: 9 -> 10; matrix products, arithmetic and copies ran while one was open for 0% -> 0% of each run, Pallas kernels for 9% -> 12%
where the time goes in v4:
time: 47.9 us; the launch traced here: 47.7 us
  starting transfers between devices  20.4 us (43%)
  waiting for transfers between devices  16.7 us (35%)
  Pallas kernels  10.5 us (22%)
    ppermute x7, starting transfers between devices, swap_row(): return lax.ppermute(value, ('row', 'col'), pairs)  11.8 us
    ppermute x5, waiting for transfers between devices, swap_col(): lax.ppermute(value, 'col', [(i, i ^ 1 << col_orders[i % 2][stage]) for i...  8.91 us
    ppermute x7, waiting for transfers between devices, swap_row(): return lax.ppermute(value, ('row', 'col'), pairs)  6.8 us
    ppermute x5, starting transfers between devices, swap_col(): lax.ppermute(value, 'col', [(i, i ^ 1 << col_orders[i % 2][stage]) for i...  6.76 us
    pallas_call x4, Pallas kernels, products(): pl.pallas_call(functools.partial(product_kernel, plan, width, chunks, pol...  5.48 us
    pallas_call x13, Pallas kernels, local(): pl.pallas_call(kernel, in_specs=[pl.BlockSpec(memory_space=pltpu.VMEM)] *...  2.16 us
    pallas_call x1, Pallas kernels, panel_blocks(): pl.pallas_call(functools.partial(panel_kernel, row_codes, row_orders, blo...  1.87 us
    ppermute x6, starting transfers between devices, swap_cores(): return lax.ppermute(value, 'col', [(i, i ^ 1) for i in range(n_col)])  1.79 us
  transfers between devices with their start and end apart: 18, of which 10 were waited for; matrix products, arithmetic and copies ran while one was open for 0% of the time, Pallas kernels for 12%

profile of v4, /device:TPU:0, one launch (start us, length us, event | category | flops | bytes accessed | tf_op | source)
XLA Modules:
  0.0 47.7 jit_solution(5227800675096424792)
XLA Ops:
  0.0 1.9 %shard_map.82 = (bf16[2,512,256]{2,1,0:T(8,128)(2,1)S(1)}, bf16[256,256]{1,0:T(8,128)(2,1)S(1)}, bf16[320,256]{1,0:T(8,128)(2,1)S(1)}, f32[64,256]{1,0:T(8,128)S...) custom-call(bf16[512,2048]{1,0:T(8,128)(2,1)} %refs_0_.1, ...), custom_call_target="tpu_custom_call" | custom-call | flops 1 | bytes 1 | tf_op jit(solution)/shard_map/pallas_call | solution.py:225
  1.9 1.4 %shard_map.83 = (bf16[512,256]{1,0:T(8,128)(2,1)S(1)}, bf16[512,256]{1,0:T(8,128)(2,1)S(1)}) custom-call(bf16[512,2048]{1,0:T(8,128)(2,1)S(1)} %get-tuple-element.44.refs_0_, f32[1,2048]{1,0:T(1,128)S(1)} %get-tuple-element.45.refs_1_, f32[1,2048]{1,0:T(1,128)S(1)} %get-tuple-element.46.refs_2_, f32[1,2048]{1,0:T(1,128)S(1)} %get-tuple-element.47.refs_3_, ...), custom_call_target="tpu_custom_call" | custom-call | flops 1 | bytes 1 | tf_op jit(solution)/shard_map/pallas_call | solution.py:140
  3.3 0.5 %collective-permute-start.2 = (bf16[512,256]{1,0:T(8,128)(2,1)S(1)}, bf16[512,256]{1,0:T(8,128)(2,1)S(1)}, u32[]{:S(2)}, u32[]{:S(2)}) collective-permute-start(bf16[512,256]{1,0:T(8,128)(2,1)S(1)} %get-tuple-element.52), channel_id=1, source_target_pairs={{0,1},{1,0},{2,3},{3,2},{4,5},{5,4},{6,7},{7,6},{8,9},{9,8},{10,11... | collective-permute-start | bytes 786440 | tf_op jit(solution)/shard_map/ppermute | solution.py:326
  3.8 1.4 %shard_map.84 = (bf16[512,256]{1,0:T(8,128)(2,1)S(1)}, bf16[512,256]{1,0:T(8,128)(2,1)S(1)}) custom-call(bf16[512,2048]{1,0:T(8,128)(2,1)S(1)} %get-tuple-element.44.refs_0_, f32[1,2048]{1,0:T(1,128)S(1)} %get-tuple-element.45.refs_1_, f32[1,2048]{1,0:T(1,128)S(1)} %get-tuple-element.46.refs_2_, f32[1,2048]{1,0:T(1,128)S(1)} %get-tuple-element.47.refs_3_, ...), custom_call_target="tpu_custom_call" | custom-call | flops 1 | bytes 1 | tf_op jit(solution)/shard_map/pallas_call | solution.py:140
  5.2 0.1 collective-permute-start.1
  5.3 3.0 %collective-permute-start = (bf16[320,256]{1,0:T(8,128)(2,1)S(1)}, bf16[320,256]{1,0:T(8,128)(2,1)S(1)}, u32[]{:S(2)}, u32[]{:S(2)}) collective-permute-start(bf16[320,256]{1,0:T(8,128)(2,1)S(1)} %get-tuple-element.43), channel_id=1, source_target_pairs={{0,8},{1,17},{2,10},{3,19},{4,12},{5,21},{6,14},{7,23},{8,0},{9,25... | collective-permute-start | bytes 491528 | tf_op jit(solution)/shard_map/ppermute | solution.py:333
  8.3 0.0 collective-permute-done.2.refs_1_
  8.3 0.1 shard_map.85.refs_3_
  8.4 1.6 %collective-permute-start.5 = (bf16[512,256]{1,0:T(8,128)(2,1)S(1)}, bf16[512,256]{1,0:T(8,128)(2,1)S(1)}, u32[]{:S(2)}, u32[]{:S(2)}) collective-permute-start(bf16[512,256]{1,0:T(8,128)(2,1)S(1)} %shard_map.85.refs_3_), channel_id=1, source_target_pairs={{0,2},{1,5},{2,0},{3,7},{4,6},{5,1},{6,4},{7,3},{8,10},{9,13},{10,... | collective-permute-start | bytes 786440 | tf_op jit(solution)/shard_map/ppermute | solution.py:329
  9.9 0.0 collective-permute-done.1.refs_1_
  9.9 0.1 shard_map.86.refs_5_
  10.0 0.6 %collective-permute-start.7 = (bf16[512,256]{1,0:T(8,128)(2,1)S(1)}, bf16[512,256]{1,0:T(8,128)(2,1)S(1)}, u32[]{:S(2)}, u32[]{:S(2)}) collective-permute-start(bf16[512,256]{1,0:T(8,128)(2,1)S(1)} %shard_map.86.refs_5_), channel_id=1, source_target_pairs={{0,2},{1,5},{2,0},{3,7},{4,6},{5,1},{6,4},{7,3},{8,10},{9,13},{10,... | collective-permute-start | bytes 786440 | tf_op jit(solution)/shard_map/ppermute | solution.py:329
  10.6 1.4 %shard_map.87 = (bf16[512,256]{1,0:T(8,128)(2,1)S(1)}, bf16[512,256]{1,0:T(8,128)(2,1)S(1)}) custom-call(bf16[512,2048]{1,0:T(8,128)(2,1)S(1)} %get-tuple-element.44.refs_0_, f32[1,2048]{1,0:T(1,128)S(1)} %get-tuple-element.45.refs_1_, f32[1,2048]{1,0:T(1,128)S(1)} %get-tuple-element.46.refs_2_, f32[1,2048]{1,0:T(1,128)S(1)} %get-tuple-element.47.refs_3_, ...), custom_call_target="tpu_custom_call" | custom-call | flops 1 | bytes 1 | tf_op jit(solution)/shard_map/pallas_call | solution.py:140
  12.0 0.3 collective-permute-start.6
  12.2 0.3 collective-permute-start.4
  12.5 0.6 %collective-permute-done.refs_2_ = bf16[320,256]{1,0:T(8,128)(2,1)S(1)} collective-permute-done((bf16[320,256]{1,0:T(8,128)(2,1)S(1)}, bf16[320,256]{1,0:T(8,128)(2,1)S(1)}, u32[]{:S(2)}, u32[]{:S(2)}) %collective-permute-start) | collective-permute-done | bytes 163872 | tf_op jit(solution)/shard_map/ppermute | solution.py:333
  13.1 2.4 %collective-permute-start.3 = (bf16[320,256]{1,0:T(8,128)(2,1)S(1)}, bf16[320,256]{1,0:T(8,128)(2,1)S(1)}, u32[]{:S(2)}, u32[]{:S(2)}) collective-permute-start(bf16[320,256]{1,0:T(8,128)(2,1)S(1)} %get-tuple-element.56), channel_id=1, source_target_pairs={{0,16},{1,9},{2,18},{3,11},{4,20},{5,13},{6,22},{7,15},{8,24},{9,1... | collective-permute-start | bytes 491528 | tf_op jit(solution)/shard_map/ppermute | solution.py:333
  15.5 1.4 %shard_map.89 = (bf16[512,256]{1,0:T(8,128)(2,1)S(1)}, bf16[512,256]{1,0:T(8,128)(2,1)S(1)}) custom-call(bf16[512,2048]{1,0:T(8,128)(2,1)S(1)} %get-tuple-element.44.refs_0_, f32[1,2048]{1,0:T(1,128)S(1)} %get-tuple-element.45.refs_1_, f32[1,2048]{1,0:T(1,128)S(1)} %get-tuple-element.46.refs_2_, f32[1,2048]{1,0:T(1,128)S(1)} %get-tuple-element.47.refs_3_, ...), custom_call_target="tpu_custom_call" | custom-call | flops 1 | bytes 1 | tf_op jit(solution)/shard_map/pallas_call | solution.py:140
  16.9 0.7 %collective-permute-done.7.refs_5_ = bf16[512,256]{1,0:T(8,128)(2,1)S(1)} collective-permute-done((bf16[512,256]{1,0:T(8,128)(2,1)S(1)}, bf16[512,256]{1,0:T(8,128)(2,1)S(1)}, u32[]{:S(2)}, u32[]{:S(2)}) %collective-permute-start.7) | collective-permute-done | bytes 262176 | tf_op jit(solution)/shard_map/ppermute | solution.py:329
  17.6 0.0 collective-permute-done.5.refs_2_
  17.6 0.0 collective-permute-done.6.refs_4_
  17.6 0.0 collective-permute-done.4.refs_1_
  17.6 0.0 copy-start
  17.6 0.2 shard_map.90
  17.8 1.6 %collective-permute-start.11 = (bf16[512,256]{1,0:T(8,128)(2,1)S(1)}, bf16[512,256]{1,0:T(8,128)(2,1)S(1)}, u32[]{:S(2)}, u32[]{:S(2)}) collective-permute-start(bf16[512,256]{1,0:T(8,128)(2,1)S(1)} %get-tuple-element.60.refs_3_), channel_id=1, source_target_pairs={{0,4},{1,3},{2,6},{3,1},{4,0},{5,7},{6,2},{7,5},{8,12},{9,11},{10,... | collective-permute-start | bytes 786440 | tf_op jit(solution)/shard_map/ppermute | solution.py:329
  19.4 0.2 collective-permute-done.3.refs_2_
  19.7 0.2 collective-permute-start.9
  19.9 0.4 collective-permute-start.10
  20.2 1.0 %collective-permute-done.10.refs_2_ = bf16[128,256]{1,0:T(8,128)(2,1)S(1)} collective-permute-done((bf16[128,256]{1,0:T(8,128)(2,1)S(1)}, bf16[128,256]{1,0:T(8,128)(2,1)S(1)}, u32[]{:S(2)}, u32[]{:S(2)}) %collective-permute-start.10) | collective-permute-done | bytes 65568 | tf_op jit(solution)/shard_map/ppermute | solution.py:326
  21.3 3.0 %collective-permute-done.11.refs_5_ = bf16[512,256]{1,0:T(8,128)(2,1)S(1)} collective-permute-done((bf16[512,256]{1,0:T(8,128)(2,1)S(1)}, bf16[512,256]{1,0:T(8,128)(2,1)S(1)}, u32[]{:S(2)}, u32[]{:S(2)}) %collective-permute-start.11) | collective-permute-done | bytes 262176 | tf_op jit(solution)/shard_map/ppermute | solution.py:329
  24.3 0.3 shard_map.92
  24.6 2.6 %collective-permute-start.14 = (bf16[256,256]{1,0:T(8,128)(2,1)S(1)}, bf16[256,256]{1,0:T(8,128)(2,1)S(1)}, u32[]{:S(2)}, u32[]{:S(2)}) collective-permute-start(bf16[256,256]{1,0:T(8,128)(2,1)S(1)} %get-tuple-element.71), channel_id=1, source_target_pairs={{0,16},{1,17},{2,18},{3,19},{4,20},{5,21},{6,22},{7,23},{8,24},{9,... | collective-permute-start | bytes 393224 | tf_op jit(solution)/shard_map/ppermute | solution.py:333
  27.3 0.4 collective-permute-start.13
  27.7 1.5 %collective-permute-start.8 = (bf16[64,256]{1,0:T(8,128)(2,1)S(1)}, bf16[64,256]{1,0:T(8,128)(2,1)S(1)}, u32[]{:S(2)}, u32[]{:S(2)}) collective-permute-start(bf16[64,256]{1,0:T(8,128)(2,1)S(1)} %get-tuple-element.61.refs_0_), channel_id=1, source_target_pairs={{0,2},{1,5},{2,0},{3,7},{4,6},{5,1},{6,4},{7,3},{8,10},{9,13},{10,... | collective-permute-start | bytes 98312 | tf_op jit(solution)/shard_map/ppermute | solution.py:329
  29.2 2.4 %collective-permute-done.8.refs_1_ = bf16[64,256]{1,0:T(8,128)(2,1)S(1)} collective-permute-done((bf16[64,256]{1,0:T(8,128)(2,1)S(1)}, bf16[64,256]{1,0:T(8,128)(2,1)S(1)}, u32[]{:S(2)}, u32[]{:S(2)}) %collective-permute-start.8) | collective-permute-done | bytes 32800 | tf_op jit(solution)/shard_map/ppermute | solution.py:329
  31.6 1.3 %collective-permute-done.14.refs_1_ = bf16[256,256]{1,0:T(8,128)(2,1)S(1)} collective-permute-done((bf16[256,256]{1,0:T(8,128)(2,1)S(1)}, bf16[256,256]{1,0:T(8,128)(2,1)S(1)}, u32[]{:S(2)}, u32[]{:S(2)}) %collective-permute-start.14) | collective-permute-done | bytes 131104 | tf_op jit(solution)/shard_map/ppermute | solution.py:333
  33.0 0.4 collective-permute-start.15
  33.3 0.0 collective-permute-done.13.refs_1_
  33.4 2.7 %collective-permute-start.16 = (bf16[256,256]{1,0:T(8,128)(2,1)S(1)}, bf16[256,256]{1,0:T(8,128)(2,1)S(1)}, u32[]{:S(2)}, u32[]{:S(2)}) collective-permute-start(bf16[256,256]{1,0:T(8,128)(2,1)S(1)} %get-tuple-element.69.refs_4_), channel_id=1, source_target_pairs={{0,16},{1,17},{2,18},{3,19},{4,20},{5,21},{6,22},{7,23},{8,24},{9,... | collective-permute-start | bytes 393224 | tf_op jit(solution)/shard_map/ppermute | solution.py:333
  36.1 1.5 %collective-permute-start.12 = (bf16[128,256]{1,0:T(8,128)(2,1)S(1)}, bf16[128,256]{1,0:T(8,128)(2,1)S(1)}, u32[]{:S(2)}, u32[]{:S(2)}) collective-permute-start(bf16[128,256]{1,0:T(8,128)(2,1)S(1)} %shard_map.93.refs_2_), channel_id=1, source_target_pairs={{0,4},{1,3},{2,6},{3,1},{4,0},{5,7},{6,2},{7,5},{8,12},{9,11},{10,... | collective-permute-start | bytes 196616 | tf_op jit(solution)/shard_map/ppermute | solution.py:329
  37.6 2.7 %collective-permute-done.12.refs_3_ = bf16[128,256]{1,0:T(8,128)(2,1)S(1)} collective-permute-done((bf16[128,256]{1,0:T(8,128)(2,1)S(1)}, bf16[128,256]{1,0:T(8,128)(2,1)S(1)}, u32[]{:S(2)}, u32[]{:S(2)}) %collective-permute-start.12) | collective-permute-done | bytes 65568 | tf_op jit(solution)/shard_map/ppermute | solution.py:329
  40.4 1.1 %shard_map.95.refs_3_.refs_0_.update = bf16[512,512]{1,0:T(8,128)(2,1)S(1)} custom-call(bf16[2,512,256]{2,1,0:T(8,128)(2,1)S(1)} %get-tuple-element.40.refs_0_, f32[2,256,256]{2,1,0:T(8,128)S(1)} %copy-done, bf16[128,256]{1,0:T(8,128)(2,1)S(1)} %shard_map.93.refs_2_, bf16[128,256]{1,0:T(8,128)(2,1)S(1)} %collective-permute-done.12.refs_3_, ...), custom_call_target="tpu_custom_call" | custom-call | flops 1 | bytes 1 | tf_op jit(solution)/shard_map/pallas_call | solution.py:70
  41.5 0.0 collective-permute-done.15.refs_1_
  41.5 0.2 collective-permute-done.16.refs_1_
  41.7 0.3 collective-permute-start.17
  42.0 0.2 shard_map.99.total
  42.3 4.5 %collective-permute-done.17.project = bf16[256,256]{1,0:T(8,128)(2,1)S(1)} collective-permute-done((bf16[256,256]{1,0:T(8,128)(2,1)S(1)}, bf16[256,256]{1,0:T(8,128)(2,1)S(1)}, u32[]{:S(2)}, u32[]{:S(2)}) %collective-permute-start.17) | collective-permute-done | bytes 131104 | tf_op jit(solution)/shard_map/ppermute | solution.py:333
  46.8 1.0 %shard_map.100 = bf16[512,256]{1,0:T(8,128)(2,1)} custom-call(f32[512,256]{1,0:T(8,128)S(1)} %shard_map.99.total, bf16[512,512]{1,0:T(8,128)(2,1)S(1)} %shard_map.95.refs_3_.refs_0_.update, bf16[256,256]{1,0:T(8,128)(2,1)S(1)} %collective-permute-done.17.project), custom_call_target="tpu_custom_call" | custom-call | flops 1 | bytes 1 | tf_op jit(solution)/shard_map/pallas_call | solution.py:271
  (9 shorter events, 0.2 us)
Async XLA Ops:
  3.3 5.0 %collective-permute-start.2 = (bf16[512,256]{1,0:T(8,128)(2,1)S(1)}, bf16[512,256]{1,0:T(8,128)(2,1)S(1)}, u32[]{:S(2)}, u32[]{:S(2)}) collective-permute-start(bf16[512,256]{1,0:T(8,128)(2,1)S(1)} %get-tuple-element.52), channel_id=1, source_target_pairs={{0,1},{1,0},{2,3},{3,2},{4,5},{5,4},{6,7},{7,6},{8,9},{9,8},{10,11... | collective-permute-start | bytes 786440 | tf_op jit(solution)/shard_map/ppermute | solution.py:326
  5.2 4.8 %collective-permute-start.1 = (bf16[512,256]{1,0:T(8,128)(2,1)S(1)}, bf16[512,256]{1,0:T(8,128)(2,1)S(1)}, u32[]{:S(2)}, u32[]{:S(2)}) collective-permute-start(bf16[512,256]{1,0:T(8,128)(2,1)S(1)} %get-tuple-element.51), channel_id=1, source_target_pairs={{0,1},{1,0},{2,3},{3,2},{4,5},{5,4},{6,7},{7,6},{8,9},{9,8},{10,11... | collective-permute-start | bytes 786440 | tf_op jit(solution)/shard_map/ppermute | solution.py:326
  5.3 7.8 %collective-permute-start = (bf16[320,256]{1,0:T(8,128)(2,1)S(1)}, bf16[320,256]{1,0:T(8,128)(2,1)S(1)}, u32[]{:S(2)}, u32[]{:S(2)}) collective-permute-start(bf16[320,256]{1,0:T(8,128)(2,1)S(1)} %get-tuple-element.43), channel_id=1, source_target_pairs={{0,8},{1,17},{2,10},{3,19},{4,12},{5,21},{6,14},{7,23},{8,0},{9,25... | collective-permute-start | bytes 491528 | tf_op jit(solution)/shard_map/ppermute | solution.py:333
  8.4 9.2 %collective-permute-start.5 = (bf16[512,256]{1,0:T(8,128)(2,1)S(1)}, bf16[512,256]{1,0:T(8,128)(2,1)S(1)}, u32[]{:S(2)}, u32[]{:S(2)}) collective-permute-start(bf16[512,256]{1,0:T(8,128)(2,1)S(1)} %shard_map.85.refs_3_), channel_id=1, source_target_pairs={{0,2},{1,5},{2,0},{3,7},{4,6},{5,1},{6,4},{7,3},{8,10},{9,13},{10,... | collective-permute-start | bytes 786440 | tf_op jit(solution)/shard_map/ppermute | solution.py:329
  10.0 7.6 %collective-permute-start.7 = (bf16[512,256]{1,0:T(8,128)(2,1)S(1)}, bf16[512,256]{1,0:T(8,128)(2,1)S(1)}, u32[]{:S(2)}, u32[]{:S(2)}) collective-permute-start(bf16[512,256]{1,0:T(8,128)(2,1)S(1)} %shard_map.86.refs_5_), channel_id=1, source_target_pairs={{0,2},{1,5},{2,0},{3,7},{4,6},{5,1},{6,4},{7,3},{8,10},{9,13},{10,... | collective-permute-start | bytes 786440 | tf_op jit(solution)/shard_map/ppermute | solution.py:329
  12.0 5.7 %collective-permute-start.6 = (bf16[512,256]{1,0:T(8,128)(2,1)S(1)}, bf16[512,256]{1,0:T(8,128)(2,1)S(1)}, u32[]{:S(2)}, u32[]{:S(2)}) collective-permute-start(bf16[512,256]{1,0:T(8,128)(2,1)S(1)} %get-tuple-element.59), channel_id=1, source_target_pairs={{0,1},{1,0},{2,3},{3,2},{4,5},{5,4},{6,7},{7,6},{8,9},{9,8},{10,11... | collective-permute-start | bytes 786440 | tf_op jit(solution)/shard_map/ppermute | solution.py:326
  12.2 5.4 %collective-permute-start.4 = (bf16[512,256]{1,0:T(8,128)(2,1)S(1)}, bf16[512,256]{1,0:T(8,128)(2,1)S(1)}, u32[]{:S(2)}, u32[]{:S(2)}) collective-permute-start(bf16[512,256]{1,0:T(8,128)(2,1)S(1)} %get-tuple-element.53.refs_3_.refs_5_), channel_id=1, source_target_pairs={{0,1},{1,0},{2,3},{3,2},{4,5},{5,4},{6,7},{7,6},{8,9},{9,8},{10,11... | collective-permute-start | bytes 786440 | tf_op jit(solution)/shard_map/ppermute | solution.py:326
  13.1 6.5 %collective-permute-start.3 = (bf16[320,256]{1,0:T(8,128)(2,1)S(1)}, bf16[320,256]{1,0:T(8,128)(2,1)S(1)}, u32[]{:S(2)}, u32[]{:S(2)}) collective-permute-start(bf16[320,256]{1,0:T(8,128)(2,1)S(1)} %get-tuple-element.56), channel_id=1, source_target_pairs={{0,16},{1,9},{2,18},{3,11},{4,20},{5,13},{6,22},{7,15},{8,24},{9,1... | collective-permute-start | bytes 491528 | tf_op jit(solution)/shard_map/ppermute | solution.py:333
  17.6 22.7 %copy-start = (f32[2,256,256]{2,1,0:T(8,128)S(1)}, f32[2,256,256]{2,1,0:T(8,128)}, u32[]{:S(2)}) copy-start(f32[2,256,256]{2,1,0:T(8,128)} %refs_1_.3) | copy-start | bytes 1572868
  17.8 6.4 %collective-permute-start.11 = (bf16[512,256]{1,0:T(8,128)(2,1)S(1)}, bf16[512,256]{1,0:T(8,128)(2,1)S(1)}, u32[]{:S(2)}, u32[]{:S(2)}) collective-permute-start(bf16[512,256]{1,0:T(8,128)(2,1)S(1)} %get-tuple-element.60.refs_3_), channel_id=1, source_target_pairs={{0,4},{1,3},{2,6},{3,1},{4,0},{5,7},{6,2},{7,5},{8,12},{9,11},{10,... | collective-permute-start | bytes 786440 | tf_op jit(solution)/shard_map/ppermute | solution.py:329
  19.7 1.6 %collective-permute-start.9 = (bf16[384,256]{1,0:T(8,128)(2,1)S(1)}, bf16[384,256]{1,0:T(8,128)(2,1)S(1)}, u32[]{:S(2)}, u32[]{:S(2)}) collective-permute-start(bf16[384,256]{1,0:T(8,128)(2,1)S(1)} %get-tuple-element.63), channel_id=1, source_target_pairs={{0,1},{1,0},{2,3},{3,2},{4,5},{5,4},{6,7},{7,6},{8,9},{9,8},{10,11... | collective-permute-start | bytes 589832 | tf_op jit(solution)/shard_map/ppermute | solution.py:326
  19.9 1.4 %collective-permute-start.10 = (bf16[128,256]{1,0:T(8,128)(2,1)S(1)}, bf16[128,256]{1,0:T(8,128)(2,1)S(1)}, u32[]{:S(2)}, u32[]{:S(2)}) collective-permute-start(bf16[128,256]{1,0:T(8,128)(2,1)S(1)} %get-tuple-element.64), channel_id=1, source_target_pairs={{0,1},{1,0},{2,3},{3,2},{4,5},{5,4},{6,7},{7,6},{8,9},{9,8},{10,11... | collective-permute-start | bytes 196616 | tf_op jit(solution)/shard_map/ppermute | solution.py:326
  24.6 8.3 %collective-permute-start.14 = (bf16[256,256]{1,0:T(8,128)(2,1)S(1)}, bf16[256,256]{1,0:T(8,128)(2,1)S(1)}, u32[]{:S(2)}, u32[]{:S(2)}) collective-permute-start(bf16[256,256]{1,0:T(8,128)(2,1)S(1)} %get-tuple-element.71), channel_id=1, source_target_pairs={{0,16},{1,17},{2,18},{3,19},{4,20},{5,21},{6,22},{7,23},{8,24},{9,... | collective-permute-start | bytes 393224 | tf_op jit(solution)/shard_map/ppermute | solution.py:333
  27.3 6.1 %collective-permute-start.13 = (bf16[256,256]{1,0:T(8,128)(2,1)S(1)}, bf16[256,256]{1,0:T(8,128)(2,1)S(1)}, u32[]{:S(2)}, u32[]{:S(2)}) collective-permute-start(bf16[256,256]{1,0:T(8,128)(2,1)S(1)} %get-tuple-element.67.refs_2_), channel_id=1, source_target_pairs={{0,8},{1,9},{2,10},{3,11},{4,12},{5,13},{6,14},{7,15},{8,0},{9,1},... | collective-permute-start | bytes 393224 | tf_op jit(solution)/shard_map/ppermute | solution.py:333
  27.7 3.9 %collective-permute-start.8 = (bf16[64,256]{1,0:T(8,128)(2,1)S(1)}, bf16[64,256]{1,0:T(8,128)(2,1)S(1)}, u32[]{:S(2)}, u32[]{:S(2)}) collective-permute-start(bf16[64,256]{1,0:T(8,128)(2,1)S(1)} %get-tuple-element.61.refs_0_), channel_id=1, source_target_pairs={{0,2},{1,5},{2,0},{3,7},{4,6},{5,1},{6,4},{7,3},{8,10},{9,13},{10,... | collective-permute-start | bytes 98312 | tf_op jit(solution)/shard_map/ppermute | solution.py:329
  33.0 8.5 %collective-permute-start.15 = (bf16[256,256]{1,0:T(8,128)(2,1)S(1)}, bf16[256,256]{1,0:T(8,128)(2,1)S(1)}, u32[]{:S(2)}, u32[]{:S(2)}) collective-permute-start(bf16[256,256]{1,0:T(8,128)(2,1)S(1)} %get-tuple-element.73), channel_id=1, source_target_pairs={{0,8},{1,9},{2,10},{3,11},{4,12},{5,13},{6,14},{7,15},{8,0},{9,1},... | collective-permute-start | bytes 393224 | tf_op jit(solution)/shard_map/ppermute | solution.py:333
  33.4 8.3 %collective-permute-start.16 = (bf16[256,256]{1,0:T(8,128)(2,1)S(1)}, bf16[256,256]{1,0:T(8,128)(2,1)S(1)}, u32[]{:S(2)}, u32[]{:S(2)}) collective-permute-start(bf16[256,256]{1,0:T(8,128)(2,1)S(1)} %get-tuple-element.69.refs_4_), channel_id=1, source_target_pairs={{0,16},{1,17},{2,18},{3,19},{4,20},{5,21},{6,22},{7,23},{8,24},{9,... | collective-permute-start | bytes 393224 | tf_op jit(solution)/shard_map/ppermute | solution.py:333
  36.1 4.3 %collective-permute-start.12 = (bf16[128,256]{1,0:T(8,128)(2,1)S(1)}, bf16[128,256]{1,0:T(8,128)(2,1)S(1)}, u32[]{:S(2)}, u32[]{:S(2)}) collective-permute-start(bf16[128,256]{1,0:T(8,128)(2,1)S(1)} %shard_map.93.refs_2_), channel_id=1, source_target_pairs={{0,4},{1,3},{2,6},{3,1},{4,0},{5,7},{6,2},{7,5},{8,12},{9,11},{10,... | collective-permute-start | bytes 196616 | tf_op jit(solution)/shard_map/ppermute | solution.py:329
  41.7 5.0 %collective-permute-start.17 = (bf16[256,256]{1,0:T(8,128)(2,1)S(1)}, bf16[256,256]{1,0:T(8,128)(2,1)S(1)}, u32[]{:S(2)}, u32[]{:S(2)}) collective-permute-start(bf16[256,256]{1,0:T(8,128)(2,1)S(1)} %shard_map.98.refs_2_), channel_id=1, source_target_pairs={{0,8},{1,9},{2,10},{3,11},{4,12},{5,13},{6,14},{7,15},{8,0},{9,1},... | collective-permute-start | bytes 393224 | tf_op jit(solution)/shard_map/ppermute | solution.py:333

commit v5 on v4

--- a/solution.py
+++ b/solution.py
@@ -55,7 +55,7 @@
     return value
 
 
-def local(fn, outs, values, after=()):
+def local(fn, outs, values, after=(), cost=1):
     outs = [jax.ShapeDtypeStruct(shape, dtype) for shape, dtype in outs]
     if any(v.shape[-1] % 128 or v.shape[-2] % 16 for v in list(values) + outs):
         return list(fn(*values))
@@ -74,7 +74,7 @@
             out_specs=[pl.BlockSpec(memory_space=pltpu.VMEM)] * len(outs),
             out_shape=[pltpu.VMEM(o.shape, o.dtype) for o in outs],
             compiler_params=pltpu.CompilerParams(vmem_limit_bytes=16 * MIB),
-            cost_estimate=pl.CostEstimate(flops=1, bytes_accessed=1, transcendentals=0),
+            cost_estimate=pl.CostEstimate(flops=cost, bytes_accessed=1, transcendentals=0),
         )(*[pltpu.with_memory_space_constraint(v, pltpu.VMEM) for v in values], *after)
     )
 
@@ -411,7 +411,8 @@
                 next_panel,
                 [((rows // 2, panel_width), BF), ((near + rows // 2, panel_width), BF), ((near, panel_width), F32)],
                 [kept, correlation, panel_got],
-                after=(other_kept[0],),
+                after=(sent[-1],),
+                cost=5000000000,
             )
     panel_places = [[source_codes(order).index(code) for code in range(n_row)] for order in row_orders]
 
@@ -512,6 +513,7 @@
         [((rows, wide), BF)],
         [vectors, panel_factors, correlation, other_correlation],
         after=(message,),
+        cost=1000000000,
     )
 
     for stage in range(1, row_stages):
@@ -531,7 +533,6 @@
         lambda project, got: [(project + got.astype(F32)).astype(BF)],
         [((summed, width), BF)],
         [project, project_got],
-        after=(cyclic, update),
     )
     (total,) = local(
         lambda update, cyclic, project: [
@@ -539,6 +540,7 @@
         ],
         [((rows, width), F32)],
         [update, cyclic, project],
+        cost=1000000000,
     )
     for stage in reversed(range(row_stages - 1)):
         got = swap_row(project, [sum_order[stage]] * 2)

time: 47.9 us -> 45.7 us (0.954)
  starting transfers between devices: 20.4 us -> 19.1 us
  waiting for transfers between devices: 16.7 us -> 15.9 us
    ppermute x5, waiting for transfers between devices: 8.91 us -> 6.16 us  [swap_col(): lax.ppermute(value, 'col', [(i, i ^ 1 << col_orders[i % 2][stage]) for i...]
    ppermute x7, waiting for transfers between devices: 6.8 us -> 8.69 us  [swap_row(): return lax.ppermute(value, ('row', 'col'), pairs)]
    ppermute x7, starting transfers between devices: 11.8 us -> 10.5 us  [swap_row(): return lax.ppermute(value, ('row', 'col'), pairs)]
  transfers between devices with their start and end apart: 18 -> 18, of which waited for: 10 -> 10; matrix products, arithmetic and copies ran while one was open for 0% -> 0% of each run, Pallas kernels for 12% -> 13%
where the time goes in v5:
time: 45.7 us; the launch traced here: 45.6 us
  starting transfers between devices  19.1 us (42%)
  waiting for transfers between devices  15.9 us (35%)
  Pallas kernels  10.5 us (23%)
    ppermute x7, starting transfers between devices, swap_row(): return lax.ppermute(value, ('row', 'col'), pairs)  10.5 us
    ppermute x7, waiting for transfers between devices, swap_row(): return lax.ppermute(value, ('row', 'col'), pairs)  8.69 us
    ppermute x5, starting transfers between devices, swap_col(): lax.ppermute(value, 'col', [(i, i ^ 1 << col_orders[i % 2][stage]) for i...  6.77 us
    ppermute x5, waiting for transfers between devices, swap_col(): lax.ppermute(value, 'col', [(i, i ^ 1 << col_orders[i % 2][stage]) for i...  6.16 us
    pallas_call x4, Pallas kernels, products(): pl.pallas_call(functools.partial(product_kernel, plan, width, chunks, pol...  5.48 us
    pallas_call x13, Pallas kernels, local(): pl.pallas_call(kernel, in_specs=[pl.BlockSpec(memory_space=pltpu.VMEM)] *...  2.16 us
    pallas_call x1, Pallas kernels, panel_blocks(): pl.pallas_call(functools.partial(panel_kernel, row_codes, row_orders, blo...  1.87 us
    ppermute x6, starting transfers between devices, swap_cores(): return lax.ppermute(value, 'col', [(i, i ^ 1) for i in range(n_col)])  1.79 us
  transfers between devices with their start and end apart: 18, of which 10 were waited for; matrix products, arithmetic and copies ran while one was open for 0% of the time, Pallas kernels for 13%

profile of v5, /device:TPU:0, one launch (start us, length us, event | category | flops | bytes accessed | tf_op | source)
XLA Modules:
  0.0 45.6 jit_solution(4308469962182296890)
XLA Ops:
  0.0 1.9 %shard_map.82 = (bf16[2,512,256]{2,1,0:T(8,128)(2,1)S(1)}, bf16[256,256]{1,0:T(8,128)(2,1)S(1)}, bf16[320,256]{1,0:T(8,128)(2,1)S(1)}, f32[64,256]{1,0:T(8,128)S...) custom-call(bf16[512,2048]{1,0:T(8,128)(2,1)} %refs_0_.1, ...), custom_call_target="tpu_custom_call" | custom-call | flops 1 | bytes 1 | tf_op jit(solution)/shard_map/pallas_call | solution.py:225
  1.9 1.4 %shard_map.83 = (bf16[512,256]{1,0:T(8,128)(2,1)S(1)}, bf16[512,256]{1,0:T(8,128)(2,1)S(1)}) custom-call(bf16[512,2048]{1,0:T(8,128)(2,1)S(1)} %get-tuple-element.44.refs_0_, f32[1,2048]{1,0:T(1,128)S(1)} %get-tuple-element.45.refs_1_, f32[1,2048]{1,0:T(1,128)S(1)} %get-tuple-element.46.refs_2_, f32[1,2048]{1,0:T(1,128)S(1)} %get-tuple-element.47.refs_3_, ...), custom_call_target="tpu_custom_call" | custom-call | flops 1 | bytes 1 | tf_op jit(solution)/shard_map/pallas_call | solution.py:140
  3.3 0.5 %collective-permute-start.2 = (bf16[512,256]{1,0:T(8,128)(2,1)S(1)}, bf16[512,256]{1,0:T(8,128)(2,1)S(1)}, u32[]{:S(2)}, u32[]{:S(2)}) collective-permute-start(bf16[512,256]{1,0:T(8,128)(2,1)S(1)} %get-tuple-element.52), channel_id=1, source_target_pairs={{0,1},{1,0},{2,3},{3,2},{4,5},{5,4},{6,7},{7,6},{8,9},{9,8},{10,11... | collective-permute-start | bytes 786440 | tf_op jit(solution)/shard_map/ppermute | solution.py:326
  3.8 1.4 %shard_map.84 = (bf16[512,256]{1,0:T(8,128)(2,1)S(1)}, bf16[512,256]{1,0:T(8,128)(2,1)S(1)}) custom-call(bf16[512,2048]{1,0:T(8,128)(2,1)S(1)} %get-tuple-element.44.refs_0_, f32[1,2048]{1,0:T(1,128)S(1)} %get-tuple-element.45.refs_1_, f32[1,2048]{1,0:T(1,128)S(1)} %get-tuple-element.46.refs_2_, f32[1,2048]{1,0:T(1,128)S(1)} %get-tuple-element.47.refs_3_, ...), custom_call_target="tpu_custom_call" | custom-call | flops 1 | bytes 1 | tf_op jit(solution)/shard_map/pallas_call | solution.py:140
  5.2 0.1 collective-permute-start.1
  5.3 3.0 %collective-permute-start = (bf16[320,256]{1,0:T(8,128)(2,1)S(1)}, bf16[320,256]{1,0:T(8,128)(2,1)S(1)}, u32[]{:S(2)}, u32[]{:S(2)}) collective-permute-start(bf16[320,256]{1,0:T(8,128)(2,1)S(1)} %get-tuple-element.43), channel_id=1, source_target_pairs={{0,8},{1,17},{2,10},{3,19},{4,12},{5,21},{6,14},{7,23},{8,0},{9,25... | collective-permute-start | bytes 491528 | tf_op jit(solution)/shard_map/ppermute | solution.py:333
  8.3 0.0 collective-permute-done.2.refs_1_
  8.3 0.1 shard_map.85.refs_3_
  8.4 1.6 %collective-permute-start.5 = (bf16[512,256]{1,0:T(8,128)(2,1)S(1)}, bf16[512,256]{1,0:T(8,128)(2,1)S(1)}, u32[]{:S(2)}, u32[]{:S(2)}) collective-permute-start(bf16[512,256]{1,0:T(8,128)(2,1)S(1)} %shard_map.85.refs_3_), channel_id=1, source_target_pairs={{0,2},{1,5},{2,0},{3,7},{4,6},{5,1},{6,4},{7,3},{8,10},{9,13},{10,... | collective-permute-start | bytes 786440 | tf_op jit(solution)/shard_map/ppermute | solution.py:329
  9.9 0.0 collective-permute-done.1.refs_1_
  9.9 0.1 shard_map.86.refs_3_.refs_5_
  10.0 0.6 %collective-permute-start.7 = (bf16[512,256]{1,0:T(8,128)(2,1)S(1)}, bf16[512,256]{1,0:T(8,128)(2,1)S(1)}, u32[]{:S(2)}, u32[]{:S(2)}) collective-permute-start(bf16[512,256]{1,0:T(8,128)(2,1)S(1)} %shard_map.86.refs_3_.refs_5_), channel_id=1, source_target_pairs={{0,2},{1,5},{2,0},{3,7},{4,6},{5,1},{6,4},{7,3},{8,10},{9,13},{10,... | collective-permute-start | bytes 786440 | tf_op jit(solution)/shard_map/ppermute | solution.py:329
  10.6 1.4 %shard_map.88 = (bf16[512,256]{1,0:T(8,128)(2,1)S(1)}, bf16[512,256]{1,0:T(8,128)(2,1)S(1)}) custom-call(bf16[512,2048]{1,0:T(8,128)(2,1)S(1)} %get-tuple-element.44.refs_0_, f32[1,2048]{1,0:T(1,128)S(1)} %get-tuple-element.45.refs_1_, f32[1,2048]{1,0:T(1,128)S(1)} %get-tuple-element.46.refs_2_, f32[1,2048]{1,0:T(1,128)S(1)} %get-tuple-element.47.refs_3_, ...), custom_call_target="tpu_custom_call" | custom-call | flops 1 | bytes 1 | tf_op jit(solution)/shard_map/pallas_call | solution.py:140
  12.0 0.3 collective-permute-start.6
  12.2 0.3 collective-permute-start.4
  12.5 0.6 %collective-permute-done.refs_2_ = bf16[320,256]{1,0:T(8,128)(2,1)S(1)} collective-permute-done((bf16[320,256]{1,0:T(8,128)(2,1)S(1)}, bf16[320,256]{1,0:T(8,128)(2,1)S(1)}, u32[]{:S(2)}, u32[]{:S(2)}) %collective-permute-start) | collective-permute-done | bytes 163872 | tf_op jit(solution)/shard_map/ppermute | solution.py:333
  13.1 2.4 %collective-permute-start.3 = (bf16[320,256]{1,0:T(8,128)(2,1)S(1)}, bf16[320,256]{1,0:T(8,128)(2,1)S(1)}, u32[]{:S(2)}, u32[]{:S(2)}) collective-permute-start(bf16[320,256]{1,0:T(8,128)(2,1)S(1)} %get-tuple-element.55), channel_id=1, source_target_pairs={{0,16},{1,9},{2,18},{3,11},{4,20},{5,13},{6,22},{7,15},{8,24},{9,1... | collective-permute-start | bytes 491528 | tf_op jit(solution)/shard_map/ppermute | solution.py:333
  15.5 1.4 %shard_map.89 = (bf16[512,256]{1,0:T(8,128)(2,1)S(1)}, bf16[512,256]{1,0:T(8,128)(2,1)S(1)}) custom-call(bf16[512,2048]{1,0:T(8,128)(2,1)S(1)} %get-tuple-element.44.refs_0_, f32[1,2048]{1,0:T(1,128)S(1)} %get-tuple-element.45.refs_1_, f32[1,2048]{1,0:T(1,128)S(1)} %get-tuple-element.46.refs_2_, f32[1,2048]{1,0:T(1,128)S(1)} %get-tuple-element.47.refs_3_, ...), custom_call_target="tpu_custom_call" | custom-call | flops 1 | bytes 1 | tf_op jit(solution)/shard_map/pallas_call | solution.py:140
  16.9 0.7 %collective-permute-done.7.refs_5_ = bf16[512,256]{1,0:T(8,128)(2,1)S(1)} collective-permute-done((bf16[512,256]{1,0:T(8,128)(2,1)S(1)}, bf16[512,256]{1,0:T(8,128)(2,1)S(1)}, u32[]{:S(2)}, u32[]{:S(2)}) %collective-permute-start.7) | collective-permute-done | bytes 262176 | tf_op jit(solution)/shard_map/ppermute | solution.py:329
  17.6 0.0 collective-permute-done.5.refs_2_
  17.6 0.0 collective-permute-done.6.refs_4_
  17.6 0.0 collective-permute-done.4.refs_1_
  17.6 0.2 shard_map.90
  17.8 0.0 copy-start
  17.8 1.6 %collective-permute-start.11 = (bf16[512,256]{1,0:T(8,128)(2,1)S(1)}, bf16[512,256]{1,0:T(8,128)(2,1)S(1)}, u32[]{:S(2)}, u32[]{:S(2)}) collective-permute-start(bf16[512,256]{1,0:T(8,128)(2,1)S(1)} %get-tuple-element.60.refs_3_), channel_id=1, source_target_pairs={{0,4},{1,3},{2,6},{3,1},{4,0},{5,7},{6,2},{7,5},{8,12},{9,11},{10,... | collective-permute-start | bytes 786440 | tf_op jit(solution)/shard_map/ppermute | solution.py:329
  19.4 0.2 collective-permute-done.3.refs_2_
  19.7 0.2 collective-permute-start.9
  19.9 0.4 collective-permute-start.10
  20.2 1.0 %collective-permute-done.10.refs_2_ = bf16[128,256]{1,0:T(8,128)(2,1)S(1)} collective-permute-done((bf16[128,256]{1,0:T(8,128)(2,1)S(1)}, bf16[128,256]{1,0:T(8,128)(2,1)S(1)}, u32[]{:S(2)}, u32[]{:S(2)}) %collective-permute-start.10) | collective-permute-done | bytes 65568 | tf_op jit(solution)/shard_map/ppermute | solution.py:326
  21.3 3.0 %collective-permute-done.11.refs_5_ = bf16[512,256]{1,0:T(8,128)(2,1)S(1)} collective-permute-done((bf16[512,256]{1,0:T(8,128)(2,1)S(1)}, bf16[512,256]{1,0:T(8,128)(2,1)S(1)}, u32[]{:S(2)}, u32[]{:S(2)}) %collective-permute-start.11) | collective-permute-done | bytes 262176 | tf_op jit(solution)/shard_map/ppermute | solution.py:329
  24.3 0.3 shard_map.92
  24.6 1.9 %collective-permute-start.13 = (bf16[256,256]{1,0:T(8,128)(2,1)S(1)}, bf16[256,256]{1,0:T(8,128)(2,1)S(1)}, u32[]{:S(2)}, u32[]{:S(2)}) collective-permute-start(bf16[256,256]{1,0:T(8,128)(2,1)S(1)} %get-tuple-element.67.refs_2_), channel_id=1, source_target_pairs={{0,8},{1,9},{2,10},{3,11},{4,12},{5,13},{6,14},{7,15},{8,0},{9,1},... | collective-permute-start | bytes 393224 | tf_op jit(solution)/shard_map/ppermute | solution.py:333
  26.5 1.2 %collective-permute-start.14 = (bf16[256,256]{1,0:T(8,128)(2,1)S(1)}, bf16[256,256]{1,0:T(8,128)(2,1)S(1)}, u32[]{:S(2)}, u32[]{:S(2)}) collective-permute-start(bf16[256,256]{1,0:T(8,128)(2,1)S(1)} %get-tuple-element.71), channel_id=1, source_target_pairs={{0,16},{1,17},{2,18},{3,19},{4,20},{5,21},{6,22},{7,23},{8,24},{9,... | collective-permute-start | bytes 393224 | tf_op jit(solution)/shard_map/ppermute | solution.py:333
  27.7 1.5 %collective-permute-start.8 = (bf16[64,256]{1,0:T(8,128)(2,1)S(1)}, bf16[64,256]{1,0:T(8,128)(2,1)S(1)}, u32[]{:S(2)}, u32[]{:S(2)}) collective-permute-start(bf16[64,256]{1,0:T(8,128)(2,1)S(1)} %get-tuple-element.61.refs_0_), channel_id=1, source_target_pairs={{0,2},{1,5},{2,0},{3,7},{4,6},{5,1},{6,4},{7,3},{8,10},{9,13},{10,... | collective-permute-start | bytes 98312 | tf_op jit(solution)/shard_map/ppermute | solution.py:329
  29.2 2.4 %collective-permute-done.8.refs_1_ = bf16[64,256]{1,0:T(8,128)(2,1)S(1)} collective-permute-done((bf16[64,256]{1,0:T(8,128)(2,1)S(1)}, bf16[64,256]{1,0:T(8,128)(2,1)S(1)}, u32[]{:S(2)}, u32[]{:S(2)}) %collective-permute-start.8) | collective-permute-done | bytes 32800 | tf_op jit(solution)/shard_map/ppermute | solution.py:329
  31.6 0.0 collective-permute-done.13.refs_1_
  31.7 1.8 %collective-permute-start.16 = (bf16[256,256]{1,0:T(8,128)(2,1)S(1)}, bf16[256,256]{1,0:T(8,128)(2,1)S(1)}, u32[]{:S(2)}, u32[]{:S(2)}) collective-permute-start(bf16[256,256]{1,0:T(8,128)(2,1)S(1)} %get-tuple-element.69.refs_4_), channel_id=1, source_target_pairs={{0,16},{1,17},{2,18},{3,19},{4,20},{5,21},{6,22},{7,23},{8,24},{9,... | collective-permute-start | bytes 393224 | tf_op jit(solution)/shard_map/ppermute | solution.py:333
  33.5 1.5 %collective-permute-start.12 = (bf16[128,256]{1,0:T(8,128)(2,1)S(1)}, bf16[128,256]{1,0:T(8,128)(2,1)S(1)}, u32[]{:S(2)}, u32[]{:S(2)}) collective-permute-start(bf16[128,256]{1,0:T(8,128)(2,1)S(1)} %shard_map.93.refs_2_), channel_id=1, source_target_pairs={{0,4},{1,3},{2,6},{3,1},{4,0},{5,7},{6,2},{7,5},{8,12},{9,11},{10,... | collective-permute-start | bytes 196616 | tf_op jit(solution)/shard_map/ppermute | solution.py:329
  35.0 0.9 %collective-permute-done.14.refs_1_ = bf16[256,256]{1,0:T(8,128)(2,1)S(1)} collective-permute-done((bf16[256,256]{1,0:T(8,128)(2,1)S(1)}, bf16[256,256]{1,0:T(8,128)(2,1)S(1)}, u32[]{:S(2)}, u32[]{:S(2)}) %collective-permute-start.14) | collective-permute-done | bytes 131104 | tf_op jit(solution)/shard_map/ppermute | solution.py:333
  35.9 0.1 collective-permute-start.15
  36.1 3.5 %collective-permute-done.16.refs_1_ = bf16[256,256]{1,0:T(8,128)(2,1)S(1)} collective-permute-done((bf16[256,256]{1,0:T(8,128)(2,1)S(1)}, bf16[256,256]{1,0:T(8,128)(2,1)S(1)}, u32[]{:S(2)}, u32[]{:S(2)}) %collective-permute-start.16) | collective-permute-done | bytes 131104 | tf_op jit(solution)/shard_map/ppermute | solution.py:333
  39.6 0.1 collective-permute-start.17
  39.7 0.0 collective-permute-done.12.refs_3_
  39.7 1.1 %shard_map.95.refs_0_.update = bf16[512,512]{1,0:T(8,128)(2,1)S(1)} custom-call(bf16[2,512,256]{2,1,0:T(8,128)(2,1)S(1)} %get-tuple-element.40.refs_0_, f32[2,256,256]{2,1,0:T(8,128)S(1)} %copy-done, bf16[128,256]{1,0:T(8,128)(2,1)S(1)} %shard_map.93.refs_2_, bf16[128,256]{1,0:T(8,128)(2,1)S(1)} %collective-permute-done.12.refs_3_, ...), custom_call_target="tpu_custom_call" | custom-call | flops 1000000000 | bytes 1 | tf_op jit(solution)/shard_map/pallas_call | solution.py:70
  40.8 1.3 %collective-permute-done.15.refs_1_ = bf16[256,256]{1,0:T(8,128)(2,1)S(1)} collective-permute-done((bf16[256,256]{1,0:T(8,128)(2,1)S(1)}, bf16[256,256]{1,0:T(8,128)(2,1)S(1)}, u32[]{:S(2)}, u32[]{:S(2)}) %collective-permute-start.15) | collective-permute-done | bytes 131104 | tf_op jit(solution)/shard_map/ppermute | solution.py:333
  42.1 0.2 shard_map.99.total
  42.3 2.3 %collective-permute-done.17.project = bf16[256,256]{1,0:T(8,128)(2,1)S(1)} collective-permute-done((bf16[256,256]{1,0:T(8,128)(2,1)S(1)}, bf16[256,256]{1,0:T(8,128)(2,1)S(1)}, u32[]{:S(2)}, u32[]{:S(2)}) %collective-permute-start.17) | collective-permute-done | bytes 131104 | tf_op jit(solution)/shard_map/ppermute | solution.py:333
  44.6 1.0 %shard_map.100 = bf16[512,256]{1,0:T(8,128)(2,1)} custom-call(f32[512,256]{1,0:T(8,128)S(1)} %shard_map.99.total, bf16[512,512]{1,0:T(8,128)(2,1)S(1)} %shard_map.95.refs_0_.update, bf16[256,256]{1,0:T(8,128)(2,1)S(1)} %collective-permute-done.17.project), custom_call_target="tpu_custom_call" | custom-call | flops 1 | bytes 1 | tf_op jit(solution)/shard_map/pallas_call | solution.py:271
  (9 shorter events, 0.2 us)
Async XLA Ops:
  3.3 5.0 %collective-permute-start.2 = (bf16[512,256]{1,0:T(8,128)(2,1)S(1)}, bf16[512,256]{1,0:T(8,128)(2,1)S(1)}, u32[]{:S(2)}, u32[]{:S(2)}) collective-permute-start(bf16[512,256]{1,0:T(8,128)(2,1)S(1)} %get-tuple-element.52), channel_id=1, source_target_pairs={{0,1},{1,0},{2,3},{3,2},{4,5},{5,4},{6,7},{7,6},{8,9},{9,8},{10,11... | collective-permute-start | bytes 786440 | tf_op jit(solution)/shard_map/ppermute | solution.py:326
  5.2 4.8 %collective-permute-start.1 = (bf16[512,256]{1,0:T(8,128)(2,1)S(1)}, bf16[512,256]{1,0:T(8,128)(2,1)S(1)}, u32[]{:S(2)}, u32[]{:S(2)}) collective-permute-start(bf16[512,256]{1,0:T(8,128)(2,1)S(1)} %get-tuple-element.51), channel_id=1, source_target_pairs={{0,1},{1,0},{2,3},{3,2},{4,5},{5,4},{6,7},{7,6},{8,9},{9,8},{10,11... | collective-permute-start | bytes 786440 | tf_op jit(solution)/shard_map/ppermute | solution.py:326
  5.3 7.8 %collective-permute-start = (bf16[320,256]{1,0:T(8,128)(2,1)S(1)}, bf16[320,256]{1,0:T(8,128)(2,1)S(1)}, u32[]{:S(2)}, u32[]{:S(2)}) collective-permute-start(bf16[320,256]{1,0:T(8,128)(2,1)S(1)} %get-tuple-element.43), channel_id=1, source_target_pairs={{0,8},{1,17},{2,10},{3,19},{4,12},{5,21},{6,14},{7,23},{8,0},{9,25... | collective-permute-start | bytes 491528 | tf_op jit(solution)/shard_map/ppermute | solution.py:333
  8.4 9.2 %collective-permute-start.5 = (bf16[512,256]{1,0:T(8,128)(2,1)S(1)}, bf16[512,256]{1,0:T(8,128)(2,1)S(1)}, u32[]{:S(2)}, u32[]{:S(2)}) collective-permute-start(bf16[512,256]{1,0:T(8,128)(2,1)S(1)} %shard_map.85.refs_3_), channel_id=1, source_target_pairs={{0,2},{1,5},{2,0},{3,7},{4,6},{5,1},{6,4},{7,3},{8,10},{9,13},{10,... | collective-permute-start | bytes 786440 | tf_op jit(solution)/shard_map/ppermute | solution.py:329
  10.0 7.6 %collective-permute-start.7 = (bf16[512,256]{1,0:T(8,128)(2,1)S(1)}, bf16[512,256]{1,0:T(8,128)(2,1)S(1)}, u32[]{:S(2)}, u32[]{:S(2)}) collective-permute-start(bf16[512,256]{1,0:T(8,128)(2,1)S(1)} %shard_map.86.refs_3_.refs_5_), channel_id=1, source_target_pairs={{0,2},{1,5},{2,0},{3,7},{4,6},{5,1},{6,4},{7,3},{8,10},{9,13},{10,... | collective-permute-start | bytes 786440 | tf_op jit(solution)/shard_map/ppermute | solution.py:329
  12.0 5.7 %collective-permute-start.6 = (bf16[512,256]{1,0:T(8,128)(2,1)S(1)}, bf16[512,256]{1,0:T(8,128)(2,1)S(1)}, u32[]{:S(2)}, u32[]{:S(2)}) collective-permute-start(bf16[512,256]{1,0:T(8,128)(2,1)S(1)} %get-tuple-element.59), channel_id=1, source_target_pairs={{0,1},{1,0},{2,3},{3,2},{4,5},{5,4},{6,7},{7,6},{8,9},{9,8},{10,11... | collective-permute-start | bytes 786440 | tf_op jit(solution)/shard_map/ppermute | solution.py:326
  12.2 5.4 %collective-permute-start.4 = (bf16[512,256]{1,0:T(8,128)(2,1)S(1)}, bf16[512,256]{1,0:T(8,128)(2,1)S(1)}, u32[]{:S(2)}, u32[]{:S(2)}) collective-permute-start(bf16[512,256]{1,0:T(8,128)(2,1)S(1)} %get-tuple-element.56.refs_5_), channel_id=1, source_target_pairs={{0,1},{1,0},{2,3},{3,2},{4,5},{5,4},{6,7},{7,6},{8,9},{9,8},{10,11... | collective-permute-start | bytes 786440 | tf_op jit(solution)/shard_map/ppermute | solution.py:326
  13.1 6.5 %collective-permute-start.3 = (bf16[320,256]{1,0:T(8,128)(2,1)S(1)}, bf16[320,256]{1,0:T(8,128)(2,1)S(1)}, u32[]{:S(2)}, u32[]{:S(2)}) collective-permute-start(bf16[320,256]{1,0:T(8,128)(2,1)S(1)} %get-tuple-element.55), channel_id=1, source_target_pairs={{0,16},{1,9},{2,18},{3,11},{4,20},{5,13},{6,22},{7,15},{8,24},{9,1... | collective-permute-start | bytes 491528 | tf_op jit(solution)/shard_map/ppermute | solution.py:333
  17.8 21.8 %copy-start = (f32[2,256,256]{2,1,0:T(8,128)S(1)}, f32[2,256,256]{2,1,0:T(8,128)}, u32[]{:S(2)}) copy-start(f32[2,256,256]{2,1,0:T(8,128)} %refs_1_.3) | copy-start | bytes 1572868
  17.8 6.4 %collective-permute-start.11 = (bf16[512,256]{1,0:T(8,128)(2,1)S(1)}, bf16[512,256]{1,0:T(8,128)(2,1)S(1)}, u32[]{:S(2)}, u32[]{:S(2)}) collective-permute-start(bf16[512,256]{1,0:T(8,128)(2,1)S(1)} %get-tuple-element.60.refs_3_), channel_id=1, source_target_pairs={{0,4},{1,3},{2,6},{3,1},{4,0},{5,7},{6,2},{7,5},{8,12},{9,11},{10,... | collective-permute-start | bytes 786440 | tf_op jit(solution)/shard_map/ppermute | solution.py:329
  19.7 1.6 %collective-permute-start.9 = (bf16[384,256]{1,0:T(8,128)(2,1)S(1)}, bf16[384,256]{1,0:T(8,128)(2,1)S(1)}, u32[]{:S(2)}, u32[]{:S(2)}) collective-permute-start(bf16[384,256]{1,0:T(8,128)(2,1)S(1)} %get-tuple-element.63), channel_id=1, source_target_pairs={{0,1},{1,0},{2,3},{3,2},{4,5},{5,4},{6,7},{7,6},{8,9},{9,8},{10,11... | collective-permute-start | bytes 589832 | tf_op jit(solution)/shard_map/ppermute | solution.py:326
  19.9 1.4 %collective-permute-start.10 = (bf16[128,256]{1,0:T(8,128)(2,1)S(1)}, bf16[128,256]{1,0:T(8,128)(2,1)S(1)}, u32[]{:S(2)}, u32[]{:S(2)}) collective-permute-start(bf16[128,256]{1,0:T(8,128)(2,1)S(1)} %get-tuple-element.64), channel_id=1, source_target_pairs={{0,1},{1,0},{2,3},{3,2},{4,5},{5,4},{6,7},{7,6},{8,9},{9,8},{10,11... | collective-permute-start | bytes 196616 | tf_op jit(solution)/shard_map/ppermute | solution.py:326
  24.6 7.0 %collective-permute-start.13 = (bf16[256,256]{1,0:T(8,128)(2,1)S(1)}, bf16[256,256]{1,0:T(8,128)(2,1)S(1)}, u32[]{:S(2)}, u32[]{:S(2)}) collective-permute-start(bf16[256,256]{1,0:T(8,128)(2,1)S(1)} %get-tuple-element.67.refs_2_), channel_id=1, source_target_pairs={{0,8},{1,9},{2,10},{3,11},{4,12},{5,13},{6,14},{7,15},{8,0},{9,1},... | collective-permute-start | bytes 393224 | tf_op jit(solution)/shard_map/ppermute | solution.py:333
  26.5 9.4 %collective-permute-start.14 = (bf16[256,256]{1,0:T(8,128)(2,1)S(1)}, bf16[256,256]{1,0:T(8,128)(2,1)S(1)}, u32[]{:S(2)}, u32[]{:S(2)}) collective-permute-start(bf16[256,256]{1,0:T(8,128)(2,1)S(1)} %get-tuple-element.71), channel_id=1, source_target_pairs={{0,16},{1,17},{2,18},{3,19},{4,20},{5,21},{6,22},{7,23},{8,24},{9,... | collective-permute-start | bytes 393224 | tf_op jit(solution)/shard_map/ppermute | solution.py:333
  27.7 3.9 %collective-permute-start.8 = (bf16[64,256]{1,0:T(8,128)(2,1)S(1)}, bf16[64,256]{1,0:T(8,128)(2,1)S(1)}, u32[]{:S(2)}, u32[]{:S(2)}) collective-permute-start(bf16[64,256]{1,0:T(8,128)(2,1)S(1)} %get-tuple-element.61.refs_0_), channel_id=1, source_target_pairs={{0,2},{1,5},{2,0},{3,7},{4,6},{5,1},{6,4},{7,3},{8,10},{9,13},{10,... | collective-permute-start | bytes 98312 | tf_op jit(solution)/shard_map/ppermute | solution.py:329
  31.7 7.9 %collective-permute-start.16 = (bf16[256,256]{1,0:T(8,128)(2,1)S(1)}, bf16[256,256]{1,0:T(8,128)(2,1)S(1)}, u32[]{:S(2)}, u32[]{:S(2)}) collective-permute-start(bf16[256,256]{1,0:T(8,128)(2,1)S(1)} %get-tuple-element.69.refs_4_), channel_id=1, source_target_pairs={{0,16},{1,17},{2,18},{3,19},{4,20},{5,21},{6,22},{7,23},{8,24},{9,... | collective-permute-start | bytes 393224 | tf_op jit(solution)/shard_map/ppermute | solution.py:333
  33.5 6.2 %collective-permute-start.12 = (bf16[128,256]{1,0:T(8,128)(2,1)S(1)}, bf16[128,256]{1,0:T(8,128)(2,1)S(1)}, u32[]{:S(2)}, u32[]{:S(2)}) collective-permute-start(bf16[128,256]{1,0:T(8,128)(2,1)S(1)} %shard_map.93.refs_2_), channel_id=1, source_target_pairs={{0,4},{1,3},{2,6},{3,1},{4,0},{5,7},{6,2},{7,5},{8,12},{9,11},{10,... | collective-permute-start | bytes 196616 | tf_op jit(solution)/shard_map/ppermute | solution.py:329
  35.9 6.1 %collective-permute-start.15 = (bf16[256,256]{1,0:T(8,128)(2,1)S(1)}, bf16[256,256]{1,0:T(8,128)(2,1)S(1)}, u32[]{:S(2)}, u32[]{:S(2)}) collective-permute-start(bf16[256,256]{1,0:T(8,128)(2,1)S(1)} %get-tuple-element.73), channel_id=1, source_target_pairs={{0,8},{1,9},{2,10},{3,11},{4,12},{5,13},{6,14},{7,15},{8,0},{9,1},... | collective-permute-start | bytes 393224 | tf_op jit(solution)/shard_map/ppermute | solution.py:333
  39.6 5.0 %collective-permute-start.17 = (bf16[256,256]{1,0:T(8,128)(2,1)S(1)}, bf16[256,256]{1,0:T(8,128)(2,1)S(1)}, u32[]{:S(2)}, u32[]{:S(2)}) collective-permute-start(bf16[256,256]{1,0:T(8,128)(2,1)S(1)} %shard_map.98.refs_2_), channel_id=1, source_target_pairs={{0,8},{1,9},{2,10},{3,11},{4,12},{5,13},{6,14},{7,15},{8,0},{9,1},... | collective-permute-start | bytes 393224 | tf_op jit(solution)/shard_map/ppermute | solution.py:333

commit v6 on v5

--- a/solution.py
+++ b/solution.py
@@ -247,16 +247,13 @@
 def finish_kernel(blocks, start, total, update, project, out_hbm, result, sem):
     block = total.shape[0] // blocks
     row = lax.axis_index("row")
-    value = total[...] - jnp.dot(update[:, start:], project[...], preferred_element_type=F32)
-    result[...] = value.astype(BF)
     copies = []
     for code in range(blocks):
+        rows = slice(code * block, (code + 1) * block)
+        value = total[rows] - jnp.dot(update[rows, start:], project[...], preferred_element_type=F32)
+        result[rows] = value.astype(BF)
         at = pl.multiple_of(jnp.bitwise_xor(row, code) * block, block)
-        copies.append(
-            pltpu.make_async_copy(
-                result.at[code * block:(code + 1) * block], out_hbm.at[pl.ds(at, block)], sem.at[code]
-            )
-        )
+        copies.append(pltpu.make_async_copy(result.at[rows], out_hbm.at[pl.ds(at, block)], sem.at[code]))
         copies[-1].start()
     for copy in copies:
         copy.wait()

time: 45.7 us -> 45.7 us (level)
  no operation moved by 1% of the time
where the time goes in v6:
time: 45.7 us; the launch traced here: 45.5 us
  starting transfers between devices  19.1 us (42%)
  waiting for transfers between devices  15.9 us (35%)
  Pallas kernels  10.4 us (23%)
    ppermute x7, starting transfers between devices, swap_row(): return lax.ppermute(value, ('row', 'col'), pairs)  10.5 us
    ppermute x7, waiting for transfers between devices, swap_row(): return lax.ppermute(value, ('row', 'col'), pairs)  8.69 us
    ppermute x5, starting transfers between devices, swap_col(): lax.ppermute(value, 'col', [(i, i ^ 1 << col_orders[i % 2][stage]) for i...  6.77 us
    ppermute x5, waiting for transfers between devices, swap_col(): lax.ppermute(value, 'col', [(i, i ^ 1 << col_orders[i % 2][stage]) for i...  6.16 us
    pallas_call x4, Pallas kernels, products(): pl.pallas_call(functools.partial(product_kernel, plan, width, chunks, pol...  5.48 us
    pallas_call x13, Pallas kernels, local(): pl.pallas_call(kernel, in_specs=[pl.BlockSpec(memory_space=pltpu.VMEM)] *...  2.16 us
    pallas_call x1, Pallas kernels, panel_blocks(): pl.pallas_call(functools.partial(panel_kernel, row_codes, row_orders, blo...  1.87 us
    ppermute x6, starting transfers between devices, swap_cores(): return lax.ppermute(value, 'col', [(i, i ^ 1) for i in range(n_col)])  1.79 us
  transfers between devices with their start and end apart: 18, of which 10 were waited for; matrix products, arithmetic and copies ran while one was open for 0% of the time, Pallas kernels for 13%

profile of v6, /device:TPU:0, one launch (start us, length us, event | category | flops | bytes accessed | tf_op | source)
XLA Modules:
  0.0 45.5 jit_solution(9301944778896962939)
XLA Ops:
  0.0 1.9 %shard_map.82 = (bf16[2,512,256]{2,1,0:T(8,128)(2,1)S(1)}, bf16[256,256]{1,0:T(8,128)(2,1)S(1)}, bf16[320,256]{1,0:T(8,128)(2,1)S(1)}, f32[64,256]{1,0:T(8,128)S...) custom-call(bf16[512,2048]{1,0:T(8,128)(2,1)} %refs_0_.1, ...), custom_call_target="tpu_custom_call" | custom-call | flops 1 | bytes 1 | tf_op jit(solution)/shard_map/pallas_call | solution.py:225
  1.9 1.4 %shard_map.83 = (bf16[512,256]{1,0:T(8,128)(2,1)S(1)}, bf16[512,256]{1,0:T(8,128)(2,1)S(1)}) custom-call(bf16[512,2048]{1,0:T(8,128)(2,1)S(1)} %get-tuple-element.44.refs_0_, f32[1,2048]{1,0:T(1,128)S(1)} %get-tuple-element.45.refs_1_, f32[1,2048]{1,0:T(1,128)S(1)} %get-tuple-element.46.refs_2_, f32[1,2048]{1,0:T(1,128)S(1)} %get-tuple-element.47.refs_3_, ...), custom_call_target="tpu_custom_call" | custom-call | flops 1 | bytes 1 | tf_op jit(solution)/shard_map/pallas_call | solution.py:140
  3.3 0.5 %collective-permute-start.2 = (bf16[512,256]{1,0:T(8,128)(2,1)S(1)}, bf16[512,256]{1,0:T(8,128)(2,1)S(1)}, u32[]{:S(2)}, u32[]{:S(2)}) collective-permute-start(bf16[512,256]{1,0:T(8,128)(2,1)S(1)} %get-tuple-element.52), channel_id=1, source_target_pairs={{0,1},{1,0},{2,3},{3,2},{4,5},{5,4},{6,7},{7,6},{8,9},{9,8},{10,11... | collective-permute-start | bytes 786440 | tf_op jit(solution)/shard_map/ppermute | solution.py:323
  3.8 1.4 %shard_map.84 = (bf16[512,256]{1,0:T(8,128)(2,1)S(1)}, bf16[512,256]{1,0:T(8,128)(2,1)S(1)}) custom-call(bf16[512,2048]{1,0:T(8,128)(2,1)S(1)} %get-tuple-element.44.refs_0_, f32[1,2048]{1,0:T(1,128)S(1)} %get-tuple-element.45.refs_1_, f32[1,2048]{1,0:T(1,128)S(1)} %get-tuple-element.46.refs_2_, f32[1,2048]{1,0:T(1,128)S(1)} %get-tuple-element.47.refs_3_, ...), custom_call_target="tpu_custom_call" | custom-call | flops 1 | bytes 1 | tf_op jit(solution)/shard_map/pallas_call | solution.py:140
  5.2 0.1 collective-permute-start.1
  5.3 3.0 %collective-permute-start = (bf16[320,256]{1,0:T(8,128)(2,1)S(1)}, bf16[320,256]{1,0:T(8,128)(2,1)S(1)}, u32[]{:S(2)}, u32[]{:S(2)}) collective-permute-start(bf16[320,256]{1,0:T(8,128)(2,1)S(1)} %get-tuple-element.43), channel_id=1, source_target_pairs={{0,8},{1,17},{2,10},{3,19},{4,12},{5,21},{6,14},{7,23},{8,0},{9,25... | collective-permute-start | bytes 491528 | tf_op jit(solution)/shard_map/ppermute | solution.py:330
  8.3 0.0 collective-permute-done.2.refs_1_
  8.3 0.1 shard_map.85.refs_3_
  8.4 1.6 %collective-permute-start.5 = (bf16[512,256]{1,0:T(8,128)(2,1)S(1)}, bf16[512,256]{1,0:T(8,128)(2,1)S(1)}, u32[]{:S(2)}, u32[]{:S(2)}) collective-permute-start(bf16[512,256]{1,0:T(8,128)(2,1)S(1)} %shard_map.85.refs_3_), channel_id=1, source_target_pairs={{0,2},{1,5},{2,0},{3,7},{4,6},{5,1},{6,4},{7,3},{8,10},{9,13},{10,... | collective-permute-start | bytes 786440 | tf_op jit(solution)/shard_map/ppermute | solution.py:326
  9.9 0.0 collective-permute-done.1.refs_1_
  9.9 0.1 shard_map.86.refs_3_.refs_5_
  10.0 0.6 %collective-permute-start.7 = (bf16[512,256]{1,0:T(8,128)(2,1)S(1)}, bf16[512,256]{1,0:T(8,128)(2,1)S(1)}, u32[]{:S(2)}, u32[]{:S(2)}) collective-permute-start(bf16[512,256]{1,0:T(8,128)(2,1)S(1)} %shard_map.86.refs_3_.refs_5_), channel_id=1, source_target_pairs={{0,2},{1,5},{2,0},{3,7},{4,6},{5,1},{6,4},{7,3},{8,10},{9,13},{10,... | collective-permute-start | bytes 786440 | tf_op jit(solution)/shard_map/ppermute | solution.py:326
  10.6 1.4 %shard_map.88 = (bf16[512,256]{1,0:T(8,128)(2,1)S(1)}, bf16[512,256]{1,0:T(8,128)(2,1)S(1)}) custom-call(bf16[512,2048]{1,0:T(8,128)(2,1)S(1)} %get-tuple-element.44.refs_0_, f32[1,2048]{1,0:T(1,128)S(1)} %get-tuple-element.45.refs_1_, f32[1,2048]{1,0:T(1,128)S(1)} %get-tuple-element.46.refs_2_, f32[1,2048]{1,0:T(1,128)S(1)} %get-tuple-element.47.refs_3_, ...), custom_call_target="tpu_custom_call" | custom-call | flops 1 | bytes 1 | tf_op jit(solution)/shard_map/pallas_call | solution.py:140
  12.0 0.3 collective-permute-start.6
  12.2 0.3 collective-permute-start.4
  12.5 0.6 %collective-permute-done.refs_2_ = bf16[320,256]{1,0:T(8,128)(2,1)S(1)} collective-permute-done((bf16[320,256]{1,0:T(8,128)(2,1)S(1)}, bf16[320,256]{1,0:T(8,128)(2,1)S(1)}, u32[]{:S(2)}, u32[]{:S(2)}) %collective-permute-start) | collective-permute-done | bytes 163872 | tf_op jit(solution)/shard_map/ppermute | solution.py:330
  13.1 2.4 %collective-permute-start.3 = (bf16[320,256]{1,0:T(8,128)(2,1)S(1)}, bf16[320,256]{1,0:T(8,128)(2,1)S(1)}, u32[]{:S(2)}, u32[]{:S(2)}) collective-permute-start(bf16[320,256]{1,0:T(8,128)(2,1)S(1)} %get-tuple-element.55), channel_id=1, source_target_pairs={{0,16},{1,9},{2,18},{3,11},{4,20},{5,13},{6,22},{7,15},{8,24},{9,1... | collective-permute-start | bytes 491528 | tf_op jit(solution)/shard_map/ppermute | solution.py:330
  15.5 1.4 %shard_map.89 = (bf16[512,256]{1,0:T(8,128)(2,1)S(1)}, bf16[512,256]{1,0:T(8,128)(2,1)S(1)}) custom-call(bf16[512,2048]{1,0:T(8,128)(2,1)S(1)} %get-tuple-element.44.refs_0_, f32[1,2048]{1,0:T(1,128)S(1)} %get-tuple-element.45.refs_1_, f32[1,2048]{1,0:T(1,128)S(1)} %get-tuple-element.46.refs_2_, f32[1,2048]{1,0:T(1,128)S(1)} %get-tuple-element.47.refs_3_, ...), custom_call_target="tpu_custom_call" | custom-call | flops 1 | bytes 1 | tf_op jit(solution)/shard_map/pallas_call | solution.py:140
  16.9 0.7 %collective-permute-done.7.refs_5_ = bf16[512,256]{1,0:T(8,128)(2,1)S(1)} collective-permute-done((bf16[512,256]{1,0:T(8,128)(2,1)S(1)}, bf16[512,256]{1,0:T(8,128)(2,1)S(1)}, u32[]{:S(2)}, u32[]{:S(2)}) %collective-permute-start.7) | collective-permute-done | bytes 262176 | tf_op jit(solution)/shard_map/ppermute | solution.py:326
  17.6 0.0 collective-permute-done.5.refs_2_
  17.6 0.0 collective-permute-done.6.refs_4_
  17.6 0.0 collective-permute-done.4.refs_1_
  17.6 0.2 shard_map.90
  17.8 0.0 copy-start
  17.8 1.6 %collective-permute-start.11 = (bf16[512,256]{1,0:T(8,128)(2,1)S(1)}, bf16[512,256]{1,0:T(8,128)(2,1)S(1)}, u32[]{:S(2)}, u32[]{:S(2)}) collective-permute-start(bf16[512,256]{1,0:T(8,128)(2,1)S(1)} %get-tuple-element.60.refs_3_), channel_id=1, source_target_pairs={{0,4},{1,3},{2,6},{3,1},{4,0},{5,7},{6,2},{7,5},{8,12},{9,11},{10,... | collective-permute-start | bytes 786440 | tf_op jit(solution)/shard_map/ppermute | solution.py:326
  19.4 0.2 collective-permute-done.3.refs_2_
  19.7 0.2 collective-permute-start.9
  19.9 0.4 collective-permute-start.10
  20.2 1.0 %collective-permute-done.10.refs_2_ = bf16[128,256]{1,0:T(8,128)(2,1)S(1)} collective-permute-done((bf16[128,256]{1,0:T(8,128)(2,1)S(1)}, bf16[128,256]{1,0:T(8,128)(2,1)S(1)}, u32[]{:S(2)}, u32[]{:S(2)}) %collective-permute-start.10) | collective-permute-done | bytes 65568 | tf_op jit(solution)/shard_map/ppermute | solution.py:323
  21.3 3.0 %collective-permute-done.11.refs_5_ = bf16[512,256]{1,0:T(8,128)(2,1)S(1)} collective-permute-done((bf16[512,256]{1,0:T(8,128)(2,1)S(1)}, bf16[512,256]{1,0:T(8,128)(2,1)S(1)}, u32[]{:S(2)}, u32[]{:S(2)}) %collective-permute-start.11) | collective-permute-done | bytes 262176 | tf_op jit(solution)/shard_map/ppermute | solution.py:326
  24.3 0.3 shard_map.92
  24.6 1.9 %collective-permute-start.13 = (bf16[256,256]{1,0:T(8,128)(2,1)S(1)}, bf16[256,256]{1,0:T(8,128)(2,1)S(1)}, u32[]{:S(2)}, u32[]{:S(2)}) collective-permute-start(bf16[256,256]{1,0:T(8,128)(2,1)S(1)} %get-tuple-element.67.refs_2_), channel_id=1, source_target_pairs={{0,8},{1,9},{2,10},{3,11},{4,12},{5,13},{6,14},{7,15},{8,0},{9,1},... | collective-permute-start | bytes 393224 | tf_op jit(solution)/shard_map/ppermute | solution.py:330
  26.5 1.2 %collective-permute-start.14 = (bf16[256,256]{1,0:T(8,128)(2,1)S(1)}, bf16[256,256]{1,0:T(8,128)(2,1)S(1)}, u32[]{:S(2)}, u32[]{:S(2)}) collective-permute-start(bf16[256,256]{1,0:T(8,128)(2,1)S(1)} %get-tuple-element.71), channel_id=1, source_target_pairs={{0,16},{1,17},{2,18},{3,19},{4,20},{5,21},{6,22},{7,23},{8,24},{9,... | collective-permute-start | bytes 393224 | tf_op jit(solution)/shard_map/ppermute | solution.py:330
  27.7 1.5 %collective-permute-start.8 = (bf16[64,256]{1,0:T(8,128)(2,1)S(1)}, bf16[64,256]{1,0:T(8,128)(2,1)S(1)}, u32[]{:S(2)}, u32[]{:S(2)}) collective-permute-start(bf16[64,256]{1,0:T(8,128)(2,1)S(1)} %get-tuple-element.61.refs_0_), channel_id=1, source_target_pairs={{0,2},{1,5},{2,0},{3,7},{4,6},{5,1},{6,4},{7,3},{8,10},{9,13},{10,... | collective-permute-start | bytes 98312 | tf_op jit(solution)/shard_map/ppermute | solution.py:326
  29.2 2.4 %collective-permute-done.8.refs_1_ = bf16[64,256]{1,0:T(8,128)(2,1)S(1)} collective-permute-done((bf16[64,256]{1,0:T(8,128)(2,1)S(1)}, bf16[64,256]{1,0:T(8,128)(2,1)S(1)}, u32[]{:S(2)}, u32[]{:S(2)}) %collective-permute-start.8) | collective-permute-done | bytes 32800 | tf_op jit(solution)/shard_map/ppermute | solution.py:326
  31.6 0.0 collective-permute-done.13.refs_1_
  31.7 1.8 %collective-permute-start.16 = (bf16[256,256]{1,0:T(8,128)(2,1)S(1)}, bf16[256,256]{1,0:T(8,128)(2,1)S(1)}, u32[]{:S(2)}, u32[]{:S(2)}) collective-permute-start(bf16[256,256]{1,0:T(8,128)(2,1)S(1)} %get-tuple-element.69.refs_4_), channel_id=1, source_target_pairs={{0,16},{1,17},{2,18},{3,19},{4,20},{5,21},{6,22},{7,23},{8,24},{9,... | collective-permute-start | bytes 393224 | tf_op jit(solution)/shard_map/ppermute | solution.py:330
  33.5 1.5 %collective-permute-start.12 = (bf16[128,256]{1,0:T(8,128)(2,1)S(1)}, bf16[128,256]{1,0:T(8,128)(2,1)S(1)}, u32[]{:S(2)}, u32[]{:S(2)}) collective-permute-start(bf16[128,256]{1,0:T(8,128)(2,1)S(1)} %shard_map.93.refs_2_), channel_id=1, source_target_pairs={{0,4},{1,3},{2,6},{3,1},{4,0},{5,7},{6,2},{7,5},{8,12},{9,11},{10,... | collective-permute-start | bytes 196616 | tf_op jit(solution)/shard_map/ppermute | solution.py:326
  35.0 0.9 %collective-permute-done.14.refs_1_ = bf16[256,256]{1,0:T(8,128)(2,1)S(1)} collective-permute-done((bf16[256,256]{1,0:T(8,128)(2,1)S(1)}, bf16[256,256]{1,0:T(8,128)(2,1)S(1)}, u32[]{:S(2)}, u32[]{:S(2)}) %collective-permute-start.14) | collective-permute-done | bytes 131104 | tf_op jit(solution)/shard_map/ppermute | solution.py:330
  35.9 0.1 collective-permute-start.15
  36.1 3.5 %collective-permute-done.16.refs_1_ = bf16[256,256]{1,0:T(8,128)(2,1)S(1)} collective-permute-done((bf16[256,256]{1,0:T(8,128)(2,1)S(1)}, bf16[256,256]{1,0:T(8,128)(2,1)S(1)}, u32[]{:S(2)}, u32[]{:S(2)}) %collective-permute-start.16) | collective-permute-done | bytes 131104 | tf_op jit(solution)/shard_map/ppermute | solution.py:330
  39.6 0.1 collective-permute-start.17
  39.7 0.0 collective-permute-done.12.refs_3_
  39.7 1.1 %shard_map.95.refs_0_.update = bf16[512,512]{1,0:T(8,128)(2,1)S(1)} custom-call(bf16[2,512,256]{2,1,0:T(8,128)(2,1)S(1)} %get-tuple-element.40.refs_0_, f32[2,256,256]{2,1,0:T(8,128)S(1)} %copy-done, bf16[128,256]{1,0:T(8,128)(2,1)S(1)} %shard_map.93.refs_2_, bf16[128,256]{1,0:T(8,128)(2,1)S(1)} %collective-permute-done.12.refs_3_, ...), custom_call_target="tpu_custom_call" | custom-call | flops 1000000000 | bytes 1 | tf_op jit(solution)/shard_map/pallas_call | solution.py:70
  40.8 1.3 %collective-permute-done.15.refs_1_ = bf16[256,256]{1,0:T(8,128)(2,1)S(1)} collective-permute-done((bf16[256,256]{1,0:T(8,128)(2,1)S(1)}, bf16[256,256]{1,0:T(8,128)(2,1)S(1)}, u32[]{:S(2)}, u32[]{:S(2)}) %collective-permute-start.15) | collective-permute-done | bytes 131104 | tf_op jit(solution)/shard_map/ppermute | solution.py:330
  42.1 0.2 shard_map.99.total
  42.3 2.3 %collective-permute-done.17.project = bf16[256,256]{1,0:T(8,128)(2,1)S(1)} collective-permute-done((bf16[256,256]{1,0:T(8,128)(2,1)S(1)}, bf16[256,256]{1,0:T(8,128)(2,1)S(1)}, u32[]{:S(2)}, u32[]{:S(2)}) %collective-permute-start.17) | collective-permute-done | bytes 131104 | tf_op jit(solution)/shard_map/ppermute | solution.py:330
  44.6 0.9 %shard_map.100 = bf16[512,256]{1,0:T(8,128)(2,1)} custom-call(f32[512,256]{1,0:T(8,128)S(1)} %shard_map.99.total, bf16[512,512]{1,0:T(8,128)(2,1)S(1)} %shard_map.95.refs_0_.update, bf16[256,256]{1,0:T(8,128)(2,1)S(1)} %collective-permute-done.17.project), custom_call_target="tpu_custom_call" | custom-call | flops 1 | bytes 1 | tf_op jit(solution)/shard_map/pallas_call | solution.py:268
  (9 shorter events, 0.2 us)
Async XLA Ops:
  3.3 5.0 %collective-permute-start.2 = (bf16[512,256]{1,0:T(8,128)(2,1)S(1)}, bf16[512,256]{1,0:T(8,128)(2,1)S(1)}, u32[]{:S(2)}, u32[]{:S(2)}) collective-permute-start(bf16[512,256]{1,0:T(8,128)(2,1)S(1)} %get-tuple-element.52), channel_id=1, source_target_pairs={{0,1},{1,0},{2,3},{3,2},{4,5},{5,4},{6,7},{7,6},{8,9},{9,8},{10,11... | collective-permute-start | bytes 786440 | tf_op jit(solution)/shard_map/ppermute | solution.py:323
  5.2 4.8 %collective-permute-start.1 = (bf16[512,256]{1,0:T(8,128)(2,1)S(1)}, bf16[512,256]{1,0:T(8,128)(2,1)S(1)}, u32[]{:S(2)}, u32[]{:S(2)}) collective-permute-start(bf16[512,256]{1,0:T(8,128)(2,1)S(1)} %get-tuple-element.51), channel_id=1, source_target_pairs={{0,1},{1,0},{2,3},{3,2},{4,5},{5,4},{6,7},{7,6},{8,9},{9,8},{10,11... | collective-permute-start | bytes 786440 | tf_op jit(solution)/shard_map/ppermute | solution.py:323
  5.3 7.8 %collective-permute-start = (bf16[320,256]{1,0:T(8,128)(2,1)S(1)}, bf16[320,256]{1,0:T(8,128)(2,1)S(1)}, u32[]{:S(2)}, u32[]{:S(2)}) collective-permute-start(bf16[320,256]{1,0:T(8,128)(2,1)S(1)} %get-tuple-element.43), channel_id=1, source_target_pairs={{0,8},{1,17},{2,10},{3,19},{4,12},{5,21},{6,14},{7,23},{8,0},{9,25... | collective-permute-start | bytes 491528 | tf_op jit(solution)/shard_map/ppermute | solution.py:330
  8.4 9.2 %collective-permute-start.5 = (bf16[512,256]{1,0:T(8,128)(2,1)S(1)}, bf16[512,256]{1,0:T(8,128)(2,1)S(1)}, u32[]{:S(2)}, u32[]{:S(2)}) collective-permute-start(bf16[512,256]{1,0:T(8,128)(2,1)S(1)} %shard_map.85.refs_3_), channel_id=1, source_target_pairs={{0,2},{1,5},{2,0},{3,7},{4,6},{5,1},{6,4},{7,3},{8,10},{9,13},{10,... | collective-permute-start | bytes 786440 | tf_op jit(solution)/shard_map/ppermute | solution.py:326
  10.0 7.6 %collective-permute-start.7 = (bf16[512,256]{1,0:T(8,128)(2,1)S(1)}, bf16[512,256]{1,0:T(8,128)(2,1)S(1)}, u32[]{:S(2)}, u32[]{:S(2)}) collective-permute-start(bf16[512,256]{1,0:T(8,128)(2,1)S(1)} %shard_map.86.refs_3_.refs_5_), channel_id=1, source_target_pairs={{0,2},{1,5},{2,0},{3,7},{4,6},{5,1},{6,4},{7,3},{8,10},{9,13},{10,... | collective-permute-start | bytes 786440 | tf_op jit(solution)/shard_map/ppermute | solution.py:326
  12.0 5.7 %collective-permute-start.6 = (bf16[512,256]{1,0:T(8,128)(2,1)S(1)}, bf16[512,256]{1,0:T(8,128)(2,1)S(1)}, u32[]{:S(2)}, u32[]{:S(2)}) collective-permute-start(bf16[512,256]{1,0:T(8,128)(2,1)S(1)} %get-tuple-element.59), channel_id=1, source_target_pairs={{0,1},{1,0},{2,3},{3,2},{4,5},{5,4},{6,7},{7,6},{8,9},{9,8},{10,11... | collective-permute-start | bytes 786440 | tf_op jit(solution)/shard_map/ppermute | solution.py:323
  12.2 5.4 %collective-permute-start.4 = (bf16[512,256]{1,0:T(8,128)(2,1)S(1)}, bf16[512,256]{1,0:T(8,128)(2,1)S(1)}, u32[]{:S(2)}, u32[]{:S(2)}) collective-permute-start(bf16[512,256]{1,0:T(8,128)(2,1)S(1)} %get-tuple-element.56.refs_5_), channel_id=1, source_target_pairs={{0,1},{1,0},{2,3},{3,2},{4,5},{5,4},{6,7},{7,6},{8,9},{9,8},{10,11... | collective-permute-start | bytes 786440 | tf_op jit(solution)/shard_map/ppermute | solution.py:323
  13.1 6.5 %collective-permute-start.3 = (bf16[320,256]{1,0:T(8,128)(2,1)S(1)}, bf16[320,256]{1,0:T(8,128)(2,1)S(1)}, u32[]{:S(2)}, u32[]{:S(2)}) collective-permute-start(bf16[320,256]{1,0:T(8,128)(2,1)S(1)} %get-tuple-element.55), channel_id=1, source_target_pairs={{0,16},{1,9},{2,18},{3,11},{4,20},{5,13},{6,22},{7,15},{8,24},{9,1... | collective-permute-start | bytes 491528 | tf_op jit(solution)/shard_map/ppermute | solution.py:330
  17.8 21.8 %copy-start = (f32[2,256,256]{2,1,0:T(8,128)S(1)}, f32[2,256,256]{2,1,0:T(8,128)}, u32[]{:S(2)}) copy-start(f32[2,256,256]{2,1,0:T(8,128)} %refs_1_.3) | copy-start | bytes 1572868
  17.8 6.4 %collective-permute-start.11 = (bf16[512,256]{1,0:T(8,128)(2,1)S(1)}, bf16[512,256]{1,0:T(8,128)(2,1)S(1)}, u32[]{:S(2)}, u32[]{:S(2)}) collective-permute-start(bf16[512,256]{1,0:T(8,128)(2,1)S(1)} %get-tuple-element.60.refs_3_), channel_id=1, source_target_pairs={{0,4},{1,3},{2,6},{3,1},{4,0},{5,7},{6,2},{7,5},{8,12},{9,11},{10,... | collective-permute-start | bytes 786440 | tf_op jit(solution)/shard_map/ppermute | solution.py:326
  19.7 1.6 %collective-permute-start.9 = (bf16[384,256]{1,0:T(8,128)(2,1)S(1)}, bf16[384,256]{1,0:T(8,128)(2,1)S(1)}, u32[]{:S(2)}, u32[]{:S(2)}) collective-permute-start(bf16[384,256]{1,0:T(8,128)(2,1)S(1)} %get-tuple-element.63), channel_id=1, source_target_pairs={{0,1},{1,0},{2,3},{3,2},{4,5},{5,4},{6,7},{7,6},{8,9},{9,8},{10,11... | collective-permute-start | bytes 589832 | tf_op jit(solution)/shard_map/ppermute | solution.py:323
  19.9 1.4 %collective-permute-start.10 = (bf16[128,256]{1,0:T(8,128)(2,1)S(1)}, bf16[128,256]{1,0:T(8,128)(2,1)S(1)}, u32[]{:S(2)}, u32[]{:S(2)}) collective-permute-start(bf16[128,256]{1,0:T(8,128)(2,1)S(1)} %get-tuple-element.64), channel_id=1, source_target_pairs={{0,1},{1,0},{2,3},{3,2},{4,5},{5,4},{6,7},{7,6},{8,9},{9,8},{10,11... | collective-permute-start | bytes 196616 | tf_op jit(solution)/shard_map/ppermute | solution.py:323
  24.6 7.0 %collective-permute-start.13 = (bf16[256,256]{1,0:T(8,128)(2,1)S(1)}, bf16[256,256]{1,0:T(8,128)(2,1)S(1)}, u32[]{:S(2)}, u32[]{:S(2)}) collective-permute-start(bf16[256,256]{1,0:T(8,128)(2,1)S(1)} %get-tuple-element.67.refs_2_), channel_id=1, source_target_pairs={{0,8},{1,9},{2,10},{3,11},{4,12},{5,13},{6,14},{7,15},{8,0},{9,1},... | collective-permute-start | bytes 393224 | tf_op jit(solution)/shard_map/ppermute | solution.py:330
  26.5 9.4 %collective-permute-start.14 = (bf16[256,256]{1,0:T(8,128)(2,1)S(1)}, bf16[256,256]{1,0:T(8,128)(2,1)S(1)}, u32[]{:S(2)}, u32[]{:S(2)}) collective-permute-start(bf16[256,256]{1,0:T(8,128)(2,1)S(1)} %get-tuple-element.71), channel_id=1, source_target_pairs={{0,16},{1,17},{2,18},{3,19},{4,20},{5,21},{6,22},{7,23},{8,24},{9,... | collective-permute-start | bytes 393224 | tf_op jit(solution)/shard_map/ppermute | solution.py:330
  27.7 3.9 %collective-permute-start.8 = (bf16[64,256]{1,0:T(8,128)(2,1)S(1)}, bf16[64,256]{1,0:T(8,128)(2,1)S(1)}, u32[]{:S(2)}, u32[]{:S(2)}) collective-permute-start(bf16[64,256]{1,0:T(8,128)(2,1)S(1)} %get-tuple-element.61.refs_0_), channel_id=1, source_target_pairs={{0,2},{1,5},{2,0},{3,7},{4,6},{5,1},{6,4},{7,3},{8,10},{9,13},{10,... | collective-permute-start | bytes 98312 | tf_op jit(solution)/shard_map/ppermute | solution.py:326
  31.7 7.9 %collective-permute-start.16 = (bf16[256,256]{1,0:T(8,128)(2,1)S(1)}, bf16[256,256]{1,0:T(8,128)(2,1)S(1)}, u32[]{:S(2)}, u32[]{:S(2)}) collective-permute-start(bf16[256,256]{1,0:T(8,128)(2,1)S(1)} %get-tuple-element.69.refs_4_), channel_id=1, source_target_pairs={{0,16},{1,17},{2,18},{3,19},{4,20},{5,21},{6,22},{7,23},{8,24},{9,... | collective-permute-start | bytes 393224 | tf_op jit(solution)/shard_map/ppermute | solution.py:330
  33.5 6.2 %collective-permute-start.12 = (bf16[128,256]{1,0:T(8,128)(2,1)S(1)}, bf16[128,256]{1,0:T(8,128)(2,1)S(1)}, u32[]{:S(2)}, u32[]{:S(2)}) collective-permute-start(bf16[128,256]{1,0:T(8,128)(2,1)S(1)} %shard_map.93.refs_2_), channel_id=1, source_target_pairs={{0,4},{1,3},{2,6},{3,1},{4,0},{5,7},{6,2},{7,5},{8,12},{9,11},{10,... | collective-permute-start | bytes 196616 | tf_op jit(solution)/shard_map/ppermute | solution.py:326
  35.9 6.1 %collective-permute-start.15 = (bf16[256,256]{1,0:T(8,128)(2,1)S(1)}, bf16[256,256]{1,0:T(8,128)(2,1)S(1)}, u32[]{:S(2)}, u32[]{:S(2)}) collective-permute-start(bf16[256,256]{1,0:T(8,128)(2,1)S(1)} %get-tuple-element.73), channel_id=1, source_target_pairs={{0,8},{1,9},{2,10},{3,11},{4,12},{5,13},{6,14},{7,15},{8,0},{9,1},... | collective-permute-start | bytes 393224 | tf_op jit(solution)/shard_map/ppermute | solution.py:330
  39.6 5.0 %collective-permute-start.17 = (bf16[256,256]{1,0:T(8,128)(2,1)S(1)}, bf16[256,256]{1,0:T(8,128)(2,1)S(1)}, u32[]{:S(2)}, u32[]{:S(2)}) collective-permute-start(bf16[256,256]{1,0:T(8,128)(2,1)S(1)} %shard_map.98.refs_2_), channel_id=1, source_target_pairs={{0,8},{1,9},{2,10},{3,11},{4,12},{5,13},{6,14},{7,15},{8,0},{9,1},... | collective-permute-start | bytes 393224 | tf_op jit(solution)/shard_map/ppermute | solution.py:330

commit v7 on v6

--- a/solution.py
+++ b/solution.py
@@ -304,7 +304,7 @@
     panel_vectors,
     panel_factors,
 ):
-    col_orders = bit_orders(n_col, 1)
+    col_orders = bit_orders(n_col, 1)[::-1]
     row_orders = bit_orders(n_row, 0)
     col_stages = len(col_orders[0])
     row_stages = len(row_orders[0])

time: 45.7 us -> 45.7 us (level)
  no operation moved by 1% of the time
where the time goes in v7:
time: 45.7 us; the launch traced here: 45.5 us
  starting transfers between devices  19 us (42%)
  waiting for transfers between devices  16 us (35%)
  Pallas kernels  10.4 us (23%)
    ppermute x7, starting transfers between devices, swap_row(): return lax.ppermute(value, ('row', 'col'), pairs)  10.5 us
    ppermute x7, waiting for transfers between devices, swap_row(): return lax.ppermute(value, ('row', 'col'), pairs)  8.78 us
    ppermute x5, starting transfers between devices, swap_col(): lax.ppermute(value, 'col', [(i, i ^ 1 << col_orders[i % 2][stage]) for i...  6.73 us
    ppermute x5, waiting for transfers between devices, swap_col(): lax.ppermute(value, 'col', [(i, i ^ 1 << col_orders[i % 2][stage]) for i...  6.14 us
    pallas_call x4, Pallas kernels, products(): pl.pallas_call(functools.partial(product_kernel, plan, width, chunks, pol...  5.48 us
    pallas_call x13, Pallas kernels, local(): pl.pallas_call(kernel, in_specs=[pl.BlockSpec(memory_space=pltpu.VMEM)] *...  2.16 us
    pallas_call x1, Pallas kernels, panel_blocks(): pl.pallas_call(functools.partial(panel_kernel, row_codes, row_orders, blo...  1.87 us
    ppermute x6, starting transfers between devices, swap_cores(): return lax.ppermute(value, 'col', [(i, i ^ 1) for i in range(n_col)])  1.79 us
  transfers between devices with their start and end apart: 18, of which 10 were waited for; matrix products, arithmetic and copies ran while one was open for 0% of the time, Pallas kernels for 13%

profile of v7, /device:TPU:0, one launch (start us, length us, event | category | flops | bytes accessed | tf_op | source)
XLA Modules:
  0.0 45.5 jit_solution(13426553018094425414)
XLA Ops:
  0.0 1.9 %shard_map.82 = (bf16[2,512,256]{2,1,0:T(8,128)(2,1)S(1)}, bf16[256,256]{1,0:T(8,128)(2,1)S(1)}, bf16[320,256]{1,0:T(8,128)(2,1)S(1)}, f32[64,256]{1,0:T(8,128)S...) custom-call(bf16[512,2048]{1,0:T(8,128)(2,1)} %refs_0_.1, ...), custom_call_target="tpu_custom_call" | custom-call | flops 1 | bytes 1 | tf_op jit(solution)/shard_map/pallas_call | solution.py:225
  1.9 1.4 %shard_map.83 = (bf16[512,256]{1,0:T(8,128)(2,1)S(1)}, bf16[512,256]{1,0:T(8,128)(2,1)S(1)}) custom-call(bf16[512,2048]{1,0:T(8,128)(2,1)S(1)} %get-tuple-element.44.refs_0_, f32[1,2048]{1,0:T(1,128)S(1)} %get-tuple-element.45.refs_1_, f32[1,2048]{1,0:T(1,128)S(1)} %get-tuple-element.46.refs_2_, f32[1,2048]{1,0:T(1,128)S(1)} %get-tuple-element.47.refs_3_, ...), custom_call_target="tpu_custom_call" | custom-call | flops 1 | bytes 1 | tf_op jit(solution)/shard_map/pallas_call | solution.py:140
  3.3 0.5 %collective-permute-start.2 = (bf16[512,256]{1,0:T(8,128)(2,1)S(1)}, bf16[512,256]{1,0:T(8,128)(2,1)S(1)}, u32[]{:S(2)}, u32[]{:S(2)}) collective-permute-start(bf16[512,256]{1,0:T(8,128)(2,1)S(1)} %get-tuple-element.52), channel_id=1, source_target_pairs={{0,1},{1,0},{2,3},{3,2},{4,5},{5,4},{6,7},{7,6},{8,9},{9,8},{10,11... | collective-permute-start | bytes 786440 | tf_op jit(solution)/shard_map/ppermute | solution.py:323
  3.8 1.4 %shard_map.84 = (bf16[512,256]{1,0:T(8,128)(2,1)S(1)}, bf16[512,256]{1,0:T(8,128)(2,1)S(1)}) custom-call(bf16[512,2048]{1,0:T(8,128)(2,1)S(1)} %get-tuple-element.44.refs_0_, f32[1,2048]{1,0:T(1,128)S(1)} %get-tuple-element.45.refs_1_, f32[1,2048]{1,0:T(1,128)S(1)} %get-tuple-element.46.refs_2_, f32[1,2048]{1,0:T(1,128)S(1)} %get-tuple-element.47.refs_3_, ...), custom_call_target="tpu_custom_call" | custom-call | flops 1 | bytes 1 | tf_op jit(solution)/shard_map/pallas_call | solution.py:140
  5.2 0.1 collective-permute-start.1
  5.3 3.0 %collective-permute-start = (bf16[320,256]{1,0:T(8,128)(2,1)S(1)}, bf16[320,256]{1,0:T(8,128)(2,1)S(1)}, u32[]{:S(2)}, u32[]{:S(2)}) collective-permute-start(bf16[320,256]{1,0:T(8,128)(2,1)S(1)} %get-tuple-element.43), channel_id=1, source_target_pairs={{0,8},{1,17},{2,10},{3,19},{4,12},{5,21},{6,14},{7,23},{8,0},{9,25... | collective-permute-start | bytes 491528 | tf_op jit(solution)/shard_map/ppermute | solution.py:330
  8.3 0.0 collective-permute-done.2.refs_1_
  8.3 0.1 shard_map.85.refs_3_
  8.4 1.6 %collective-permute-start.5 = (bf16[512,256]{1,0:T(8,128)(2,1)S(1)}, bf16[512,256]{1,0:T(8,128)(2,1)S(1)}, u32[]{:S(2)}, u32[]{:S(2)}) collective-permute-start(bf16[512,256]{1,0:T(8,128)(2,1)S(1)} %shard_map.85.refs_3_), channel_id=1, source_target_pairs={{0,4},{1,3},{2,6},{3,1},{4,0},{5,7},{6,2},{7,5},{8,12},{9,11},{10,... | collective-permute-start | bytes 786440 | tf_op jit(solution)/shard_map/ppermute | solution.py:326
  10.0 0.0 collective-permute-done.1.refs_1_
  10.0 0.1 shard_map.86.refs_3_.refs_5_
  10.0 0.6 %collective-permute-start.7 = (bf16[512,256]{1,0:T(8,128)(2,1)S(1)}, bf16[512,256]{1,0:T(8,128)(2,1)S(1)}, u32[]{:S(2)}, u32[]{:S(2)}) collective-permute-start(bf16[512,256]{1,0:T(8,128)(2,1)S(1)} %shard_map.86.refs_3_.refs_5_), channel_id=1, source_target_pairs={{0,4},{1,3},{2,6},{3,1},{4,0},{5,7},{6,2},{7,5},{8,12},{9,11},{10,... | collective-permute-start | bytes 786440 | tf_op jit(solution)/shard_map/ppermute | solution.py:326
  10.6 1.4 %shard_map.88 = (bf16[512,256]{1,0:T(8,128)(2,1)S(1)}, bf16[512,256]{1,0:T(8,128)(2,1)S(1)}) custom-call(bf16[512,2048]{1,0:T(8,128)(2,1)S(1)} %get-tuple-element.44.refs_0_, f32[1,2048]{1,0:T(1,128)S(1)} %get-tuple-element.45.refs_1_, f32[1,2048]{1,0:T(1,128)S(1)} %get-tuple-element.46.refs_2_, f32[1,2048]{1,0:T(1,128)S(1)} %get-tuple-element.47.refs_3_, ...), custom_call_target="tpu_custom_call" | custom-call | flops 1 | bytes 1 | tf_op jit(solution)/shard_map/pallas_call | solution.py:140
  12.0 0.3 collective-permute-start.6
  12.2 0.3 collective-permute-start.4
  12.5 0.6 %collective-permute-done.refs_2_ = bf16[320,256]{1,0:T(8,128)(2,1)S(1)} collective-permute-done((bf16[320,256]{1,0:T(8,128)(2,1)S(1)}, bf16[320,256]{1,0:T(8,128)(2,1)S(1)}, u32[]{:S(2)}, u32[]{:S(2)}) %collective-permute-start) | collective-permute-done | bytes 163872 | tf_op jit(solution)/shard_map/ppermute | solution.py:330
  13.1 2.4 %collective-permute-start.3 = (bf16[320,256]{1,0:T(8,128)(2,1)S(1)}, bf16[320,256]{1,0:T(8,128)(2,1)S(1)}, u32[]{:S(2)}, u32[]{:S(2)}) collective-permute-start(bf16[320,256]{1,0:T(8,128)(2,1)S(1)} %get-tuple-element.55), channel_id=1, source_target_pairs={{0,16},{1,9},{2,18},{3,11},{4,20},{5,13},{6,22},{7,15},{8,24},{9,1... | collective-permute-start | bytes 491528 | tf_op jit(solution)/shard_map/ppermute | solution.py:330
  15.5 1.4 %shard_map.89 = (bf16[512,256]{1,0:T(8,128)(2,1)S(1)}, bf16[512,256]{1,0:T(8,128)(2,1)S(1)}) custom-call(bf16[512,2048]{1,0:T(8,128)(2,1)S(1)} %get-tuple-element.44.refs_0_, f32[1,2048]{1,0:T(1,128)S(1)} %get-tuple-element.45.refs_1_, f32[1,2048]{1,0:T(1,128)S(1)} %get-tuple-element.46.refs_2_, f32[1,2048]{1,0:T(1,128)S(1)} %get-tuple-element.47.refs_3_, ...), custom_call_target="tpu_custom_call" | custom-call | flops 1 | bytes 1 | tf_op jit(solution)/shard_map/pallas_call | solution.py:140
  16.9 0.7 %collective-permute-done.7.refs_5_ = bf16[512,256]{1,0:T(8,128)(2,1)S(1)} collective-permute-done((bf16[512,256]{1,0:T(8,128)(2,1)S(1)}, bf16[512,256]{1,0:T(8,128)(2,1)S(1)}, u32[]{:S(2)}, u32[]{:S(2)}) %collective-permute-start.7) | collective-permute-done | bytes 262176 | tf_op jit(solution)/shard_map/ppermute | solution.py:326
  17.6 0.0 collective-permute-done.5.refs_2_
  17.6 0.0 collective-permute-done.6.refs_4_
  17.6 0.0 collective-permute-done.4.refs_1_
  17.6 0.2 shard_map.90
  17.8 0.0 copy-start
  17.8 1.6 %collective-permute-start.11 = (bf16[512,256]{1,0:T(8,128)(2,1)S(1)}, bf16[512,256]{1,0:T(8,128)(2,1)S(1)}, u32[]{:S(2)}, u32[]{:S(2)}) collective-permute-start(bf16[512,256]{1,0:T(8,128)(2,1)S(1)} %get-tuple-element.60.refs_3_), channel_id=1, source_target_pairs={{0,2},{1,5},{2,0},{3,7},{4,6},{5,1},{6,4},{7,3},{8,10},{9,13},{10,... | collective-permute-start | bytes 786440 | tf_op jit(solution)/shard_map/ppermute | solution.py:326
  19.4 0.2 collective-permute-done.3.refs_2_
  19.7 0.2 collective-permute-start.9
  19.9 0.4 collective-permute-start.10
  20.2 1.0 %collective-permute-done.10.refs_2_ = bf16[128,256]{1,0:T(8,128)(2,1)S(1)} collective-permute-done((bf16[128,256]{1,0:T(8,128)(2,1)S(1)}, bf16[128,256]{1,0:T(8,128)(2,1)S(1)}, u32[]{:S(2)}, u32[]{:S(2)}) %collective-permute-start.10) | collective-permute-done | bytes 65568 | tf_op jit(solution)/shard_map/ppermute | solution.py:323
  21.3 3.0 %collective-permute-done.11.refs_5_ = bf16[512,256]{1,0:T(8,128)(2,1)S(1)} collective-permute-done((bf16[512,256]{1,0:T(8,128)(2,1)S(1)}, bf16[512,256]{1,0:T(8,128)(2,1)S(1)}, u32[]{:S(2)}, u32[]{:S(2)}) %collective-permute-start.11) | collective-permute-done | bytes 262176 | tf_op jit(solution)/shard_map/ppermute | solution.py:326
  24.3 0.3 shard_map.92
  24.6 1.9 %collective-permute-start.13 = (bf16[256,256]{1,0:T(8,128)(2,1)S(1)}, bf16[256,256]{1,0:T(8,128)(2,1)S(1)}, u32[]{:S(2)}, u32[]{:S(2)}) collective-permute-start(bf16[256,256]{1,0:T(8,128)(2,1)S(1)} %get-tuple-element.67.refs_2_), channel_id=1, source_target_pairs={{0,8},{1,9},{2,10},{3,11},{4,12},{5,13},{6,14},{7,15},{8,0},{9,1},... | collective-permute-start | bytes 393224 | tf_op jit(solution)/shard_map/ppermute | solution.py:330
  26.5 1.2 %collective-permute-start.14 = (bf16[256,256]{1,0:T(8,128)(2,1)S(1)}, bf16[256,256]{1,0:T(8,128)(2,1)S(1)}, u32[]{:S(2)}, u32[]{:S(2)}) collective-permute-start(bf16[256,256]{1,0:T(8,128)(2,1)S(1)} %get-tuple-element.71), channel_id=1, source_target_pairs={{0,16},{1,17},{2,18},{3,19},{4,20},{5,21},{6,22},{7,23},{8,24},{9,... | collective-permute-start | bytes 393224 | tf_op jit(solution)/shard_map/ppermute | solution.py:330
  27.7 1.5 %collective-permute-start.8 = (bf16[64,256]{1,0:T(8,128)(2,1)S(1)}, bf16[64,256]{1,0:T(8,128)(2,1)S(1)}, u32[]{:S(2)}, u32[]{:S(2)}) collective-permute-start(bf16[64,256]{1,0:T(8,128)(2,1)S(1)} %get-tuple-element.61.refs_0_), channel_id=1, source_target_pairs={{0,4},{1,3},{2,6},{3,1},{4,0},{5,7},{6,2},{7,5},{8,12},{9,11},{10,... | collective-permute-start | bytes 98312 | tf_op jit(solution)/shard_map/ppermute | solution.py:326
  29.2 2.4 %collective-permute-done.8.refs_1_ = bf16[64,256]{1,0:T(8,128)(2,1)S(1)} collective-permute-done((bf16[64,256]{1,0:T(8,128)(2,1)S(1)}, bf16[64,256]{1,0:T(8,128)(2,1)S(1)}, u32[]{:S(2)}, u32[]{:S(2)}) %collective-permute-start.8) | collective-permute-done | bytes 32800 | tf_op jit(solution)/shard_map/ppermute | solution.py:326
  31.6 0.0 collective-permute-done.13.refs_1_
  31.7 1.8 %collective-permute-start.16 = (bf16[256,256]{1,0:T(8,128)(2,1)S(1)}, bf16[256,256]{1,0:T(8,128)(2,1)S(1)}, u32[]{:S(2)}, u32[]{:S(2)}) collective-permute-start(bf16[256,256]{1,0:T(8,128)(2,1)S(1)} %get-tuple-element.69.refs_4_), channel_id=1, source_target_pairs={{0,16},{1,17},{2,18},{3,19},{4,20},{5,21},{6,22},{7,23},{8,24},{9,... | collective-permute-start | bytes 393224 | tf_op jit(solution)/shard_map/ppermute | solution.py:330
  33.5 1.5 %collective-permute-start.12 = (bf16[128,256]{1,0:T(8,128)(2,1)S(1)}, bf16[128,256]{1,0:T(8,128)(2,1)S(1)}, u32[]{:S(2)}, u32[]{:S(2)}) collective-permute-start(bf16[128,256]{1,0:T(8,128)(2,1)S(1)} %shard_map.93.refs_2_), channel_id=1, source_target_pairs={{0,2},{1,5},{2,0},{3,7},{4,6},{5,1},{6,4},{7,3},{8,10},{9,13},{10,... | collective-permute-start | bytes 196616 | tf_op jit(solution)/shard_map/ppermute | solution.py:326
  35.0 0.9 %collective-permute-done.14.refs_1_ = bf16[256,256]{1,0:T(8,128)(2,1)S(1)} collective-permute-done((bf16[256,256]{1,0:T(8,128)(2,1)S(1)}, bf16[256,256]{1,0:T(8,128)(2,1)S(1)}, u32[]{:S(2)}, u32[]{:S(2)}) %collective-permute-start.14) | collective-permute-done | bytes 131104 | tf_op jit(solution)/shard_map/ppermute | solution.py:330
  35.9 0.1 collective-permute-start.15
  36.0 3.5 %collective-permute-done.16.refs_1_ = bf16[256,256]{1,0:T(8,128)(2,1)S(1)} collective-permute-done((bf16[256,256]{1,0:T(8,128)(2,1)S(1)}, bf16[256,256]{1,0:T(8,128)(2,1)S(1)}, u32[]{:S(2)}, u32[]{:S(2)}) %collective-permute-start.16) | collective-permute-done | bytes 131104 | tf_op jit(solution)/shard_map/ppermute | solution.py:330
  39.6 0.1 collective-permute-start.17
  39.7 0.0 collective-permute-done.12.refs_3_
  39.7 1.1 %shard_map.95.refs_0_.update = bf16[512,512]{1,0:T(8,128)(2,1)S(1)} custom-call(bf16[2,512,256]{2,1,0:T(8,128)(2,1)S(1)} %get-tuple-element.40.refs_0_, f32[2,256,256]{2,1,0:T(8,128)S(1)} %copy-done, bf16[128,256]{1,0:T(8,128)(2,1)S(1)} %shard_map.93.refs_2_, bf16[128,256]{1,0:T(8,128)(2,1)S(1)} %collective-permute-done.12.refs_3_, ...), custom_call_target="tpu_custom_call" | custom-call | flops 1000000000 | bytes 1 | tf_op jit(solution)/shard_map/pallas_call | solution.py:70
  40.8 1.3 %collective-permute-done.15.refs_1_ = bf16[256,256]{1,0:T(8,128)(2,1)S(1)} collective-permute-done((bf16[256,256]{1,0:T(8,128)(2,1)S(1)}, bf16[256,256]{1,0:T(8,128)(2,1)S(1)}, u32[]{:S(2)}, u32[]{:S(2)}) %collective-permute-start.15) | collective-permute-done | bytes 131104 | tf_op jit(solution)/shard_map/ppermute | solution.py:330
  42.1 0.2 shard_map.99.total
  42.3 2.3 %collective-permute-done.17.project = bf16[256,256]{1,0:T(8,128)(2,1)S(1)} collective-permute-done((bf16[256,256]{1,0:T(8,128)(2,1)S(1)}, bf16[256,256]{1,0:T(8,128)(2,1)S(1)}, u32[]{:S(2)}, u32[]{:S(2)}) %collective-permute-start.17) | collective-permute-done | bytes 131104 | tf_op jit(solution)/shard_map/ppermute | solution.py:330
  44.6 0.9 %shard_map.100 = bf16[512,256]{1,0:T(8,128)(2,1)} custom-call(f32[512,256]{1,0:T(8,128)S(1)} %shard_map.99.total, bf16[512,512]{1,0:T(8,128)(2,1)S(1)} %shard_map.95.refs_0_.update, bf16[256,256]{1,0:T(8,128)(2,1)S(1)} %collective-permute-done.17.project), custom_call_target="tpu_custom_call" | custom-call | flops 1 | bytes 1 | tf_op jit(solution)/shard_map/pallas_call | solution.py:268
  (9 shorter events, 0.2 us)
Async XLA Ops:
  3.3 5.0 %collective-permute-start.2 = (bf16[512,256]{1,0:T(8,128)(2,1)S(1)}, bf16[512,256]{1,0:T(8,128)(2,1)S(1)}, u32[]{:S(2)}, u32[]{:S(2)}) collective-permute-start(bf16[512,256]{1,0:T(8,128)(2,1)S(1)} %get-tuple-element.52), channel_id=1, source_target_pairs={{0,1},{1,0},{2,3},{3,2},{4,5},{5,4},{6,7},{7,6},{8,9},{9,8},{10,11... | collective-permute-start | bytes 786440 | tf_op jit(solution)/shard_map/ppermute | solution.py:323
  5.2 4.8 %collective-permute-start.1 = (bf16[512,256]{1,0:T(8,128)(2,1)S(1)}, bf16[512,256]{1,0:T(8,128)(2,1)S(1)}, u32[]{:S(2)}, u32[]{:S(2)}) collective-permute-start(bf16[512,256]{1,0:T(8,128)(2,1)S(1)} %get-tuple-element.51), channel_id=1, source_target_pairs={{0,1},{1,0},{2,3},{3,2},{4,5},{5,4},{6,7},{7,6},{8,9},{9,8},{10,11... | collective-permute-start | bytes 786440 | tf_op jit(solution)/shard_map/ppermute | solution.py:323
  5.3 7.8 %collective-permute-start = (bf16[320,256]{1,0:T(8,128)(2,1)S(1)}, bf16[320,256]{1,0:T(8,128)(2,1)S(1)}, u32[]{:S(2)}, u32[]{:S(2)}) collective-permute-start(bf16[320,256]{1,0:T(8,128)(2,1)S(1)} %get-tuple-element.43), channel_id=1, source_target_pairs={{0,8},{1,17},{2,10},{3,19},{4,12},{5,21},{6,14},{7,23},{8,0},{9,25... | collective-permute-start | bytes 491528 | tf_op jit(solution)/shard_map/ppermute | solution.py:330
  8.4 9.2 %collective-permute-start.5 = (bf16[512,256]{1,0:T(8,128)(2,1)S(1)}, bf16[512,256]{1,0:T(8,128)(2,1)S(1)}, u32[]{:S(2)}, u32[]{:S(2)}) collective-permute-start(bf16[512,256]{1,0:T(8,128)(2,1)S(1)} %shard_map.85.refs_3_), channel_id=1, source_target_pairs={{0,4},{1,3},{2,6},{3,1},{4,0},{5,7},{6,2},{7,5},{8,12},{9,11},{10,... | collective-permute-start | bytes 786440 | tf_op jit(solution)/shard_map/ppermute | solution.py:326
  10.0 7.6 %collective-permute-start.7 = (bf16[512,256]{1,0:T(8,128)(2,1)S(1)}, bf16[512,256]{1,0:T(8,128)(2,1)S(1)}, u32[]{:S(2)}, u32[]{:S(2)}) collective-permute-start(bf16[512,256]{1,0:T(8,128)(2,1)S(1)} %shard_map.86.refs_3_.refs_5_), channel_id=1, source_target_pairs={{0,4},{1,3},{2,6},{3,1},{4,0},{5,7},{6,2},{7,5},{8,12},{9,11},{10,... | collective-permute-start | bytes 786440 | tf_op jit(solution)/shard_map/ppermute | solution.py:326
  12.0 5.7 %collective-permute-start.6 = (bf16[512,256]{1,0:T(8,128)(2,1)S(1)}, bf16[512,256]{1,0:T(8,128)(2,1)S(1)}, u32[]{:S(2)}, u32[]{:S(2)}) collective-permute-start(bf16[512,256]{1,0:T(8,128)(2,1)S(1)} %get-tuple-element.59), channel_id=1, source_target_pairs={{0,1},{1,0},{2,3},{3,2},{4,5},{5,4},{6,7},{7,6},{8,9},{9,8},{10,11... | collective-permute-start | bytes 786440 | tf_op jit(solution)/shard_map/ppermute | solution.py:323
  12.2 5.4 %collective-permute-start.4 = (bf16[512,256]{1,0:T(8,128)(2,1)S(1)}, bf16[512,256]{1,0:T(8,128)(2,1)S(1)}, u32[]{:S(2)}, u32[]{:S(2)}) collective-permute-start(bf16[512,256]{1,0:T(8,128)(2,1)S(1)} %get-tuple-element.56.refs_5_), channel_id=1, source_target_pairs={{0,1},{1,0},{2,3},{3,2},{4,5},{5,4},{6,7},{7,6},{8,9},{9,8},{10,11... | collective-permute-start | bytes 786440 | tf_op jit(solution)/shard_map/ppermute | solution.py:323
  13.1 6.5 %collective-permute-start.3 = (bf16[320,256]{1,0:T(8,128)(2,1)S(1)}, bf16[320,256]{1,0:T(8,128)(2,1)S(1)}, u32[]{:S(2)}, u32[]{:S(2)}) collective-permute-start(bf16[320,256]{1,0:T(8,128)(2,1)S(1)} %get-tuple-element.55), channel_id=1, source_target_pairs={{0,16},{1,9},{2,18},{3,11},{4,20},{5,13},{6,22},{7,15},{8,24},{9,1... | collective-permute-start | bytes 491528 | tf_op jit(solution)/shard_map/ppermute | solution.py:330
  17.8 21.8 %copy-start = (f32[2,256,256]{2,1,0:T(8,128)S(1)}, f32[2,256,256]{2,1,0:T(8,128)}, u32[]{:S(2)}) copy-start(f32[2,256,256]{2,1,0:T(8,128)} %refs_1_.3) | copy-start | bytes 1572868
  17.8 6.4 %collective-permute-start.11 = (bf16[512,256]{1,0:T(8,128)(2,1)S(1)}, bf16[512,256]{1,0:T(8,128)(2,1)S(1)}, u32[]{:S(2)}, u32[]{:S(2)}) collective-permute-start(bf16[512,256]{1,0:T(8,128)(2,1)S(1)} %get-tuple-element.60.refs_3_), channel_id=1, source_target_pairs={{0,2},{1,5},{2,0},{3,7},{4,6},{5,1},{6,4},{7,3},{8,10},{9,13},{10,... | collective-permute-start | bytes 786440 | tf_op jit(solution)/shard_map/ppermute | solution.py:326
  19.7 1.6 %collective-permute-start.9 = (bf16[384,256]{1,0:T(8,128)(2,1)S(1)}, bf16[384,256]{1,0:T(8,128)(2,1)S(1)}, u32[]{:S(2)}, u32[]{:S(2)}) collective-permute-start(bf16[384,256]{1,0:T(8,128)(2,1)S(1)} %get-tuple-element.63), channel_id=1, source_target_pairs={{0,1},{1,0},{2,3},{3,2},{4,5},{5,4},{6,7},{7,6},{8,9},{9,8},{10,11... | collective-permute-start | bytes 589832 | tf_op jit(solution)/shard_map/ppermute | solution.py:323
  19.9 1.4 %collective-permute-start.10 = (bf16[128,256]{1,0:T(8,128)(2,1)S(1)}, bf16[128,256]{1,0:T(8,128)(2,1)S(1)}, u32[]{:S(2)}, u32[]{:S(2)}) collective-permute-start(bf16[128,256]{1,0:T(8,128)(2,1)S(1)} %get-tuple-element.64), channel_id=1, source_target_pairs={{0,1},{1,0},{2,3},{3,2},{4,5},{5,4},{6,7},{7,6},{8,9},{9,8},{10,11... | collective-permute-start | bytes 196616 | tf_op jit(solution)/shard_map/ppermute | solution.py:323
  24.6 7.0 %collective-permute-start.13 = (bf16[256,256]{1,0:T(8,128)(2,1)S(1)}, bf16[256,256]{1,0:T(8,128)(2,1)S(1)}, u32[]{:S(2)}, u32[]{:S(2)}) collective-permute-start(bf16[256,256]{1,0:T(8,128)(2,1)S(1)} %get-tuple-element.67.refs_2_), channel_id=1, source_target_pairs={{0,8},{1,9},{2,10},{3,11},{4,12},{5,13},{6,14},{7,15},{8,0},{9,1},... | collective-permute-start | bytes 393224 | tf_op jit(solution)/shard_map/ppermute | solution.py:330
  26.5 9.4 %collective-permute-start.14 = (bf16[256,256]{1,0:T(8,128)(2,1)S(1)}, bf16[256,256]{1,0:T(8,128)(2,1)S(1)}, u32[]{:S(2)}, u32[]{:S(2)}) collective-permute-start(bf16[256,256]{1,0:T(8,128)(2,1)S(1)} %get-tuple-element.71), channel_id=1, source_target_pairs={{0,16},{1,17},{2,18},{3,19},{4,20},{5,21},{6,22},{7,23},{8,24},{9,... | collective-permute-start | bytes 393224 | tf_op jit(solution)/shard_map/ppermute | solution.py:330
  27.7 3.9 %collective-permute-start.8 = (bf16[64,256]{1,0:T(8,128)(2,1)S(1)}, bf16[64,256]{1,0:T(8,128)(2,1)S(1)}, u32[]{:S(2)}, u32[]{:S(2)}) collective-permute-start(bf16[64,256]{1,0:T(8,128)(2,1)S(1)} %get-tuple-element.61.refs_0_), channel_id=1, source_target_pairs={{0,4},{1,3},{2,6},{3,1},{4,0},{5,7},{6,2},{7,5},{8,12},{9,11},{10,... | collective-permute-start | bytes 98312 | tf_op jit(solution)/shard_map/ppermute | solution.py:326
  31.7 7.9 %collective-permute-start.16 = (bf16[256,256]{1,0:T(8,128)(2,1)S(1)}, bf16[256,256]{1,0:T(8,128)(2,1)S(1)}, u32[]{:S(2)}, u32[]{:S(2)}) collective-permute-start(bf16[256,256]{1,0:T(8,128)(2,1)S(1)} %get-tuple-element.69.refs_4_), channel_id=1, source_target_pairs={{0,16},{1,17},{2,18},{3,19},{4,20},{5,21},{6,22},{7,23},{8,24},{9,... | collective-permute-start | bytes 393224 | tf_op jit(solution)/shard_map/ppermute | solution.py:330
  33.5 6.2 %collective-permute-start.12 = (bf16[128,256]{1,0:T(8,128)(2,1)S(1)}, bf16[128,256]{1,0:T(8,128)(2,1)S(1)}, u32[]{:S(2)}, u32[]{:S(2)}) collective-permute-start(bf16[128,256]{1,0:T(8,128)(2,1)S(1)} %shard_map.93.refs_2_), channel_id=1, source_target_pairs={{0,2},{1,5},{2,0},{3,7},{4,6},{5,1},{6,4},{7,3},{8,10},{9,13},{10,... | collective-permute-start | bytes 196616 | tf_op jit(solution)/shard_map/ppermute | solution.py:326
  35.9 6.1 %collective-permute-start.15 = (bf16[256,256]{1,0:T(8,128)(2,1)S(1)}, bf16[256,256]{1,0:T(8,128)(2,1)S(1)}, u32[]{:S(2)}, u32[]{:S(2)}) collective-permute-start(bf16[256,256]{1,0:T(8,128)(2,1)S(1)} %get-tuple-element.73), channel_id=1, source_target_pairs={{0,8},{1,9},{2,10},{3,11},{4,12},{5,13},{6,14},{7,15},{8,0},{9,1},... | collective-permute-start | bytes 393224 | tf_op jit(solution)/shard_map/ppermute | solution.py:330
  39.6 5.0 %collective-permute-start.17 = (bf16[256,256]{1,0:T(8,128)(2,1)S(1)}, bf16[256,256]{1,0:T(8,128)(2,1)S(1)}, u32[]{:S(2)}, u32[]{:S(2)}) collective-permute-start(bf16[256,256]{1,0:T(8,128)(2,1)S(1)} %shard_map.98.refs_2_), channel_id=1, source_target_pairs={{0,8},{1,9},{2,10},{3,11},{4,12},{5,13},{6,14},{7,15},{8,0},{9,1},... | collective-permute-start | bytes 393224 | tf_op jit(solution)/shard_map/ppermute | solution.py:330

commit v8 on v7

--- a/solution.py
+++ b/solution.py
@@ -138,7 +138,7 @@
         return plain_products(plan, row_codes, parts, chunks, operands)
     outs = [pltpu.VMEM((rows, width // chunks * len(codes)), BF) for _, codes in plan]
     return pl.pallas_call(
-        functools.partial(product_kernel, plan, width, chunks, poles // 2, len(after)),
+        functools.partial(product_kernel, plan, width, chunks, poles, len(after)),
         in_specs=[pl.BlockSpec(memory_space=pltpu.VMEM)] * 5 + [pl.BlockSpec(memory_space=pl.ANY)] * len(after),
         out_specs=[pl.BlockSpec(memory_space=pltpu.VMEM)] * len(outs),
         out_shape=outs,

time: 45.7 us -> 45.7 us (level)
  no operation moved by 1% of the time
where the time goes in v8:
time: 45.7 us; the launch traced here: 45.5 us
  starting transfers between devices  19 us (42%)
  waiting for transfers between devices  16 us (35%)
  Pallas kernels  10.4 us (23%)
    ppermute x7, starting transfers between devices, swap_row(): return lax.ppermute(value, ('row', 'col'), pairs)  10.5 us
    ppermute x7, waiting for transfers between devices, swap_row(): return lax.ppermute(value, ('row', 'col'), pairs)  8.78 us
    ppermute x5, starting transfers between devices, swap_col(): lax.ppermute(value, 'col', [(i, i ^ 1 << col_orders[i % 2][stage]) for i...  6.73 us
    ppermute x5, waiting for transfers between devices, swap_col(): lax.ppermute(value, 'col', [(i, i ^ 1 << col_orders[i % 2][stage]) for i...  6.14 us
    pallas_call x4, Pallas kernels, products(): pl.pallas_call(functools.partial(product_kernel, plan, width, chunks, pol...  5.48 us
    pallas_call x13, Pallas kernels, local(): pl.pallas_call(kernel, in_specs=[pl.BlockSpec(memory_space=pltpu.VMEM)] *...  2.16 us
    pallas_call x1, Pallas kernels, panel_blocks(): pl.pallas_call(functools.partial(panel_kernel, row_codes, row_orders, blo...  1.87 us
    ppermute x6, starting transfers between devices, swap_cores(): return lax.ppermute(value, 'col', [(i, i ^ 1) for i in range(n_col)])  1.79 us
  transfers between devices with their start and end apart: 18, of which 10 were waited for; matrix products, arithmetic and copies ran while one was open for 0% of the time, Pallas kernels for 13%

profile of v8, /device:TPU:0, one launch (start us, length us, event | category | flops | bytes accessed | tf_op | source)
XLA Modules:
  0.0 45.5 jit_solution(12674143621365484621)
XLA Ops:
  0.0 1.9 %shard_map.82 = (bf16[2,512,256]{2,1,0:T(8,128)(2,1)S(1)}, bf16[256,256]{1,0:T(8,128)(2,1)S(1)}, bf16[320,256]{1,0:T(8,128)(2,1)S(1)}, f32[64,256]{1,0:T(8,128)S...) custom-call(bf16[512,2048]{1,0:T(8,128)(2,1)} %refs_0_.1, ...), custom_call_target="tpu_custom_call" | custom-call | flops 1 | bytes 1 | tf_op jit(solution)/shard_map/pallas_call | solution.py:225
  1.9 1.4 %shard_map.83 = (bf16[512,256]{1,0:T(8,128)(2,1)S(1)}, bf16[512,256]{1,0:T(8,128)(2,1)S(1)}) custom-call(bf16[512,2048]{1,0:T(8,128)(2,1)S(1)} %get-tuple-element.44.refs_0_, f32[1,2048]{1,0:T(1,128)S(1)} %get-tuple-element.45.refs_1_, f32[1,2048]{1,0:T(1,128)S(1)} %get-tuple-element.46.refs_2_, f32[1,2048]{1,0:T(1,128)S(1)} %get-tuple-element.47.refs_3_, ...), custom_call_target="tpu_custom_call" | custom-call | flops 1 | bytes 1 | tf_op jit(solution)/shard_map/pallas_call | solution.py:140
  3.3 0.5 %collective-permute-start.2 = (bf16[512,256]{1,0:T(8,128)(2,1)S(1)}, bf16[512,256]{1,0:T(8,128)(2,1)S(1)}, u32[]{:S(2)}, u32[]{:S(2)}) collective-permute-start(bf16[512,256]{1,0:T(8,128)(2,1)S(1)} %get-tuple-element.52), channel_id=1, source_target_pairs={{0,1},{1,0},{2,3},{3,2},{4,5},{5,4},{6,7},{7,6},{8,9},{9,8},{10,11... | collective-permute-start | bytes 786440 | tf_op jit(solution)/shard_map/ppermute | solution.py:323
  3.8 1.4 %shard_map.84 = (bf16[512,256]{1,0:T(8,128)(2,1)S(1)}, bf16[512,256]{1,0:T(8,128)(2,1)S(1)}) custom-call(bf16[512,2048]{1,0:T(8,128)(2,1)S(1)} %get-tuple-element.44.refs_0_, f32[1,2048]{1,0:T(1,128)S(1)} %get-tuple-element.45.refs_1_, f32[1,2048]{1,0:T(1,128)S(1)} %get-tuple-element.46.refs_2_, f32[1,2048]{1,0:T(1,128)S(1)} %get-tuple-element.47.refs_3_, ...), custom_call_target="tpu_custom_call" | custom-call | flops 1 | bytes 1 | tf_op jit(solution)/shard_map/pallas_call | solution.py:140
  5.2 0.1 collective-permute-start.1
  5.3 3.0 %collective-permute-start = (bf16[320,256]{1,0:T(8,128)(2,1)S(1)}, bf16[320,256]{1,0:T(8,128)(2,1)S(1)}, u32[]{:S(2)}, u32[]{:S(2)}) collective-permute-start(bf16[320,256]{1,0:T(8,128)(2,1)S(1)} %get-tuple-element.43), channel_id=1, source_target_pairs={{0,8},{1,17},{2,10},{3,19},{4,12},{5,21},{6,14},{7,23},{8,0},{9,25... | collective-permute-start | bytes 491528 | tf_op jit(solution)/shard_map/ppermute | solution.py:330
  8.3 0.0 collective-permute-done.2.refs_1_
  8.3 0.1 shard_map.85.refs_3_
  8.4 1.6 %collective-permute-start.5 = (bf16[512,256]{1,0:T(8,128)(2,1)S(1)}, bf16[512,256]{1,0:T(8,128)(2,1)S(1)}, u32[]{:S(2)}, u32[]{:S(2)}) collective-permute-start(bf16[512,256]{1,0:T(8,128)(2,1)S(1)} %shard_map.85.refs_3_), channel_id=1, source_target_pairs={{0,4},{1,3},{2,6},{3,1},{4,0},{5,7},{6,2},{7,5},{8,12},{9,11},{10,... | collective-permute-start | bytes 786440 | tf_op jit(solution)/shard_map/ppermute | solution.py:326
  10.0 0.0 collective-permute-done.1.refs_1_
  10.0 0.1 shard_map.86.refs_3_.refs_5_
  10.0 0.6 %collective-permute-start.7 = (bf16[512,256]{1,0:T(8,128)(2,1)S(1)}, bf16[512,256]{1,0:T(8,128)(2,1)S(1)}, u32[]{:S(2)}, u32[]{:S(2)}) collective-permute-start(bf16[512,256]{1,0:T(8,128)(2,1)S(1)} %shard_map.86.refs_3_.refs_5_), channel_id=1, source_target_pairs={{0,4},{1,3},{2,6},{3,1},{4,0},{5,7},{6,2},{7,5},{8,12},{9,11},{10,... | collective-permute-start | bytes 786440 | tf_op jit(solution)/shard_map/ppermute | solution.py:326
  10.6 1.4 %shard_map.88 = (bf16[512,256]{1,0:T(8,128)(2,1)S(1)}, bf16[512,256]{1,0:T(8,128)(2,1)S(1)}) custom-call(bf16[512,2048]{1,0:T(8,128)(2,1)S(1)} %get-tuple-element.44.refs_0_, f32[1,2048]{1,0:T(1,128)S(1)} %get-tuple-element.45.refs_1_, f32[1,2048]{1,0:T(1,128)S(1)} %get-tuple-element.46.refs_2_, f32[1,2048]{1,0:T(1,128)S(1)} %get-tuple-element.47.refs_3_, ...), custom_call_target="tpu_custom_call" | custom-call | flops 1 | bytes 1 | tf_op jit(solution)/shard_map/pallas_call | solution.py:140
  12.0 0.3 collective-permute-start.6
  12.2 0.3 collective-permute-start.4
  12.5 0.6 %collective-permute-done.refs_2_ = bf16[320,256]{1,0:T(8,128)(2,1)S(1)} collective-permute-done((bf16[320,256]{1,0:T(8,128)(2,1)S(1)}, bf16[320,256]{1,0:T(8,128)(2,1)S(1)}, u32[]{:S(2)}, u32[]{:S(2)}) %collective-permute-start) | collective-permute-done | bytes 163872 | tf_op jit(solution)/shard_map/ppermute | solution.py:330
  13.1 2.4 %collective-permute-start.3 = (bf16[320,256]{1,0:T(8,128)(2,1)S(1)}, bf16[320,256]{1,0:T(8,128)(2,1)S(1)}, u32[]{:S(2)}, u32[]{:S(2)}) collective-permute-start(bf16[320,256]{1,0:T(8,128)(2,1)S(1)} %get-tuple-element.55), channel_id=1, source_target_pairs={{0,16},{1,9},{2,18},{3,11},{4,20},{5,13},{6,22},{7,15},{8,24},{9,1... | collective-permute-start | bytes 491528 | tf_op jit(solution)/shard_map/ppermute | solution.py:330
  15.5 1.4 %shard_map.89 = (bf16[512,256]{1,0:T(8,128)(2,1)S(1)}, bf16[512,256]{1,0:T(8,128)(2,1)S(1)}) custom-call(bf16[512,2048]{1,0:T(8,128)(2,1)S(1)} %get-tuple-element.44.refs_0_, f32[1,2048]{1,0:T(1,128)S(1)} %get-tuple-element.45.refs_1_, f32[1,2048]{1,0:T(1,128)S(1)} %get-tuple-element.46.refs_2_, f32[1,2048]{1,0:T(1,128)S(1)} %get-tuple-element.47.refs_3_, ...), custom_call_target="tpu_custom_call" | custom-call | flops 1 | bytes 1 | tf_op jit(solution)/shard_map/pallas_call | solution.py:140
  16.9 0.7 %collective-permute-done.7.refs_5_ = bf16[512,256]{1,0:T(8,128)(2,1)S(1)} collective-permute-done((bf16[512,256]{1,0:T(8,128)(2,1)S(1)}, bf16[512,256]{1,0:T(8,128)(2,1)S(1)}, u32[]{:S(2)}, u32[]{:S(2)}) %collective-permute-start.7) | collective-permute-done | bytes 262176 | tf_op jit(solution)/shard_map/ppermute | solution.py:326
  17.6 0.0 collective-permute-done.5.refs_2_
  17.6 0.0 collective-permute-done.6.refs_4_
  17.6 0.0 collective-permute-done.4.refs_1_
  17.6 0.2 shard_map.90
  17.8 0.0 copy-start
  17.8 1.6 %collective-permute-start.11 = (bf16[512,256]{1,0:T(8,128)(2,1)S(1)}, bf16[512,256]{1,0:T(8,128)(2,1)S(1)}, u32[]{:S(2)}, u32[]{:S(2)}) collective-permute-start(bf16[512,256]{1,0:T(8,128)(2,1)S(1)} %get-tuple-element.60.refs_3_), channel_id=1, source_target_pairs={{0,2},{1,5},{2,0},{3,7},{4,6},{5,1},{6,4},{7,3},{8,10},{9,13},{10,... | collective-permute-start | bytes 786440 | tf_op jit(solution)/shard_map/ppermute | solution.py:326
  19.4 0.2 collective-permute-done.3.refs_2_
  19.7 0.2 collective-permute-start.9
  19.9 0.4 collective-permute-start.10
  20.2 1.0 %collective-permute-done.10.refs_2_ = bf16[128,256]{1,0:T(8,128)(2,1)S(1)} collective-permute-done((bf16[128,256]{1,0:T(8,128)(2,1)S(1)}, bf16[128,256]{1,0:T(8,128)(2,1)S(1)}, u32[]{:S(2)}, u32[]{:S(2)}) %collective-permute-start.10) | collective-permute-done | bytes 65568 | tf_op jit(solution)/shard_map/ppermute | solution.py:323
  21.3 3.0 %collective-permute-done.11.refs_5_ = bf16[512,256]{1,0:T(8,128)(2,1)S(1)} collective-permute-done((bf16[512,256]{1,0:T(8,128)(2,1)S(1)}, bf16[512,256]{1,0:T(8,128)(2,1)S(1)}, u32[]{:S(2)}, u32[]{:S(2)}) %collective-permute-start.11) | collective-permute-done | bytes 262176 | tf_op jit(solution)/shard_map/ppermute | solution.py:326
  24.3 0.3 shard_map.92
  24.6 1.9 %collective-permute-start.13 = (bf16[256,256]{1,0:T(8,128)(2,1)S(1)}, bf16[256,256]{1,0:T(8,128)(2,1)S(1)}, u32[]{:S(2)}, u32[]{:S(2)}) collective-permute-start(bf16[256,256]{1,0:T(8,128)(2,1)S(1)} %get-tuple-element.67.refs_2_), channel_id=1, source_target_pairs={{0,8},{1,9},{2,10},{3,11},{4,12},{5,13},{6,14},{7,15},{8,0},{9,1},... | collective-permute-start | bytes 393224 | tf_op jit(solution)/shard_map/ppermute | solution.py:330
  26.5 1.2 %collective-permute-start.14 = (bf16[256,256]{1,0:T(8,128)(2,1)S(1)}, bf16[256,256]{1,0:T(8,128)(2,1)S(1)}, u32[]{:S(2)}, u32[]{:S(2)}) collective-permute-start(bf16[256,256]{1,0:T(8,128)(2,1)S(1)} %get-tuple-element.71), channel_id=1, source_target_pairs={{0,16},{1,17},{2,18},{3,19},{4,20},{5,21},{6,22},{7,23},{8,24},{9,... | collective-permute-start | bytes 393224 | tf_op jit(solution)/shard_map/ppermute | solution.py:330
  27.7 1.5 %collective-permute-start.8 = (bf16[64,256]{1,0:T(8,128)(2,1)S(1)}, bf16[64,256]{1,0:T(8,128)(2,1)S(1)}, u32[]{:S(2)}, u32[]{:S(2)}) collective-permute-start(bf16[64,256]{1,0:T(8,128)(2,1)S(1)} %get-tuple-element.61.refs_0_), channel_id=1, source_target_pairs={{0,4},{1,3},{2,6},{3,1},{4,0},{5,7},{6,2},{7,5},{8,12},{9,11},{10,... | collective-permute-start | bytes 98312 | tf_op jit(solution)/shard_map/ppermute | solution.py:326
  29.2 2.4 %collective-permute-done.8.refs_1_ = bf16[64,256]{1,0:T(8,128)(2,1)S(1)} collective-permute-done((bf16[64,256]{1,0:T(8,128)(2,1)S(1)}, bf16[64,256]{1,0:T(8,128)(2,1)S(1)}, u32[]{:S(2)}, u32[]{:S(2)}) %collective-permute-start.8) | collective-permute-done | bytes 32800 | tf_op jit(solution)/shard_map/ppermute | solution.py:326
  31.6 0.0 collective-permute-done.13.refs_1_
  31.7 1.8 %collective-permute-start.16 = (bf16[256,256]{1,0:T(8,128)(2,1)S(1)}, bf16[256,256]{1,0:T(8,128)(2,1)S(1)}, u32[]{:S(2)}, u32[]{:S(2)}) collective-permute-start(bf16[256,256]{1,0:T(8,128)(2,1)S(1)} %get-tuple-element.69.refs_4_), channel_id=1, source_target_pairs={{0,16},{1,17},{2,18},{3,19},{4,20},{5,21},{6,22},{7,23},{8,24},{9,... | collective-permute-start | bytes 393224 | tf_op jit(solution)/shard_map/ppermute | solution.py:330
  33.5 1.5 %collective-permute-start.12 = (bf16[128,256]{1,0:T(8,128)(2,1)S(1)}, bf16[128,256]{1,0:T(8,128)(2,1)S(1)}, u32[]{:S(2)}, u32[]{:S(2)}) collective-permute-start(bf16[128,256]{1,0:T(8,128)(2,1)S(1)} %shard_map.93.refs_2_), channel_id=1, source_target_pairs={{0,2},{1,5},{2,0},{3,7},{4,6},{5,1},{6,4},{7,3},{8,10},{9,13},{10,... | collective-permute-start | bytes 196616 | tf_op jit(solution)/shard_map/ppermute | solution.py:326
  35.0 0.9 %collective-permute-done.14.refs_1_ = bf16[256,256]{1,0:T(8,128)(2,1)S(1)} collective-permute-done((bf16[256,256]{1,0:T(8,128)(2,1)S(1)}, bf16[256,256]{1,0:T(8,128)(2,1)S(1)}, u32[]{:S(2)}, u32[]{:S(2)}) %collective-permute-start.14) | collective-permute-done | bytes 131104 | tf_op jit(solution)/shard_map/ppermute | solution.py:330
  35.9 0.1 collective-permute-start.15
  36.0 3.5 %collective-permute-done.16.refs_1_ = bf16[256,256]{1,0:T(8,128)(2,1)S(1)} collective-permute-done((bf16[256,256]{1,0:T(8,128)(2,1)S(1)}, bf16[256,256]{1,0:T(8,128)(2,1)S(1)}, u32[]{:S(2)}, u32[]{:S(2)}) %collective-permute-start.16) | collective-permute-done | bytes 131104 | tf_op jit(solution)/shard_map/ppermute | solution.py:330
  39.6 0.1 collective-permute-start.17
  39.7 0.0 collective-permute-done.12.refs_3_
  39.7 1.1 %shard_map.95.refs_0_.update = bf16[512,512]{1,0:T(8,128)(2,1)S(1)} custom-call(bf16[2,512,256]{2,1,0:T(8,128)(2,1)S(1)} %get-tuple-element.40.refs_0_, f32[2,256,256]{2,1,0:T(8,128)S(1)} %copy-done, bf16[128,256]{1,0:T(8,128)(2,1)S(1)} %shard_map.93.refs_2_, bf16[128,256]{1,0:T(8,128)(2,1)S(1)} %collective-permute-done.12.refs_3_, ...), custom_call_target="tpu_custom_call" | custom-call | flops 1000000000 | bytes 1 | tf_op jit(solution)/shard_map/pallas_call | solution.py:70
  40.8 1.3 %collective-permute-done.15.refs_1_ = bf16[256,256]{1,0:T(8,128)(2,1)S(1)} collective-permute-done((bf16[256,256]{1,0:T(8,128)(2,1)S(1)}, bf16[256,256]{1,0:T(8,128)(2,1)S(1)}, u32[]{:S(2)}, u32[]{:S(2)}) %collective-permute-start.15) | collective-permute-done | bytes 131104 | tf_op jit(solution)/shard_map/ppermute | solution.py:330
  42.1 0.2 shard_map.99.total
  42.3 2.3 %collective-permute-done.17.project = bf16[256,256]{1,0:T(8,128)(2,1)S(1)} collective-permute-done((bf16[256,256]{1,0:T(8,128)(2,1)S(1)}, bf16[256,256]{1,0:T(8,128)(2,1)S(1)}, u32[]{:S(2)}, u32[]{:S(2)}) %collective-permute-start.17) | collective-permute-done | bytes 131104 | tf_op jit(solution)/shard_map/ppermute | solution.py:330
  44.6 0.9 %shard_map.100 = bf16[512,256]{1,0:T(8,128)(2,1)} custom-call(f32[512,256]{1,0:T(8,128)S(1)} %shard_map.99.total, bf16[512,512]{1,0:T(8,128)(2,1)S(1)} %shard_map.95.refs_0_.update, bf16[256,256]{1,0:T(8,128)(2,1)S(1)} %collective-permute-done.17.project), custom_call_target="tpu_custom_call" | custom-call | flops 1 | bytes 1 | tf_op jit(solution)/shard_map/pallas_call | solution.py:268
  (9 shorter events, 0.2 us)
Async XLA Ops:
  3.3 5.0 %collective-permute-start.2 = (bf16[512,256]{1,0:T(8,128)(2,1)S(1)}, bf16[512,256]{1,0:T(8,128)(2,1)S(1)}, u32[]{:S(2)}, u32[]{:S(2)}) collective-permute-start(bf16[512,256]{1,0:T(8,128)(2,1)S(1)} %get-tuple-element.52), channel_id=1, source_target_pairs={{0,1},{1,0},{2,3},{3,2},{4,5},{5,4},{6,7},{7,6},{8,9},{9,8},{10,11... | collective-permute-start | bytes 786440 | tf_op jit(solution)/shard_map/ppermute | solution.py:323
  5.2 4.8 %collective-permute-start.1 = (bf16[512,256]{1,0:T(8,128)(2,1)S(1)}, bf16[512,256]{1,0:T(8,128)(2,1)S(1)}, u32[]{:S(2)}, u32[]{:S(2)}) collective-permute-start(bf16[512,256]{1,0:T(8,128)(2,1)S(1)} %get-tuple-element.51), channel_id=1, source_target_pairs={{0,1},{1,0},{2,3},{3,2},{4,5},{5,4},{6,7},{7,6},{8,9},{9,8},{10,11... | collective-permute-start | bytes 786440 | tf_op jit(solution)/shard_map/ppermute | solution.py:323
  5.3 7.8 %collective-permute-start = (bf16[320,256]{1,0:T(8,128)(2,1)S(1)}, bf16[320,256]{1,0:T(8,128)(2,1)S(1)}, u32[]{:S(2)}, u32[]{:S(2)}) collective-permute-start(bf16[320,256]{1,0:T(8,128)(2,1)S(1)} %get-tuple-element.43), channel_id=1, source_target_pairs={{0,8},{1,17},{2,10},{3,19},{4,12},{5,21},{6,14},{7,23},{8,0},{9,25... | collective-permute-start | bytes 491528 | tf_op jit(solution)/shard_map/ppermute | solution.py:330
  8.4 9.2 %collective-permute-start.5 = (bf16[512,256]{1,0:T(8,128)(2,1)S(1)}, bf16[512,256]{1,0:T(8,128)(2,1)S(1)}, u32[]{:S(2)}, u32[]{:S(2)}) collective-permute-start(bf16[512,256]{1,0:T(8,128)(2,1)S(1)} %shard_map.85.refs_3_), channel_id=1, source_target_pairs={{0,4},{1,3},{2,6},{3,1},{4,0},{5,7},{6,2},{7,5},{8,12},{9,11},{10,... | collective-permute-start | bytes 786440 | tf_op jit(solution)/shard_map/ppermute | solution.py:326
  10.0 7.6 %collective-permute-start.7 = (bf16[512,256]{1,0:T(8,128)(2,1)S(1)}, bf16[512,256]{1,0:T(8,128)(2,1)S(1)}, u32[]{:S(2)}, u32[]{:S(2)}) collective-permute-start(bf16[512,256]{1,0:T(8,128)(2,1)S(1)} %shard_map.86.refs_3_.refs_5_), channel_id=1, source_target_pairs={{0,4},{1,3},{2,6},{3,1},{4,0},{5,7},{6,2},{7,5},{8,12},{9,11},{10,... | collective-permute-start | bytes 786440 | tf_op jit(solution)/shard_map/ppermute | solution.py:326
  12.0 5.7 %collective-permute-start.6 = (bf16[512,256]{1,0:T(8,128)(2,1)S(1)}, bf16[512,256]{1,0:T(8,128)(2,1)S(1)}, u32[]{:S(2)}, u32[]{:S(2)}) collective-permute-start(bf16[512,256]{1,0:T(8,128)(2,1)S(1)} %get-tuple-element.59), channel_id=1, source_target_pairs={{0,1},{1,0},{2,3},{3,2},{4,5},{5,4},{6,7},{7,6},{8,9},{9,8},{10,11... | collective-permute-start | bytes 786440 | tf_op jit(solution)/shard_map/ppermute | solution.py:323
  12.2 5.4 %collective-permute-start.4 = (bf16[512,256]{1,0:T(8,128)(2,1)S(1)}, bf16[512,256]{1,0:T(8,128)(2,1)S(1)}, u32[]{:S(2)}, u32[]{:S(2)}) collective-permute-start(bf16[512,256]{1,0:T(8,128)(2,1)S(1)} %get-tuple-element.56.refs_5_), channel_id=1, source_target_pairs={{0,1},{1,0},{2,3},{3,2},{4,5},{5,4},{6,7},{7,6},{8,9},{9,8},{10,11... | collective-permute-start | bytes 786440 | tf_op jit(solution)/shard_map/ppermute | solution.py:323
  13.1 6.5 %collective-permute-start.3 = (bf16[320,256]{1,0:T(8,128)(2,1)S(1)}, bf16[320,256]{1,0:T(8,128)(2,1)S(1)}, u32[]{:S(2)}, u32[]{:S(2)}) collective-permute-start(bf16[320,256]{1,0:T(8,128)(2,1)S(1)} %get-tuple-element.55), channel_id=1, source_target_pairs={{0,16},{1,9},{2,18},{3,11},{4,20},{5,13},{6,22},{7,15},{8,24},{9,1... | collective-permute-start | bytes 491528 | tf_op jit(solution)/shard_map/ppermute | solution.py:330
  17.8 21.8 %copy-start = (f32[2,256,256]{2,1,0:T(8,128)S(1)}, f32[2,256,256]{2,1,0:T(8,128)}, u32[]{:S(2)}) copy-start(f32[2,256,256]{2,1,0:T(8,128)} %refs_1_.3) | copy-start | bytes 1572868
  17.8 6.4 %collective-permute-start.11 = (bf16[512,256]{1,0:T(8,128)(2,1)S(1)}, bf16[512,256]{1,0:T(8,128)(2,1)S(1)}, u32[]{:S(2)}, u32[]{:S(2)}) collective-permute-start(bf16[512,256]{1,0:T(8,128)(2,1)S(1)} %get-tuple-element.60.refs_3_), channel_id=1, source_target_pairs={{0,2},{1,5},{2,0},{3,7},{4,6},{5,1},{6,4},{7,3},{8,10},{9,13},{10,... | collective-permute-start | bytes 786440 | tf_op jit(solution)/shard_map/ppermute | solution.py:326
  19.7 1.6 %collective-permute-start.9 = (bf16[384,256]{1,0:T(8,128)(2,1)S(1)}, bf16[384,256]{1,0:T(8,128)(2,1)S(1)}, u32[]{:S(2)}, u32[]{:S(2)}) collective-permute-start(bf16[384,256]{1,0:T(8,128)(2,1)S(1)} %get-tuple-element.63), channel_id=1, source_target_pairs={{0,1},{1,0},{2,3},{3,2},{4,5},{5,4},{6,7},{7,6},{8,9},{9,8},{10,11... | collective-permute-start | bytes 589832 | tf_op jit(solution)/shard_map/ppermute | solution.py:323
  19.9 1.4 %collective-permute-start.10 = (bf16[128,256]{1,0:T(8,128)(2,1)S(1)}, bf16[128,256]{1,0:T(8,128)(2,1)S(1)}, u32[]{:S(2)}, u32[]{:S(2)}) collective-permute-start(bf16[128,256]{1,0:T(8,128)(2,1)S(1)} %get-tuple-element.64), channel_id=1, source_target_pairs={{0,1},{1,0},{2,3},{3,2},{4,5},{5,4},{6,7},{7,6},{8,9},{9,8},{10,11... | collective-permute-start | bytes 196616 | tf_op jit(solution)/shard_map/ppermute | solution.py:323
  24.6 7.0 %collective-permute-start.13 = (bf16[256,256]{1,0:T(8,128)(2,1)S(1)}, bf16[256,256]{1,0:T(8,128)(2,1)S(1)}, u32[]{:S(2)}, u32[]{:S(2)}) collective-permute-start(bf16[256,256]{1,0:T(8,128)(2,1)S(1)} %get-tuple-element.67.refs_2_), channel_id=1, source_target_pairs={{0,8},{1,9},{2,10},{3,11},{4,12},{5,13},{6,14},{7,15},{8,0},{9,1},... | collective-permute-start | bytes 393224 | tf_op jit(solution)/shard_map/ppermute | solution.py:330
  26.5 9.4 %collective-permute-start.14 = (bf16[256,256]{1,0:T(8,128)(2,1)S(1)}, bf16[256,256]{1,0:T(8,128)(2,1)S(1)}, u32[]{:S(2)}, u32[]{:S(2)}) collective-permute-start(bf16[256,256]{1,0:T(8,128)(2,1)S(1)} %get-tuple-element.71), channel_id=1, source_target_pairs={{0,16},{1,17},{2,18},{3,19},{4,20},{5,21},{6,22},{7,23},{8,24},{9,... | collective-permute-start | bytes 393224 | tf_op jit(solution)/shard_map/ppermute | solution.py:330
  27.7 3.9 %collective-permute-start.8 = (bf16[64,256]{1,0:T(8,128)(2,1)S(1)}, bf16[64,256]{1,0:T(8,128)(2,1)S(1)}, u32[]{:S(2)}, u32[]{:S(2)}) collective-permute-start(bf16[64,256]{1,0:T(8,128)(2,1)S(1)} %get-tuple-element.61.refs_0_), channel_id=1, source_target_pairs={{0,4},{1,3},{2,6},{3,1},{4,0},{5,7},{6,2},{7,5},{8,12},{9,11},{10,... | collective-permute-start | bytes 98312 | tf_op jit(solution)/shard_map/ppermute | solution.py:326
  31.7 7.9 %collective-permute-start.16 = (bf16[256,256]{1,0:T(8,128)(2,1)S(1)}, bf16[256,256]{1,0:T(8,128)(2,1)S(1)}, u32[]{:S(2)}, u32[]{:S(2)}) collective-permute-start(bf16[256,256]{1,0:T(8,128)(2,1)S(1)} %get-tuple-element.69.refs_4_), channel_id=1, source_target_pairs={{0,16},{1,17},{2,18},{3,19},{4,20},{5,21},{6,22},{7,23},{8,24},{9,... | collective-permute-start | bytes 393224 | tf_op jit(solution)/shard_map/ppermute | solution.py:330
  33.5 6.2 %collective-permute-start.12 = (bf16[128,256]{1,0:T(8,128)(2,1)S(1)}, bf16[128,256]{1,0:T(8,128)(2,1)S(1)}, u32[]{:S(2)}, u32[]{:S(2)}) collective-permute-start(bf16[128,256]{1,0:T(8,128)(2,1)S(1)} %shard_map.93.refs_2_), channel_id=1, source_target_pairs={{0,2},{1,5},{2,0},{3,7},{4,6},{5,1},{6,4},{7,3},{8,10},{9,13},{10,... | collective-permute-start | bytes 196616 | tf_op jit(solution)/shard_map/ppermute | solution.py:326
  35.9 6.1 %collective-permute-start.15 = (bf16[256,256]{1,0:T(8,128)(2,1)S(1)}, bf16[256,256]{1,0:T(8,128)(2,1)S(1)}, u32[]{:S(2)}, u32[]{:S(2)}) collective-permute-start(bf16[256,256]{1,0:T(8,128)(2,1)S(1)} %get-tuple-element.73), channel_id=1, source_target_pairs={{0,8},{1,9},{2,10},{3,11},{4,12},{5,13},{6,14},{7,15},{8,0},{9,1},... | collective-permute-start | bytes 393224 | tf_op jit(solution)/shard_map/ppermute | solution.py:330
  39.6 5.0 %collective-permute-start.17 = (bf16[256,256]{1,0:T(8,128)(2,1)S(1)}, bf16[256,256]{1,0:T(8,128)(2,1)S(1)}, u32[]{:S(2)}, u32[]{:S(2)}) collective-permute-start(bf16[256,256]{1,0:T(8,128)(2,1)S(1)} %shard_map.98.refs_2_), channel_id=1, source_target_pairs={{0,8},{1,9},{2,10},{3,11},{4,12},{5,13},{6,14},{7,15},{8,0},{9,1},... | collective-permute-start | bytes 393224 | tf_op jit(solution)/shard_map/ppermute | solution.py:330
